TPU v7x, 32 devices: a whole 2x2x4 slice. The times are simulated.
32 devices in a mesh: groups: 2 (over x), shard: 16 (over z, y, core).
Axes of the slice: x: 2, y: 2, z: 4, core: 2. Of those that a mesh axis runs over, the one named last changes fastest.
Arguments:
- queries: bfloat16 [256, 32, 128], P(('groups', 'shard')), parts along dimension 0, may hold values from -2 to 2
- passages: bfloat16 [8192, 180, 128], P(('groups', 'shard')), parts along dimension 0, may hold values from -2 to 2
- lengths: int32 [8192], P(('groups', 'shard')), parts along dimension 0, may hold values from 45 to 180
- candidates: int32 [256, 256], P(('groups', 'shard')), parts along dimension 0, may hold values from 0 to 4095, as said below
- placement: int32 [8192], P('groups'), parts along dimension 0, may hold values from 0 to 4095, as said below
Outputs:
- scores: float32 [256, 256], P(('groups', 'shard')), parts along dimension 0
There are 2 independent parts, one for each index of `groups`. A program takes and returns all parts, laid end to end along the dimension named above; each array names one. Nothing has to cross between parts.
Inputs may be any that keep to these rules, and one draw needn't show every extreme that they name: placement is a permutation; a passage in slot s is stored on device s // 256 of the shard axis, row s % 256 of that device's passages. Within a part, no passage is named by more than 16 entries of candidates, and some passage by exactly 16; every passage is named at least once; a query may name a passage twice. The entries of the 8 queries of one device that name passages stored on one device number at most 256, and exactly 256 for some storing device.
All inputs are finite; a program needn't handle non-finite values.
Results may differ from a plain program's by a relative error of at most 0.0003.
Values may be sent and summed in bfloat16 or wider, within the bound.
No kernel may reach another device: no remote copies, remote signals or barrier semaphores. Data moves between devices by JAX's collectives and lax.ppermute only.
A program may use at most 128 MiB of HBM per device.

v0:
```python
import jax
import jax.numpy as jnp
from jax import lax
from jax.sharding import PartitionSpec as P

CAND = 256
PMOST = 16


def shards(queries, passages, lengths, candidates, placement):
    shard_count = lax.axis_size("shard")
    held_count = passages.shape[0]
    query_count = queries.shape[0]
    own_total = query_count * CAND
    route_most = held_count * PMOST // shard_count
    entry_total = shard_count * route_most
    own_slots = placement[candidates.reshape(own_total)]
    target = own_slots // held_count
    matches = (target[:, None] == jnp.arange(shard_count, dtype=jnp.int32)[None, :]).astype(
        jnp.int32
    )
    running = jnp.cumsum(matches, axis=0) - matches
    route_rank = jnp.sum(running * matches, axis=1)
    pair_ids = jnp.arange(own_total, dtype=jnp.int32)
    empty_routes = jnp.full((shard_count, route_most), -1, jnp.int32)
    out_pairs = empty_routes.at[target, route_rank].set(pair_ids)
    out_slots = empty_routes.at[target, route_rank].set(own_slots % held_count)
    in_pairs, in_slots = (
        lax.all_to_all(out_pairs, "shard", split_axis=0, concat_axis=0, tiled=True),
        lax.all_to_all(out_slots, "shard", split_axis=0, concat_axis=0, tiled=True),
    )
    entry_pairs = in_pairs.reshape(entry_total)
    entry_slots = in_slots.reshape(entry_total)
    live_entry = entry_slots >= 0
    sort_key = jnp.where(live_entry, entry_slots, held_count)
    order = jnp.argsort(sort_key, stable=True)
    slot_match = sort_key[:, None] == jnp.arange(held_count, dtype=jnp.int32)[None, :]
    slot_counts = jnp.sum(slot_match.astype(jnp.int32), axis=0)
    slot_starts = jnp.cumsum(slot_counts) - slot_counts
    ranks = jnp.arange(PMOST, dtype=jnp.int32)
    positions = jnp.minimum(slot_starts[:, None] + ranks[None, :], entry_total - 1)
    occupied = ranks[None, :] < slot_counts[:, None]
    entry_index = order[positions]
    source_owner = entry_index // route_most
    local_pair = jnp.maximum(entry_pairs[entry_index], 0)
    query_rows = source_owner * query_count + local_pair // CAND
    whole_queries = lax.all_gather(queries, "shard", axis=0, tiled=True)
    token_slots = jnp.arange(passages.shape[1], dtype=jnp.int32)

    def score_tile(inputs):
        document, length, rows, live_slots = inputs
        query_block = whole_queries[rows]
        similar = jnp.einsum(
            "kqd,pd->kqp", query_block, document, preferred_element_type=jnp.float32
        )
        similar = jnp.where(token_slots < length, similar, -1e30)
        closest = jnp.max(similar, axis=2)
        return jnp.where(live_slots, jnp.mean(closest, axis=1), 0.0)

    tile_scores = lax.map(score_tile, (passages, lengths, query_rows, occupied), batch_size=32)
    sorted_place = (
        jnp.zeros((entry_total,), jnp.int32).at[order].set(jnp.arange(entry_total, dtype=jnp.int32))
    )
    safe_slot = jnp.minimum(sort_key, held_count - 1)
    entry_rank = jnp.clip(sorted_place - slot_starts[safe_slot], 0, PMOST - 1)
    entry_scores = jnp.where(live_entry, tile_scores[safe_slot, entry_rank], 0.0)
    returned = lax.all_to_all(
        entry_scores.reshape(shard_count, route_most),
        "shard",
        split_axis=0,
        concat_axis=0,
        tiled=True,
    )
    result = returned[target, route_rank].reshape(query_count, CAND)
    return result


def solution(mesh):
    in_specs = (
        P(("groups", "shard"), None, None),
        P(("groups", "shard"), None, None),
        P(("groups", "shard")),
        P(("groups", "shard"), None),
        P("groups"),
    )
    out_specs = P(("groups", "shard"), None)
    return jax.shard_map(shards, mesh=mesh, in_specs=in_specs, out_specs=out_specs, check_vma=False)
```

profile of v0, /device:TPU:0, one launch (start us, length us, event | category | flops | bytes accessed | tf_op | source)
XLA Modules:
  0.0 316.6 jit_solution(11043335084055475591)
XLA Ops:
  6.5 0.7 copy.19
  7.3 11.8 %gather_fusion.1 = s32[2048]{0:T(1024)S(1)} fusion(s32[4096]{0:T(1024)S(1)} %copy-done, s32[2048]{0:T(1024)S(1)} %broadcast_clamp_fusion.3), kind=kCustom, calls=%fused_computation.1 | custom fusion | bytes 24576 | tf_op jit(solution)/shard_map/gather | solution.py:17
  19.2 4.5 %reduce-window.15 = s32[16,16,128]{2,1,0:T(8,128)S(1)} reduce-window(s32[16,16,128]{2,1,0:T(8,128)S(1)} %fusion.13, s32[]{:T(128)} %copy.31), window={size=1x1x128 pad=0_0x0_0x127_0}, to_apply=%region_0.1 | reduce-window | flops 4161536 | bytes 262148 | tf_op jit(solution)/shard_map/reduce-window
  23.7 0.4 slice_reduce_fusion
  24.2 0.2 reduce-window.16
  24.8 8.6 %scatter_custom_fusion.1 = s32[4096]{0:T(1024)} fusion(s32[2048]{0:T(1024)S(1)} %broadcast_select_fusion, s32[2048]{0:T(1024)S(1)} %get-tuple-element.82, s32[]{:T(128)} %constant.92.clone.1), kind=kCustom, calls=%fused_computation.90 | custom fusion | bytes 16388
  33.5 7.4 %all-to-all-start = ((s32[16,1,256]{2,1,0:T(1,128)}), s32[16,1,256]{2,1,0:T(1,128)S(1)}, u32[]{:S(2)}, u32[]{:S(2)}) async-start(s32[16,1,256]{2,1,0:T(1,128)} %bitcast.5), calls=%async_computation | async-start | bytes 32768 | tf_op jit(solution)/shard_map/all_to_all | solution.py:30
  40.9 0.7 all-gather.2.cloned.1.call-update
  41.7 8.6 %scatter_custom_fusion.2 = s32[4096]{0:T(1024)} fusion(s32[2048]{0:T(1024)S(1)} %broadcast_select_fusion, s32[2048]{0:T(1024)S(1)} %iota.35, s32[]{:T(128)} %constant.92.clone.1), kind=kCustom, calls=%fused_computation.88 | custom fusion | bytes 16388
  50.3 14.3 %copy.14 = bf16[256,180,128]{2,1,0:T(8,128)(2,1)} copy(bf16[256,180,128]{2,0,1:T(8,128)(2,1)} %param.8) | data formatting | bytes 23592960 | tf_op args[1]
  64.6 6.0 %all-to-all-start.1 = ((s32[16,1,256]{2,1,0:T(1,128)}), s32[16,1,256]{2,1,0:T(1,128)S(1)}, u32[]{:S(2)}, u32[]{:S(2)}) async-start(s32[16,1,256]{2,1,0:T(1,128)} %bitcast.9), calls=%async_computation.1 | async-start | bytes 32768 | tf_op jit(solution)/shard_map/all_to_all | solution.py:29
  70.7 1.9 convert_reduce_fusion
  72.5 5.8 %sort.17 = (s32[4096]{0:T(1024)}, s32[4096]{0:T(1024)S(1)}) sort(s32[4096]{0:T(1024)S(1)} %compare_select_fusion.11, s32[4096]{0:T(1024)S(1)} %iota.34), dimensions={0}, to_apply=%region_4.5 | sort | flops 49152 | bytes 65536 | tf_op jit(solution)/shard_map/jit(argsort)/sort | solution.py:36
  78.3 0.3 reduce-window.19
  78.7 0.1 slice_reduce_fusion.1
  79.2 23.0 %gather_fusion.2 = s32[4096]{0:T(1024)S(1)} fusion(s32[4096]{0:T(1024)S(1)} %get-tuple-element.48, s32[4096]{0:T(1024)S(1)} %broadcast_clamp_fusion.2), kind=kCustom, calls=%fused_computation.2 | custom fusion | bytes 49152 | tf_op jit(solution)/shard_map/gather | solution.py:43
  102.7 25.9 %gather_fusion.4 = s32[4096]{0:T(1024)S(1)} fusion(s32[256]{0:T(256)S(1)} %bitcast_subtract_fusion, s32[4096]{0:T(1024)S(1)} %broadcast_clamp_fusion), kind=kCustom, calls=%fused_computation.4 | custom fusion | bytes 49152 | tf_op jit(solution)/shard_map/gather | solution.py:65
  128.5 23.0 %gather_fusion.3 = s32[4096]{0:T(1024)S(1)} fusion(s32[4096]{0:T(1024)S(1)} %bitcast.96, s32[4096]{0:T(1024)S(1)} %broadcast_clamp_fusion.1), kind=kCustom, calls=%fused_computation.3 | custom fusion | bytes 49152 | tf_op jit(solution)/shard_map/gather | solution.py:45
  151.9 15.7 %scatter_custom_fusion = s32[4096]{0:T(1024)S(1)} fusion(s32[4096]{0:T(1024)S(1)} %compare_select_fusion.10, s32[4096]{0:T(1024)S(1)} %iota.36, s32[]{:T(128)} %copy.31), kind=kCustom, calls=%fused_computation.92 | custom fusion | bytes 16388 | tf_op jit(solution)/shard_map/scatter | solution.py:62
  167.9 79.2 %while.11 = (s32[]{:T(128)}, f32[8,32,16]{2,1,0:T(8,128)S(1)}, pred[8,32,16]{2,1,0:T(8,128)(4,1)S(1)}, s32[8,32]{1,0:T(8,128)S(1)}, s32[8,32,16]{2,1,0:T(8,128)S...) while((s32[]{:T(128)}, f32[8,32,16]{2,1,0:T(8,128)S(1)}, ...), condition=%wide.region_12.13_spmd.clone, body=%wide.region_9.12_spmd.clone.sunk | while | flops 760881792 | bytes 14288633 | solution.py:60
  168.1 4.4 %gather_fusion = bf16[512,32,128]{2,1,0:T(8,128)(2,1)} fusion(bf16[128,32,128]{2,1,0:T(8,128)(2,1)} %get-tuple-element.151, s32[1024]{0:T(1024)S(1)} %pad_clamp_fusion.2), kind=kCustom, calls=%fused_computation.clone.clone.1 | custom fusion | bytes 8390656 | tf_op jit(solution)/shard_map/while/body/eval_jaxpr/vmap()/gather | solution.py:52
  172.5 5.1 %select_reduce_fusion.2 = f32[32,16,32]{2,1,0:T(8,128)S(1)} fusion(bf16[32,16,32,128]{3,2,1,0:T(8,128)(2,1)} %bitcast.100, pred[32,180]{1,0:T(8,128)(4,1)S(1)} %iota_compare_fusion.6, bf16[8,32,180,128]{3,2,1,0:T(8,128)(2,1)} %get-tuple-element.152, s32[]{:T(128)S(6)} %copy.27), kind=kOutput, calls=%fused_computation.11.clone.1 | convolution fusion | flops 760856576 | bytes 5772932 | tf_op jit(solution)/shard_map/while/body/eval_jaxpr/vmap(kqd,pd->kqp)/dot_general | solution.py:53
  177.6 0.1 reduce_sum.36
  178.0 4.4 %gather_fusion = bf16[512,32,128]{2,1,0:T(8,128)(2,1)} fusion(bf16[128,32,128]{2,1,0:T(8,128)(2,1)} %get-tuple-element.151, s32[1024]{0:T(1024)S(1)} %pad_clamp_fusion.2), kind=kCustom, calls=%fused_computation.clone.clone.1 | custom fusion | bytes 8390656 | tf_op jit(solution)/shard_map/while/body/eval_jaxpr/vmap()/gather | solution.py:52
  182.4 5.1 %select_reduce_fusion.2 = f32[32,16,32]{2,1,0:T(8,128)S(1)} fusion(bf16[32,16,32,128]{3,2,1,0:T(8,128)(2,1)} %bitcast.100, pred[32,180]{1,0:T(8,128)(4,1)S(1)} %iota_compare_fusion.6, bf16[8,32,180,128]{3,2,1,0:T(8,128)(2,1)} %get-tuple-element.152, s32[]{:T(128)S(6)} %copy.27), kind=kOutput, calls=%fused_computation.11.clone.1 | convolution fusion | flops 760856576 | bytes 5772932 | tf_op jit(solution)/shard_map/while/body/eval_jaxpr/vmap(kqd,pd->kqp)/dot_general | solution.py:53
  187.5 0.1 reduce_sum.36
  187.9 4.4 %gather_fusion = bf16[512,32,128]{2,1,0:T(8,128)(2,1)} fusion(bf16[128,32,128]{2,1,0:T(8,128)(2,1)} %get-tuple-element.151, s32[1024]{0:T(1024)S(1)} %pad_clamp_fusion.2), kind=kCustom, calls=%fused_computation.clone.clone.1 | custom fusion | bytes 8390656 | tf_op jit(solution)/shard_map/while/body/eval_jaxpr/vmap()/gather | solution.py:52
  192.3 5.1 %select_reduce_fusion.2 = f32[32,16,32]{2,1,0:T(8,128)S(1)} fusion(bf16[32,16,32,128]{3,2,1,0:T(8,128)(2,1)} %bitcast.100, pred[32,180]{1,0:T(8,128)(4,1)S(1)} %iota_compare_fusion.6, bf16[8,32,180,128]{3,2,1,0:T(8,128)(2,1)} %get-tuple-element.152, s32[]{:T(128)S(6)} %copy.27), kind=kOutput, calls=%fused_computation.11.clone.1 | convolution fusion | flops 760856576 | bytes 5772932 | tf_op jit(solution)/shard_map/while/body/eval_jaxpr/vmap(kqd,pd->kqp)/dot_general | solution.py:53
  197.4 0.1 reduce_sum.36
  197.8 4.4 %gather_fusion = bf16[512,32,128]{2,1,0:T(8,128)(2,1)} fusion(bf16[128,32,128]{2,1,0:T(8,128)(2,1)} %get-tuple-element.151, s32[1024]{0:T(1024)S(1)} %pad_clamp_fusion.2), kind=kCustom, calls=%fused_computation.clone.clone.1 | custom fusion | bytes 8390656 | tf_op jit(solution)/shard_map/while/body/eval_jaxpr/vmap()/gather | solution.py:52
  202.2 5.1 %select_reduce_fusion.2 = f32[32,16,32]{2,1,0:T(8,128)S(1)} fusion(bf16[32,16,32,128]{3,2,1,0:T(8,128)(2,1)} %bitcast.100, pred[32,180]{1,0:T(8,128)(4,1)S(1)} %iota_compare_fusion.6, bf16[8,32,180,128]{3,2,1,0:T(8,128)(2,1)} %get-tuple-element.152, s32[]{:T(128)S(6)} %copy.27), kind=kOutput, calls=%fused_computation.11.clone.1 | convolution fusion | flops 760856576 | bytes 5772932 | tf_op jit(solution)/shard_map/while/body/eval_jaxpr/vmap(kqd,pd->kqp)/dot_general | solution.py:53
  207.3 0.1 reduce_sum.36
  207.7 4.4 %gather_fusion = bf16[512,32,128]{2,1,0:T(8,128)(2,1)} fusion(bf16[128,32,128]{2,1,0:T(8,128)(2,1)} %get-tuple-element.151, s32[1024]{0:T(1024)S(1)} %pad_clamp_fusion.2), kind=kCustom, calls=%fused_computation.clone.clone.1 | custom fusion | bytes 8390656 | tf_op jit(solution)/shard_map/while/body/eval_jaxpr/vmap()/gather | solution.py:52
  212.1 5.1 %select_reduce_fusion.2 = f32[32,16,32]{2,1,0:T(8,128)S(1)} fusion(bf16[32,16,32,128]{3,2,1,0:T(8,128)(2,1)} %bitcast.100, pred[32,180]{1,0:T(8,128)(4,1)S(1)} %iota_compare_fusion.6, bf16[8,32,180,128]{3,2,1,0:T(8,128)(2,1)} %get-tuple-element.152, s32[]{:T(128)S(6)} %copy.27), kind=kOutput, calls=%fused_computation.11.clone.1 | convolution fusion | flops 760856576 | bytes 5772932 | tf_op jit(solution)/shard_map/while/body/eval_jaxpr/vmap(kqd,pd->kqp)/dot_general | solution.py:53
  217.2 0.1 reduce_sum.36
  217.6 4.4 %gather_fusion = bf16[512,32,128]{2,1,0:T(8,128)(2,1)} fusion(bf16[128,32,128]{2,1,0:T(8,128)(2,1)} %get-tuple-element.151, s32[1024]{0:T(1024)S(1)} %pad_clamp_fusion.2), kind=kCustom, calls=%fused_computation.clone.clone.1 | custom fusion | bytes 8390656 | tf_op jit(solution)/shard_map/while/body/eval_jaxpr/vmap()/gather | solution.py:52
  222.0 5.1 %select_reduce_fusion.2 = f32[32,16,32]{2,1,0:T(8,128)S(1)} fusion(bf16[32,16,32,128]{3,2,1,0:T(8,128)(2,1)} %bitcast.100, pred[32,180]{1,0:T(8,128)(4,1)S(1)} %iota_compare_fusion.6, bf16[8,32,180,128]{3,2,1,0:T(8,128)(2,1)} %get-tuple-element.152, s32[]{:T(128)S(6)} %copy.27), kind=kOutput, calls=%fused_computation.11.clone.1 | convolution fusion | flops 760856576 | bytes 5772932 | tf_op jit(solution)/shard_map/while/body/eval_jaxpr/vmap(kqd,pd->kqp)/dot_general | solution.py:53
  227.1 0.1 reduce_sum.36
  227.5 4.4 %gather_fusion = bf16[512,32,128]{2,1,0:T(8,128)(2,1)} fusion(bf16[128,32,128]{2,1,0:T(8,128)(2,1)} %get-tuple-element.151, s32[1024]{0:T(1024)S(1)} %pad_clamp_fusion.2), kind=kCustom, calls=%fused_computation.clone.clone.1 | custom fusion | bytes 8390656 | tf_op jit(solution)/shard_map/while/body/eval_jaxpr/vmap()/gather | solution.py:52
  231.9 5.1 %select_reduce_fusion.2 = f32[32,16,32]{2,1,0:T(8,128)S(1)} fusion(bf16[32,16,32,128]{3,2,1,0:T(8,128)(2,1)} %bitcast.100, pred[32,180]{1,0:T(8,128)(4,1)S(1)} %iota_compare_fusion.6, bf16[8,32,180,128]{3,2,1,0:T(8,128)(2,1)} %get-tuple-element.152, s32[]{:T(128)S(6)} %copy.27), kind=kOutput, calls=%fused_computation.11.clone.1 | convolution fusion | flops 760856576 | bytes 5772932 | tf_op jit(solution)/shard_map/while/body/eval_jaxpr/vmap(kqd,pd->kqp)/dot_general | solution.py:53
  237.0 0.1 reduce_sum.36
  237.4 4.4 %gather_fusion = bf16[512,32,128]{2,1,0:T(8,128)(2,1)} fusion(bf16[128,32,128]{2,1,0:T(8,128)(2,1)} %get-tuple-element.151, s32[1024]{0:T(1024)S(1)} %pad_clamp_fusion.2), kind=kCustom, calls=%fused_computation.clone.clone.1 | custom fusion | bytes 8390656 | tf_op jit(solution)/shard_map/while/body/eval_jaxpr/vmap()/gather | solution.py:52
  241.8 5.1 %select_reduce_fusion.2 = f32[32,16,32]{2,1,0:T(8,128)S(1)} fusion(bf16[32,16,32,128]{3,2,1,0:T(8,128)(2,1)} %bitcast.100, pred[32,180]{1,0:T(8,128)(4,1)S(1)} %iota_compare_fusion.6, bf16[8,32,180,128]{3,2,1,0:T(8,128)(2,1)} %get-tuple-element.152, s32[]{:T(128)S(6)} %copy.27), kind=kOutput, calls=%fused_computation.11.clone.1 | convolution fusion | flops 760856576 | bytes 5772932 | tf_op jit(solution)/shard_map/while/body/eval_jaxpr/vmap(kqd,pd->kqp)/dot_general | solution.py:53
  246.9 0.1 reduce_sum.36
  247.1 33.0 %gather_fusion.5 = f32[4096]{0:T(1024)S(1)} fusion(f32[256,16]{0,1:T(8,128)S(1)} %copy.17, s32[4096]{0:T(1024)S(1)} %bitcast.98), kind=kCustom, calls=%fused_computation.5 | custom fusion | bytes 65536 | tf_op jit(solution)/shard_map/gather | solution.py:66
  280.2 12.3 %all_to_all.27 = f32[16,1,256]{2,1,0:T(1,128)S(1)} all-to-all(f32[16,1,256]{2,1,0:T(1,128)S(1)} %compare_select_fusion.5), channel_id=1, replica_groups=mesh['groups'=2,'shard'=16] {'shard'}, dimensions={0} | all-to-all | bytes 32768 | tf_op jit(solution)/shard_map/all_to_all | solution.py:67
  292.5 16.6 %gather_fusion.6 = f32[2048]{0:T(1024)S(1)} fusion(f32[16,256]{1,0:T(8,128)S(1)} %bitcast.97, s32[2048]{0:T(1024)S(1)} %bitcast.99), kind=kCustom, calls=%fused_computation.6 | custom fusion | bytes 32768 | tf_op jit(solution)/shard_map/gather | solution.py:74
  309.1 0.6 reshape.346
  (103 shorter events, 3.6 us)
Async XLA Ops:
  6.5 0.8 copy-start
  7.3 17.3 %copy-start.3 = (s32[2]{0:T(128)S(1)}, s32[2]{0:T(128)}, u32[]{:S(2)}) copy-start(s32[2]{0:T(128)} %constant.108) | copy-start | bytes 28
  7.3 17.4 %copy-start.2 = (s32[2]{0:T(128)S(1)}, s32[2]{0:T(128)}, u32[]{:S(2)}) copy-start(s32[2]{0:T(128)} %constant.105) | copy-start | bytes 28
  7.3 34.3 %copy-start.1 = (s32[256]{0:T(256)S(1)}, s32[256]{0:T(256)}, u32[]{:S(2)}) copy-start(s32[256]{0:T(256)} %param.9) | copy-start | bytes 3076
  33.5 31.2 %all-to-all-start = ((s32[16,1,256]{2,1,0:T(1,128)}), s32[16,1,256]{2,1,0:T(1,128)S(1)}, u32[]{:S(2)}, u32[]{:S(2)}) async-start(s32[16,1,256]{2,1,0:T(1,128)} %bitcast.5), calls=%async_computation | async-start | bytes 32768 | tf_op jit(solution)/shard_map/all_to_all | solution.py:30
  40.8 127.0 %all-gather.2.cloned.1.call-start = ((), (), s32[]{:S(2)}) async-start(), calls=%async_computation.3 | async-start | bytes 1114112 | tf_op jit(solution)/shard_map/all_gather | solution.py:47
  64.6 63.9 %all-to-all-start.1 = ((s32[16,1,256]{2,1,0:T(1,128)}), s32[16,1,256]{2,1,0:T(1,128)S(1)}, u32[]{:S(2)}, u32[]{:S(2)}) async-start(s32[16,1,256]{2,1,0:T(1,128)} %bitcast.9), calls=%async_computation.1 | async-start | bytes 32768 | tf_op jit(solution)/shard_map/all_to_all | solution.py:29
Sparse Core Ops, SparseCore 0:
  43.8 39.2 all-gather.1
where the time goes:
time: 317 us
  local copies, waits for them, and re-layouts  219 us (69%)
  matrix products  40.8 us (13%)
  other arithmetic  15.7 us (5%)
  between operations  13.8 us (4%)
  starting transfers between devices  13.4 us (4%)
  blocking collectives  12.3 us (4%)
    dot_general x8, matrix products, score_tile(): jnp.einsum('kqd,pd->kqp', query_block, document, preferred_element_type=j...  40.8 us
    gather x8, local copies, waits for them, and re-layouts, score_tile(): query_block = whole_queries[rows]  35.3 us
    gather x1, local copies, waits for them, and re-layouts, shards(): tile_scores[safe_slot, entry_rank]  33 us
    unnamed x13, local copies, waits for them, and re-layouts  32.3 us
    gather x1, local copies, waits for them, and re-layouts, shards(): entry_rank = jnp.clip(sorted_place - slot_starts[safe_slot], 0, PMOST - 1)  25.9 us
    gather x3, local copies, waits for them, and re-layouts, shards(): entry_index = order[positions]  23.2 us
    gather x1, local copies, waits for them, and re-layouts, shards(): local_pair = jnp.maximum(entry_pairs[entry_index], 0)  23 us
    gather x1, local copies, waits for them, and re-layouts, shards(): result = returned[target, route_rank].reshape(query_count, CAND)  16.6 us
  transfers between devices with their start and end apart: 3, of which 0 were waited for; matrix products, arithmetic and copies ran while one was open for 38% of the time, Pallas kernels for 0%

commit v1 on v0

v1 whole, which is shorter than its diff:
```python
import functools

import jax
import jax.numpy as jnp
from jax import lax
from jax.experimental import pallas as pl
from jax.experimental.pallas import tpu as pltpu
from jax.sharding import PartitionSpec as P

PMOST = 16
LANES = 128
F32 = jnp.float32
BF16 = jnp.bfloat16
I32 = jnp.int32
NT = (((1,), (1,)), ((), ()))
NN = (((1,), (0,)), ((), ()))
VMEM = pltpu.VMEM
SMEM = pltpu.SMEM
MIB = 2**20


def iota(shape, axis):
    return lax.broadcasted_iota(I32, shape, axis)


def dot(a, b, dims, **kw):
    return lax.dot_general(a, b, dims, preferred_element_type=F32, **kw)


def lookup(table, index):
    parts = []
    for c in range(index.shape[1] // LANES):
        ids = index[:, c * LANES : (c + 1) * LANES]
        lo, hi = ids & (LANES - 1), ids >> 7
        found = jnp.zeros(ids.shape, table[0].dtype)
        for t, tile in enumerate(table):
            got = jnp.take_along_axis(tile, lo, axis=1, mode="promise_in_bounds")
            found = jnp.where(hi == t, got, found)
        parts.append(found)
    return jnp.concatenate(parts, axis=1)


def route_kernel(queries_ref, cand_ref, place_ref, slot_ref, load_ref):
    q_dev, cand = cand_ref.shape
    rows = place_ref.shape[0]
    tokens = queries_ref.shape[0]
    table = [jnp.broadcast_to(place_ref[t : t + 1, :], (q_dev, LANES)) for t in range(rows)]
    slot = lookup(table, cand_ref[...])
    slot_ref[...] = slot
    bits = jnp.zeros((rows, LANES), F32)
    for q in range(q_dev):
        line = slot[q : q + 1, :]
        hi = jnp.where(iota((rows, cand), 0) == (line >> 7), 1.0, 0.0).astype(BF16)
        lo = jnp.where(iota((LANES, cand), 0) == (line & (LANES - 1)), 1.0, 0.0).astype(BF16)
        bits = bits + jnp.where(dot(hi, lo, NT) > 0.5, float(2**q), 0.0)
    load_ref[:tokens, :] = queries_ref[...]
    load_ref[tokens:, :] = bits.astype(BF16)


def turn_kernel(len_ref, in_ref, out_ref):
    tokens, group, d = in_ref.shape
    start = pl.program_id(0) * group
    r, c = iota((group * 16, group * 16), 0), iota((group * 16, group * 16), 1)
    perm = jnp.where(c == (r % 16) * group + r // 16, 1.0, 0.0).astype(BF16)
    first = [None] * group
    for t0 in range(0, tokens, 16):
        n = min(16, tokens - t0)
        x = in_ref[t0 : t0 + n].reshape(n * group, d)
        y = dot(perm[:, : n * group], x, NN)
        for p in range(group):
            rows = y[p * 16 : (p + 1) * 16]
            if t0 == 0:
                first[p] = rows[0:1]
            rows = jnp.where(iota((16, d), 0) < len_ref[start + p] - t0, rows, first[p])
            out_ref[p, t0 : t0 + 16] = rows.astype(BF16)


def score_kernel(n, unroll, me_ref, *refs):
    loads, (pas_ref, out_ref, q_ref, list_vmem, list_smem, best_ref, sem) = refs[:n], refs[n:]
    held = pas_ref.shape[0]
    rows = n * held // LANES
    tokens = loads[0].shape[0] - rows
    per = held // LANES
    q_dev = out_ref.shape[1]
    qt = tokens // q_dev
    total = n * q_dev
    me = me_ref[0]
    for k in range(n):
        q_ref[k * tokens : (k + 1) * tokens, :] = loads[k][:tokens, :]
    bits = jnp.concatenate([loads[k][tokens:, :] for k in range(n)], axis=0)
    halves = []
    for h in range(per):
        pick = iota((n, n * rows), 1) == iota((n, n * rows), 0) * rows + me * per + h
        halves.append(dot(jnp.where(pick, 1.0, 0.0).astype(BF16), bits, NN))
    masks = jnp.concatenate(halves, axis=1).astype(I32)
    named = [
        (jnp.broadcast_to(masks[k : k + 1], (q_dev, held)) >> iota((q_dev, held), 0)) & 1
        for k in range(n)
    ]
    named = jnp.concatenate(named, axis=0)
    below = jnp.where(iota((total, total), 0) > iota((total, total), 1), 1.0, 0.0).astype(BF16)
    rank = dot(below, named.astype(F32).astype(BF16), NN)
    rank = jnp.where(named > 0, rank, -1.0)
    ids = iota((total, held), 0).astype(F32)
    lines = [
        jnp.sum(jnp.where(rank == float(r), ids, 0.0), axis=0, keepdims=True) for r in range(PMOST)
    ]
    list_vmem[...] = jnp.concatenate(lines, axis=0).astype(I32) * qt
    copy = pltpu.make_async_copy(list_vmem, list_smem, sem)
    copy.start()
    copy.wait()

    def step(i, carry):
        for g in range(0, unroll, 8):
            best = []
            for u in range(g, g + 8):
                p = i * unroll + u
                block = jnp.concatenate(
                    [q_ref[pl.ds(pl.multiple_of(list_smem[r, p], qt), qt), :] for r in range(PMOST)],
                    axis=0,
                )
                best.append(jnp.max(dot(pas_ref[p], block, NT), axis=0, keepdims=True))
            at = pl.multiple_of(i * unroll + g, 8)
            best_ref[pl.ds(at, 8), :] = jnp.concatenate(best, axis=0)
        return carry

    lax.fori_loop(0, held // unroll, step, 0)
    wide = PMOST * qt
    mean = jnp.where(iota((PMOST, wide), 1) // qt == iota((PMOST, wide), 0), 1.0 / qt, 0.0)
    score = dot(mean, best_ref[...], NT, precision=lax.Precision.HIGHEST)
    dense = jnp.zeros((total, held), F32)
    for r in range(PMOST):
        dense = jnp.where(rank == float(r), score[r : r + 1, :], dense)
    for k in range(n):
        out_ref[me ^ k] = dense[k * q_dev : (k + 1) * q_dev]


def pick_kernel(slot_ref, back_ref, out_ref):
    n, _, held = back_ref.shape
    table = [
        back_ref[s][:, h * LANES : (h + 1) * LANES] for s in range(n) for h in range(held // LANES)
    ]
    out_ref[...] = lookup(table, slot_ref[...])


def spec(space):
    return pl.BlockSpec(memory_space=space)


def spread(x, n):
    def swap(v, k):
        return lax.ppermute(v, "shard", [(i, i ^ k) for i in range(n)])

    blocks = {0: x}
    for k in range(4, n, 4):
        blocks[k] = swap(x, k)
    for k in range(0, n, 4):
        blocks[k + 2] = swap(blocks[k], 2)
    for k in range(0, n, 2):
        blocks[k + 1] = swap(blocks[k], 1)
    return [blocks[k] for k in range(n)]


def shards(queries, passages, lengths, candidates, placement):
    n = lax.axis_size("shard")
    q_dev, qt, d = queries.shape
    held, pt, _ = passages.shape
    cand = candidates.shape[1]
    me = lax.axis_index("shard").astype(I32).reshape(1)
    rows = n * held // LANES
    tokens = q_dev * qt
    padded = (pt + 15) // 16 * 16
    slot, load = pl.pallas_call(
        route_kernel,
        out_shape=(
            jax.ShapeDtypeStruct((q_dev, cand), I32),
            jax.ShapeDtypeStruct((tokens + rows, d), BF16),
        ),
        name="route",
    )(queries.reshape(tokens, d), candidates, placement.reshape(rows, LANES))
    turned = pl.pallas_call(
        turn_kernel,
        grid=(held // 16,),
        in_specs=[spec(SMEM), pl.BlockSpec((pt, 16, d), lambda i: (0, i, 0))],
        out_specs=pl.BlockSpec((16, padded, d), lambda i: (i, 0, 0)),
        out_shape=jax.ShapeDtypeStruct((held, padded, d), BF16),
        cost_estimate=pl.CostEstimate(
            flops=2 * held * padded * d * 256, bytes_accessed=held * padded * d * 4, transcendentals=0
        ),
        name="turn",
    )(lengths, passages.transpose(1, 0, 2))
    loads = spread(load, n)
    dense = pl.pallas_call(
        functools.partial(score_kernel, n, 16),
        out_shape=jax.ShapeDtypeStruct((n, q_dev, held), F32),
        in_specs=[spec(SMEM)] + [spec(VMEM)] * (n + 1),
        scratch_shapes=[
            VMEM((n * tokens, d), BF16),
            VMEM((PMOST, held), I32),
            SMEM((PMOST, held), I32),
            VMEM((held, PMOST * qt), F32),
            pltpu.SemaphoreType.DMA,
        ],
        compiler_params=pltpu.CompilerParams(vmem_limit_bytes=48 * MIB),
        name="score",
    )(me, *loads, turned)
    back = lax.all_to_all(dense, "shard", split_axis=0, concat_axis=0, tiled=True)
    return pl.pallas_call(
        pick_kernel, out_shape=jax.ShapeDtypeStruct((q_dev, cand), F32), name="pick"
    )(slot, back)


def solution(mesh):
    in_specs = (
        P(("groups", "shard"), None, None),
        P(("groups", "shard"), None, None),
        P(("groups", "shard")),
        P(("groups", "shard"), None),
        P("groups"),
    )
    out_specs = P(("groups", "shard"), None)
    return jax.shard_map(shards, mesh=mesh, in_specs=in_specs, out_specs=out_specs, check_vma=False)
```

time: 317 us -> 75.1 us (0.24)
  local copies, waits for them, and re-layouts: 219 us -> 0.01 us
  Pallas kernels: 0 us -> 43.7 us
  matrix products: 40.8 us -> 0 us
  other arithmetic: 15.7 us -> 0 us
  between operations: 13.8 us -> 0.06 us
  waiting for transfers between devices: 0.71 us -> 5.45 us
    gather x16 -> x0, local copies, waits for them, and re-layouts: 169 us -> none  [the longest x8 35.3 us: score_tile(): query_block = whole_queries[rows]]
    pallas_call x0 -> x4, Pallas kernels: none -> 43.7 us  [the longest x1 22.7 us: shards(): pl.pallas_call(functools.partial(score_kernel, n, 16), out_shape=jax.Shap...]
    dot_general x8 -> x0, matrix products: 40.8 us -> none  [score_tile(): jnp.einsum('kqd,pd->kqp', query_block, document, preferred_element_type=j...]
    unnamed x13 -> x2, local copies, waits for them, and re-layouts: 32.3 us -> 0.01 us
    scatter x1 -> x0, local copies, waits for them, and re-layouts: 15.7 us -> none  [shards(): jnp.zeros((entry_total,), jnp.int32).at[order]]
    all_to_all x2 -> x0, starting transfers between devices: 13.4 us -> none  [the longest x1 7.39 us: shards(): lax.all_to_all(out_slots, 'shard', split_axis=0, concat_axis=0, tiled=True)]
    ppermute x0 -> x15, starting transfers between devices: none -> 12.4 us  [swap(): return lax.ppermute(v, 'shard', [(i, i ^ k) for i in range(n)])]
    sort x1 -> x0, other arithmetic: 5.77 us -> none  [shards(): order = jnp.argsort(sort_key, stable=True)]
  transfers between devices with their start and end apart: 3 -> 15, of which waited for: 0 -> 4; matrix products, arithmetic and copies ran while one was open for 38% -> 0% of each run, Pallas kernels for 0% -> 23%
where the time goes in v1:
time: 75.1 us; the launch traced here: 74.5 us
  Pallas kernels  43.7 us (58%)
  blocking collectives  12.9 us (17%)
  starting transfers between devices  12.4 us (17%)
  waiting for transfers between devices  5.45 us (7%)
    pallas_call x1, Pallas kernels, shards(): pl.pallas_call(functools.partial(score_kernel, n, 16), out_shape=jax.Shap...  22.7 us
    pallas_call x1, Pallas kernels, shards(): pl.pallas_call(turn_kernel, grid=(held // 16,), in_specs=[spec(SMEM), pl....  17.5 us
    all_to_all x1, blocking collectives, shards(): lax.all_to_all(dense, 'shard', split_axis=0, concat_axis=0, tiled=True)  12.9 us
    ppermute x15, starting transfers between devices, swap(): return lax.ppermute(v, 'shard', [(i, i ^ k) for i in range(n)])  12.4 us
    ppermute x15, waiting for transfers between devices, swap(): return lax.ppermute(v, 'shard', [(i, i ^ k) for i in range(n)])  5.45 us
    pallas_call x1, Pallas kernels, shards(): pl.pallas_call(route_kernel, out_shape=(jax.ShapeDtypeStruct((q_dev, cand...  1.92 us
    pallas_call x1, Pallas kernels, shards(): pl.pallas_call(pick_kernel, out_shape=jax.ShapeDtypeStruct((q_dev, cand),...  1.66 us
  transfers between devices with their start and end apart: 15, of which 4 were waited for; matrix products, arithmetic and copies ran while one was open for 0% of the time, Pallas kernels for 23%

profile of v1, /device:TPU:0, one launch (start us, length us, event | category | flops | bytes accessed | tf_op | source)
XLA Modules:
  0.0 74.5 jit_solution(6465299520741587353)
XLA Ops:
  0.0 1.9 %route.1 = (s32[8,256]{1,0:T(8,128)}, bf16[288,128]{1,0:T(8,128)(2,1)}) custom-call(bf16[256,128]{1,0:T(8,128)(2,1)} %bitcast.5, s32[8,256]{1,0:T(8,128)} %cand_ref.1, s32[32,128]{1,0:T(8,128)} %bitcast.6), custom_call_target="tpu_custom_call" | custom-call | tf_op jit(solution)/shard_map/route/pallas_call | solution.py:173
  1.9 0.0 copy-start
  1.9 5.0 %collective-permute-start.11 = (bf16[288,128]{1,0:T(8,128)(2,1)}, bf16[288,128]{1,0:T(8,128)(2,1)S(1)}, u32[]{:S(2)}, u32[]{:S(2)}) collective-permute-start(bf16[288,128]{1,0:T(8,128)(2,1)} %get-tuple-element.8.refs_0_), channel_id=1, source_target_pairs={{0,12},{1,13},{2,14},{3,15},{4,8},{5,9},{6,10},{7,11},{8,4},{9,5},... | collective-permute-start | bytes 221192 | tf_op jit(solution)/shard_map/ppermute | solution.py:152
  7.0 0.0 collective-permute-start.7
  7.0 0.6 collective-permute-start.3
  7.5 1.7 %collective-permute-start.1 = (bf16[288,128]{1,0:T(8,128)(2,1)}, bf16[288,128]{1,0:T(8,128)(2,1)S(1)}, u32[]{:S(2)}, u32[]{:S(2)}) collective-permute-start(bf16[288,128]{1,0:T(8,128)(2,1)} %get-tuple-element.8.refs_0_), channel_id=1, source_target_pairs={{0,2},{1,3},{2,0},{3,1},{4,6},{5,7},{6,4},{7,5},{8,10},{9,11},{10,... | collective-permute-start | bytes 221192 | tf_op jit(solution)/shard_map/ppermute | solution.py:152
  9.3 0.0 collective-permute-start
  9.3 0.8 %collective-permute-done.11.refs_12_ = bf16[288,128]{1,0:T(8,128)(2,1)S(1)} collective-permute-done((bf16[288,128]{1,0:T(8,128)(2,1)}, bf16[288,128]{1,0:T(8,128)(2,1)S(1)}, u32[]{:S(2)}, u32[]{:S(2)}) %collective-permute-start.11) | collective-permute-done | bytes 73760 | tf_op jit(solution)/shard_map/ppermute | solution.py:152
  10.1 1.7 %collective-permute-start.13 = (bf16[288,128]{1,0:T(8,128)(2,1)S(1)}, bf16[288,128]{1,0:T(8,128)(2,1)S(1)}, u32[]{:S(2)}, u32[]{:S(2)}) collective-permute-start(bf16[288,128]{1,0:T(8,128)(2,1)S(1)} %collective-permute-done.11.refs_12_), channel_id=1, source_target_pairs={{0,2},{1,3},{2,0},{3,1},{4,6},{5,7},{6,4},{7,5},{8,10},{9,11},{10,... | collective-permute-start | bytes 221192 | tf_op jit(solution)/shard_map/ppermute | solution.py:152
  11.8 1.6 %collective-permute-done.7.refs_8_ = bf16[288,128]{1,0:T(8,128)(2,1)S(1)} collective-permute-done((bf16[288,128]{1,0:T(8,128)(2,1)}, bf16[288,128]{1,0:T(8,128)(2,1)S(1)}, u32[]{:S(2)}, u32[]{:S(2)}) %collective-permute-start.7) | collective-permute-done | bytes 73760 | tf_op jit(solution)/shard_map/ppermute | solution.py:152
  13.5 0.0 collective-permute-start.12
  13.5 0.0 collective-permute-done.3.refs_4_
  13.5 1.5 %collective-permute-start.9 = (bf16[288,128]{1,0:T(8,128)(2,1)S(1)}, bf16[288,128]{1,0:T(8,128)(2,1)S(1)}, u32[]{:S(2)}, u32[]{:S(2)}) collective-permute-start(bf16[288,128]{1,0:T(8,128)(2,1)S(1)} %collective-permute-done.7.refs_8_), channel_id=1, source_target_pairs={{0,2},{1,3},{2,0},{3,1},{4,6},{5,7},{6,4},{7,5},{8,10},{9,11},{10,... | collective-permute-start | bytes 221192 | tf_op jit(solution)/shard_map/ppermute | solution.py:152
  15.0 0.0 collective-permute-done.1.refs_2_
  15.0 0.2 collective-permute-start.8
  15.2 0.0 collective-permute-done.refs_1_
  15.2 0.5 collective-permute-start.5
  15.7 0.0 collective-permute-done.13.refs_14_
  15.7 0.0 collective-permute-start.4
  15.7 0.0 collective-permute-done.12.refs_13_
  15.7 0.5 collective-permute-start.2
  16.3 1.9 %collective-permute-done.9.refs_10_ = bf16[288,128]{1,0:T(8,128)(2,1)S(1)} collective-permute-done((bf16[288,128]{1,0:T(8,128)(2,1)S(1)}, bf16[288,128]{1,0:T(8,128)(2,1)S(1)}, u32[]{:S(2)}, u32[]{:S(2)}) %collective-permute-start.9) | collective-permute-done | bytes 73760 | tf_op jit(solution)/shard_map/ppermute | solution.py:152
  18.2 0.0 collective-permute-start.14
  18.2 0.0 collective-permute-done.8.refs_9_
  18.2 0.5 collective-permute-start.10
  18.7 1.0 %collective-permute-done.5.refs_6_ = bf16[288,128]{1,0:T(8,128)(2,1)S(1)} collective-permute-done((bf16[288,128]{1,0:T(8,128)(2,1)S(1)}, bf16[288,128]{1,0:T(8,128)(2,1)S(1)}, u32[]{:S(2)}, u32[]{:S(2)}) %collective-permute-start.5) | collective-permute-done | bytes 73760 | tf_op jit(solution)/shard_map/ppermute | solution.py:152
  19.7 0.0 collective-permute-start.6
  19.7 17.5 %turn.1.refs_16_ = bf16[256,192,128]{2,1,0:T(8,128)(2,1)} custom-call(s32[256]{0:T(256)} %len_ref.1, bf16[180,256,128]{2,1,0:T(8,128)(2,1)} %bitcast.4), custom_call_target="tpu_custom_call" | custom-call | flops 3221225472 | bytes 25165824 | tf_op jit(solution)/shard_map/turn/pallas_call | solution.py:181
  37.2 0.0 collective-permute-done.4.refs_5_
  37.2 0.0 collective-permute-done.2.refs_3_
  37.2 0.0 collective-permute-done.14.refs_15_
  37.2 0.0 collective-permute-done.10.refs_11_
  37.2 0.0 collective-permute-done.6.refs_7_
  37.2 0.0 copy-done
  37.3 22.7 %score.1 = f32[16,8,256]{2,1,0:T(8,128)S(1)} custom-call(s32[1]{0:T(128)} %bitcast.2.me_ref, bf16[288,128]{1,0:T(8,128)(2,1)S(1)} %copy-done, bf16[288,128]{1,0:T(8,128)(2,1)S(1)} %collective-permute-done.refs_1_, bf16[288,128]{1,0:T(8,128)(2,1)S(1)} %collective-permute-done.1.refs_2_, bf16[288,128]{1,0:T(8,128)(2,1)S(1)} %collective-permute-done.2.refs_3_, ...), custom_call_target="tpu_custom_call" | custom-call | tf_op jit(solution)/shard_map/score/pallas_call | solution.py:193
  60.0 12.9 %all_to_all.5.back_ref = f32[16,8,256]{2,1,0:T(8,128)} all-to-all(f32[16,8,256]{2,1,0:T(8,128)S(1)} %score.1), channel_id=1, replica_groups=mesh['groups'=2,'shard'=16] {'shard'}, dimensions={0} | all-to-all | bytes 262144 | tf_op jit(solution)/shard_map/all_to_all | solution.py:207
  72.8 1.7 %pick.1 = f32[8,256]{1,0:T(8,128)} custom-call(s32[8,256]{1,0:T(8,128)} %get-tuple-element.7.slot_ref, f32[16,8,256]{2,1,0:T(8,128)} %all_to_all.5.back_ref), custom_call_target="tpu_custom_call" | custom-call | tf_op jit(solution)/shard_map/pick/pallas_call | solution.py:208
Async XLA Ops:
  1.9 35.3 %copy-start = (bf16[288,128]{1,0:T(8,128)(2,1)S(1)}, bf16[288,128]{1,0:T(8,128)(2,1)}, u32[]{:S(2)}) copy-start(bf16[288,128]{1,0:T(8,128)(2,1)} %get-tuple-element.8.refs_0_) | copy-start | bytes 221188
  1.9 8.2 %collective-permute-start.11 = (bf16[288,128]{1,0:T(8,128)(2,1)}, bf16[288,128]{1,0:T(8,128)(2,1)S(1)}, u32[]{:S(2)}, u32[]{:S(2)}) collective-permute-start(bf16[288,128]{1,0:T(8,128)(2,1)} %get-tuple-element.8.refs_0_), channel_id=1, source_target_pairs={{0,12},{1,13},{2,14},{3,15},{4,8},{5,9},{6,10},{7,11},{8,4},{9,5},... | collective-permute-start | bytes 221192 | tf_op jit(solution)/shard_map/ppermute | solution.py:152
  7.0 6.5 %collective-permute-start.7 = (bf16[288,128]{1,0:T(8,128)(2,1)}, bf16[288,128]{1,0:T(8,128)(2,1)S(1)}, u32[]{:S(2)}, u32[]{:S(2)}) collective-permute-start(bf16[288,128]{1,0:T(8,128)(2,1)} %get-tuple-element.8.refs_0_), channel_id=1, source_target_pairs={{0,8},{1,9},{2,10},{3,11},{4,12},{5,13},{6,14},{7,15},{8,0},{9,1},... | collective-permute-start | bytes 221192 | tf_op jit(solution)/shard_map/ppermute | solution.py:152
  7.0 6.5 %collective-permute-start.3 = (bf16[288,128]{1,0:T(8,128)(2,1)}, bf16[288,128]{1,0:T(8,128)(2,1)S(1)}, u32[]{:S(2)}, u32[]{:S(2)}) collective-permute-start(bf16[288,128]{1,0:T(8,128)(2,1)} %get-tuple-element.8.refs_0_), channel_id=1, source_target_pairs={{0,4},{1,5},{2,6},{3,7},{4,0},{5,1},{6,2},{7,3},{8,12},{9,13},{10,... | collective-permute-start | bytes 221192 | tf_op jit(solution)/shard_map/ppermute | solution.py:152
  7.5 7.5 %collective-permute-start.1 = (bf16[288,128]{1,0:T(8,128)(2,1)}, bf16[288,128]{1,0:T(8,128)(2,1)S(1)}, u32[]{:S(2)}, u32[]{:S(2)}) collective-permute-start(bf16[288,128]{1,0:T(8,128)(2,1)} %get-tuple-element.8.refs_0_), channel_id=1, source_target_pairs={{0,2},{1,3},{2,0},{3,1},{4,6},{5,7},{6,4},{7,5},{8,10},{9,11},{10,... | collective-permute-start | bytes 221192 | tf_op jit(solution)/shard_map/ppermute | solution.py:152
  9.3 5.9 %collective-permute-start = (bf16[288,128]{1,0:T(8,128)(2,1)}, bf16[288,128]{1,0:T(8,128)(2,1)S(1)}, u32[]{:S(2)}, u32[]{:S(2)}) collective-permute-start(bf16[288,128]{1,0:T(8,128)(2,1)} %get-tuple-element.8.refs_0_), channel_id=1, source_target_pairs={{0,1},{1,0},{2,3},{3,2},{4,5},{5,4},{6,7},{7,6},{8,9},{9,8},{10,11... | collective-permute-start | bytes 221192 | tf_op jit(solution)/shard_map/ppermute | solution.py:152
  10.1 5.6 %collective-permute-start.13 = (bf16[288,128]{1,0:T(8,128)(2,1)S(1)}, bf16[288,128]{1,0:T(8,128)(2,1)S(1)}, u32[]{:S(2)}, u32[]{:S(2)}) collective-permute-start(bf16[288,128]{1,0:T(8,128)(2,1)S(1)} %collective-permute-done.11.refs_12_), channel_id=1, source_target_pairs={{0,2},{1,3},{2,0},{3,1},{4,6},{5,7},{6,4},{7,5},{8,10},{9,11},{10,... | collective-permute-start | bytes 221192 | tf_op jit(solution)/shard_map/ppermute | solution.py:152
  13.5 2.3 %collective-permute-start.12 = (bf16[288,128]{1,0:T(8,128)(2,1)S(1)}, bf16[288,128]{1,0:T(8,128)(2,1)S(1)}, u32[]{:S(2)}, u32[]{:S(2)}) collective-permute-start(bf16[288,128]{1,0:T(8,128)(2,1)S(1)} %collective-permute-done.11.refs_12_), channel_id=1, source_target_pairs={{0,1},{1,0},{2,3},{3,2},{4,5},{5,4},{6,7},{7,6},{8,9},{9,8},{10,11... | collective-permute-start | bytes 221192 | tf_op jit(solution)/shard_map/ppermute | solution.py:152
  13.5 4.7 %collective-permute-start.9 = (bf16[288,128]{1,0:T(8,128)(2,1)S(1)}, bf16[288,128]{1,0:T(8,128)(2,1)S(1)}, u32[]{:S(2)}, u32[]{:S(2)}) collective-permute-start(bf16[288,128]{1,0:T(8,128)(2,1)S(1)} %collective-permute-done.7.refs_8_), channel_id=1, source_target_pairs={{0,2},{1,3},{2,0},{3,1},{4,6},{5,7},{6,4},{7,5},{8,10},{9,11},{10,... | collective-permute-start | bytes 221192 | tf_op jit(solution)/shard_map/ppermute | solution.py:152
  15.0 3.2 %collective-permute-start.8 = (bf16[288,128]{1,0:T(8,128)(2,1)S(1)}, bf16[288,128]{1,0:T(8,128)(2,1)S(1)}, u32[]{:S(2)}, u32[]{:S(2)}) collective-permute-start(bf16[288,128]{1,0:T(8,128)(2,1)S(1)} %collective-permute-done.7.refs_8_), channel_id=1, source_target_pairs={{0,1},{1,0},{2,3},{3,2},{4,5},{5,4},{6,7},{7,6},{8,9},{9,8},{10,11... | collective-permute-start | bytes 221192 | tf_op jit(solution)/shard_map/ppermute | solution.py:152
  15.2 4.5 %collective-permute-start.5 = (bf16[288,128]{1,0:T(8,128)(2,1)S(1)}, bf16[288,128]{1,0:T(8,128)(2,1)S(1)}, u32[]{:S(2)}, u32[]{:S(2)}) collective-permute-start(bf16[288,128]{1,0:T(8,128)(2,1)S(1)} %collective-permute-done.3.refs_4_), channel_id=1, source_target_pairs={{0,2},{1,3},{2,0},{3,1},{4,6},{5,7},{6,4},{7,5},{8,10},{9,11},{10,... | collective-permute-start | bytes 221192 | tf_op jit(solution)/shard_map/ppermute | solution.py:152
  15.7 21.5 %collective-permute-start.4 = (bf16[288,128]{1,0:T(8,128)(2,1)S(1)}, bf16[288,128]{1,0:T(8,128)(2,1)S(1)}, u32[]{:S(2)}, u32[]{:S(2)}) collective-permute-start(bf16[288,128]{1,0:T(8,128)(2,1)S(1)} %collective-permute-done.3.refs_4_), channel_id=1, source_target_pairs={{0,1},{1,0},{2,3},{3,2},{4,5},{5,4},{6,7},{7,6},{8,9},{9,8},{10,11... | collective-permute-start | bytes 221192 | tf_op jit(solution)/shard_map/ppermute | solution.py:152
  15.7 21.5 %collective-permute-start.2 = (bf16[288,128]{1,0:T(8,128)(2,1)S(1)}, bf16[288,128]{1,0:T(8,128)(2,1)S(1)}, u32[]{:S(2)}, u32[]{:S(2)}) collective-permute-start(bf16[288,128]{1,0:T(8,128)(2,1)S(1)} %collective-permute-done.1.refs_2_), channel_id=1, source_target_pairs={{0,1},{1,0},{2,3},{3,2},{4,5},{5,4},{6,7},{7,6},{8,9},{9,8},{10,11... | collective-permute-start | bytes 221192 | tf_op jit(solution)/shard_map/ppermute | solution.py:152
  18.2 19.0 %collective-permute-start.14 = (bf16[288,128]{1,0:T(8,128)(2,1)S(1)}, bf16[288,128]{1,0:T(8,128)(2,1)S(1)}, u32[]{:S(2)}, u32[]{:S(2)}) collective-permute-start(bf16[288,128]{1,0:T(8,128)(2,1)S(1)} %collective-permute-done.13.refs_14_), channel_id=1, source_target_pairs={{0,1},{1,0},{2,3},{3,2},{4,5},{5,4},{6,7},{7,6},{8,9},{9,8},{10,11... | collective-permute-start | bytes 221192 | tf_op jit(solution)/shard_map/ppermute | solution.py:152
  18.2 19.0 %collective-permute-start.10 = (bf16[288,128]{1,0:T(8,128)(2,1)S(1)}, bf16[288,128]{1,0:T(8,128)(2,1)S(1)}, u32[]{:S(2)}, u32[]{:S(2)}) collective-permute-start(bf16[288,128]{1,0:T(8,128)(2,1)S(1)} %collective-permute-done.9.refs_10_), channel_id=1, source_target_pairs={{0,1},{1,0},{2,3},{3,2},{4,5},{5,4},{6,7},{7,6},{8,9},{9,8},{10,11... | collective-permute-start | bytes 221192 | tf_op jit(solution)/shard_map/ppermute | solution.py:152
  19.7 17.5 %collective-permute-start.6 = (bf16[288,128]{1,0:T(8,128)(2,1)S(1)}, bf16[288,128]{1,0:T(8,128)(2,1)S(1)}, u32[]{:S(2)}, u32[]{:S(2)}) collective-permute-start(bf16[288,128]{1,0:T(8,128)(2,1)S(1)} %collective-permute-done.5.refs_6_), channel_id=1, source_target_pairs={{0,1},{1,0},{2,3},{3,2},{4,5},{5,4},{6,7},{7,6},{8,9},{9,8},{10,11... | collective-permute-start | bytes 221192 | tf_op jit(solution)/shard_map/ppermute | solution.py:152

commit v2 on v1

v2 whole, which is shorter than its diff:
```python
import functools

import jax
import jax.numpy as jnp
from jax import lax
from jax.experimental import pallas as pl
from jax.experimental.pallas import tpu as pltpu
from jax.sharding import PartitionSpec as P

PMOST = 16
LEAST = 45
PITCH = 24
LANES = 128
F32 = jnp.float32
BF16 = jnp.bfloat16
I32 = jnp.int32
NT = (((1,), (1,)), ((), ()))
NN = (((1,), (0,)), ((), ()))
VMEM = pltpu.VMEM
SMEM = pltpu.SMEM
MIB = 2**20


def iota(shape, axis):
    return lax.broadcasted_iota(I32, shape, axis)


def dot(a, b, dims, **kw):
    return lax.dot_general(a, b, dims, preferred_element_type=F32, **kw)


def lookup(table, index):
    parts = []
    for c in range(index.shape[1] // LANES):
        ids = index[:, c * LANES : (c + 1) * LANES]
        lo, hi = ids & (LANES - 1), ids >> 7
        found = jnp.zeros(ids.shape, table[0].dtype)
        for t, tile in enumerate(table):
            got = jnp.take_along_axis(tile, lo, axis=1, mode="promise_in_bounds")
            found = jnp.where(hi == t, got, found)
        parts.append(found)
    return jnp.concatenate(parts, axis=1)


def route_kernel(queries_ref, cand_ref, place_ref, slot_ref, load_ref):
    q_dev, cand = cand_ref.shape
    rows = place_ref.shape[0]
    tokens = queries_ref.shape[0]
    table = [jnp.broadcast_to(place_ref[t : t + 1, :], (q_dev, LANES)) for t in range(rows)]
    slot = lookup(table, cand_ref[...])
    slot_ref[...] = slot
    bits = jnp.zeros((rows, LANES), F32)
    for q in range(q_dev):
        line = slot[q : q + 1, :]
        hi = jnp.where(iota((rows, cand), 0) == (line >> 7), 1.0, 0.0).astype(BF16)
        lo = jnp.where(iota((LANES, cand), 0) == (line & (LANES - 1)), 1.0, 0.0).astype(BF16)
        bits = bits + jnp.where(dot(hi, lo, NT) > 0.5, float(2**q), 0.0)
    load_ref[:tokens, :] = queries_ref[...]
    load_ref[tokens:, :] = bits.astype(BF16)


def turn(len_ref, in_ref, out_ref, wide_ref):
    tokens, held, d = in_ref.shape

    def group(g, carry):
        p0 = pl.multiple_of(g * 16, 16)
        for t in range(tokens):
            wide_ref[t * PITCH : t * PITCH + 16, :] = in_ref[t, pl.ds(p0, 16), :].astype(F32)
        for p in range(16):
            first = wide_ref[p : p + 1, :]
            length = len_ref[p0 + p]
            for t in range(0, tokens, 16):
                rows = wide_ref[pl.ds(p + t * PITCH, 16, stride=PITCH), :]
                if t + 16 > LEAST:
                    rows = jnp.where(iota((16, d), 0) < length - t, rows, first)
                out_ref[p0 + p, t : t + 16] = rows.astype(BF16)
        return carry

    lax.fori_loop(0, held // 16, group, 0)


def score_kernel(n, me_ref, count_ref, len_ref, *refs):
    loads, refs = refs[:n], refs[n:]
    in_ref, out_ref, pas_ref, wide_ref, q_ref, list_vmem, list_smem, best_ref, sem = refs
    held, padded, _ = pas_ref.shape
    rows = n * held // LANES
    tokens = loads[0].shape[0] - rows
    per = held // LANES
    q_dev = out_ref.shape[1]
    qt = tokens // q_dev
    total = n * q_dev
    low, high = (LEAST + 15) // 16, padded // 16
    me = me_ref[0]
    size = jnp.clip((len_ref[...] + 15) // 16, low, high)
    level = iota((16, held), 0)
    member = size == level
    before = jnp.where(iota((held, held), 0) < iota((held, held), 1), 1.0, 0.0).astype(BF16)
    within = dot(jnp.where(member, 1.0, 0.0).astype(BF16), before, NN)
    less = jnp.sum(jnp.where(size < level, 1.0, 0.0), axis=1, keepdims=True)
    upto = jnp.sum(jnp.where(size <= level, 1.0, 0.0), axis=1, keepdims=True)
    place = jnp.sum(jnp.where(member, less + within, 0.0), axis=0, keepdims=True)
    order = jnp.where(iota((held, held), 0) == place.astype(I32), 1.0, 0.0)
    order16 = order.astype(BF16)

    bits = jnp.concatenate([loads[k][tokens:, :] for k in range(n)], axis=0)
    halves = []
    for h in range(per):
        pick = iota((n, n * rows), 1) == iota((n, n * rows), 0) * rows + me * per + h
        halves.append(dot(jnp.where(pick, 1.0, 0.0).astype(BF16), bits, NN))
    masks = jnp.concatenate(halves, axis=1).astype(I32)
    named = [
        (jnp.broadcast_to(masks[k : k + 1], (q_dev, held)) >> iota((q_dev, held), 0)) & 1
        for k in range(n)
    ]
    named = jnp.concatenate(named, axis=0).astype(F32)
    below = jnp.where(iota((total, total), 0) > iota((total, total), 1), 1.0, 0.0).astype(BF16)
    rank = jnp.where(named > 0.5, dot(below, named.astype(BF16), NN) + 1.0, 0.0)
    ranked = dot(rank.astype(BF16), order16, NT)
    ids = iota((total, held), 0).astype(F32)
    lines = [
        jnp.sum(jnp.where(ranked == r + 1.0, ids, 0.0), axis=0, keepdims=True) for r in range(PMOST)
    ]
    list_vmem[0:PMOST, :] = jnp.concatenate(lines, axis=0).astype(I32) * qt
    own = dot(iota((16, held), 1).astype(F32).astype(BF16), order16, NT)
    list_vmem[PMOST : PMOST + 16, :] = own.astype(I32)
    list_vmem[PMOST + 16 :, :] = jnp.broadcast_to(upto, (16, held)).astype(I32)
    copy = pltpu.make_async_copy(list_vmem, list_smem, sem)
    copy.start()
    for k in range(n):
        q_ref[k * tokens : (k + 1) * tokens, :] = loads[k][:tokens, :]
    turn(count_ref, in_ref, pas_ref, wide_ref)
    copy.wait()

    def walk(size, i, carry):
        for g in (0, 8):
            best = []
            for u in range(g, g + 8):
                at = i * 16 + u
                block = jnp.concatenate(
                    [q_ref[pl.ds(pl.multiple_of(list_smem[r, at], qt), qt), :] for r in range(PMOST)],
                    axis=0,
                )
                part = pas_ref[list_smem[PMOST, at], : size * 16]
                best.append(jnp.max(dot(part, block, NT), axis=0, keepdims=True))
            at = pl.multiple_of(i * 16 + g, 8)
            best_ref[pl.ds(at, 8), :] = jnp.concatenate(best, axis=0)
        return carry

    start = 0
    for s in range(low, high + 1):
        stop = list_smem[PMOST + 16 + s, 0] // 16
        lax.fori_loop(start, stop, functools.partial(walk, s), 0)
        start = stop
    wide = PMOST * qt
    mean = jnp.where(iota((PMOST, wide), 1) // qt == iota((PMOST, wide), 0), 1.0 / qt, 0.0)
    score = dot(mean, best_ref[...], NT, precision=lax.Precision.HIGHEST)
    score = dot(score, order, NN, precision=lax.Precision.HIGHEST)
    dense = jnp.zeros((total, held), F32)
    for r in range(PMOST):
        dense = jnp.where(rank == r + 1.0, score[r : r + 1, :], dense)
    for k in range(n):
        out_ref[me ^ k] = dense[k * q_dev : (k + 1) * q_dev]


def pick_kernel(slot_ref, back_ref, out_ref):
    n, _, held = back_ref.shape
    table = [
        back_ref[s][:, h * LANES : (h + 1) * LANES] for s in range(n) for h in range(held // LANES)
    ]
    out_ref[...] = lookup(table, slot_ref[...])


def spec(space):
    return pl.BlockSpec(memory_space=space)


def swap(v, k, n):
    return lax.ppermute(v, "shard", [(i, i ^ k) for i in range(n)])


def shards(queries, passages, lengths, candidates, placement):
    n = lax.axis_size("shard")
    q_dev, qt, d = queries.shape
    held, pt, _ = passages.shape
    cand = candidates.shape[1]
    me = lax.axis_index("shard").astype(I32).reshape(1)
    rows = n * held // LANES
    tokens = q_dev * qt
    padded = (pt + 15) // 16 * 16
    slot, load = pl.pallas_call(
        route_kernel,
        out_shape=(
            jax.ShapeDtypeStruct((q_dev, cand), I32),
            jax.ShapeDtypeStruct((tokens + rows, d), BF16),
        ),
        name="route",
    )(queries.reshape(tokens, d), candidates, placement.reshape(rows, LANES))
    blocks = {0: load}
    for k in range(4, n, 4):
        blocks[k] = swap(load, k, n)
    blocks[2] = swap(load, 2, n)
    blocks[1] = swap(load, 1, n)
    for k in range(4, n, 4):
        blocks[k + 2] = swap(blocks[k], 2, n)
    for k in range(2, n, 2):
        blocks[k + 1] = swap(blocks[k], 1, n)
    loads = [blocks[k] for k in range(n)]
    dense = pl.pallas_call(
        functools.partial(score_kernel, n),
        out_shape=jax.ShapeDtypeStruct((n, q_dev, held), F32),
        in_specs=[spec(SMEM), spec(SMEM), spec(VMEM)] + [spec(VMEM)] * (n + 1),
        scratch_shapes=[
            VMEM((held, padded, d), BF16),
            VMEM((padded * PITCH, d), F32),
            VMEM((n * tokens, d), BF16),
            VMEM((PMOST + 32, held), I32),
            SMEM((PMOST + 32, held), I32),
            VMEM((held, PMOST * qt), F32),
            pltpu.SemaphoreType.DMA,
        ],
        compiler_params=pltpu.CompilerParams(vmem_limit_bytes=36 * MIB),
        name="score",
    )(me, lengths, lengths.reshape(1, held), *loads, passages.transpose(1, 0, 2))
    back = lax.all_to_all(dense, "shard", split_axis=0, concat_axis=0, tiled=True)
    return pl.pallas_call(
        pick_kernel, out_shape=jax.ShapeDtypeStruct((q_dev, cand), F32), name="pick"
    )(slot, back)


def solution(mesh):
    in_specs = (
        P(("groups", "shard"), None, None),
        P(("groups", "shard"), None, None),
        P(("groups", "shard")),
        P(("groups", "shard"), None),
        P("groups"),
    )
    out_specs = P(("groups", "shard"), None)
    return jax.shard_map(shards, mesh=mesh, in_specs=in_specs, out_specs=out_specs, check_vma=False)
```

time: 75.1 us -> 63.7 us (0.85)
  Pallas kernels: 43.7 us -> 25.7 us
  local copies, waits for them, and re-layouts: 0.01 us -> 5.91 us
  waiting for transfers between devices: 5.45 us -> 6.48 us
    pallas_call x2 -> x1, Pallas kernels: 40.2 us -> 22.1 us  [shards(): pl.pallas_call(functools.partial(score_kernel, n), out_shape=jax.ShapeDty...]
    unnamed x2 -> x6, local copies, waits for them, and re-layouts: 0.01 us -> 5.91 us
    ppermute x15, waiting for transfers between devices: 5.45 us -> 6.48 us  [swap(): return lax.ppermute(v, 'shard', [(i, i ^ k) for i in range(n)])]
  transfers between devices with their start and end apart: 15 -> 15, of which waited for: 4 -> 5; matrix products, arithmetic and copies ran while one was open for 0% -> 0% of each run, Pallas kernels for 23% -> 0%
where the time goes in v2:
time: 63.7 us; the launch traced here: 63.3 us
  Pallas kernels  25.7 us (40%)
  blocking collectives  12.6 us (20%)
  starting transfers between devices  12.5 us (20%)
  waiting for transfers between devices  6.48 us (10%)
  local copies, waits for them, and re-layouts  5.91 us (9%)
    pallas_call x1, Pallas kernels, shards(): pl.pallas_call(functools.partial(score_kernel, n), out_shape=jax.ShapeDty...  22.1 us
    all_to_all x1, blocking collectives, shards(): lax.all_to_all(dense, 'shard', split_axis=0, concat_axis=0, tiled=True)  12.6 us
    ppermute x15, starting transfers between devices, swap(): return lax.ppermute(v, 'shard', [(i, i ^ k) for i in range(n)])  12.5 us
    ppermute x15, waiting for transfers between devices, swap(): return lax.ppermute(v, 'shard', [(i, i ^ k) for i in range(n)])  6.48 us
    unnamed x6, local copies, waits for them, and re-layouts  5.91 us
    pallas_call x1, Pallas kernels, shards(): pl.pallas_call(route_kernel, out_shape=(jax.ShapeDtypeStruct((q_dev, cand...  1.94 us
    pallas_call x1, Pallas kernels, shards(): pl.pallas_call(pick_kernel, out_shape=jax.ShapeDtypeStruct((q_dev, cand),...  1.66 us
  transfers between devices with their start and end apart: 15, of which 5 were waited for; matrix products, arithmetic and copies ran while one was open for 0% of the time, Pallas kernels for 0%

profile of v2, /device:TPU:0, one launch (start us, length us, event | category | flops | bytes accessed | tf_op | source)
XLA Modules:
  0.0 63.3 jit_solution(10630371969439552235)
XLA Ops:
  0.0 1.9 %route.1 = (s32[8,256]{1,0:T(8,128)}, bf16[288,128]{1,0:T(8,128)(2,1)}) custom-call(bf16[256,128]{1,0:T(8,128)(2,1)} %bitcast.7, s32[8,256]{1,0:T(8,128)} %cand_ref.1, s32[32,128]{1,0:T(8,128)} %bitcast.8), custom_call_target="tpu_custom_call" | custom-call | tf_op jit(solution)/shard_map/route/pallas_call | solution.py:190
  1.9 5.0 %collective-permute-start.11 = (bf16[288,128]{1,0:T(8,128)(2,1)}, bf16[288,128]{1,0:T(8,128)(2,1)S(1)}, u32[]{:S(2)}, u32[]{:S(2)}) collective-permute-start(bf16[288,128]{1,0:T(8,128)(2,1)} %get-tuple-element.8.refs_0_), channel_id=1, source_target_pairs={{0,12},{1,13},{2,14},{3,15},{4,8},{5,9},{6,10},{7,11},{8,4},{9,5},... | collective-permute-start | bytes 221192 | tf_op jit(solution)/shard_map/ppermute | solution.py:178
  7.0 0.0 collective-permute-start.7
  7.0 0.6 collective-permute-start.3
  7.6 1.7 %collective-permute-start.1 = (bf16[288,128]{1,0:T(8,128)(2,1)}, bf16[288,128]{1,0:T(8,128)(2,1)S(1)}, u32[]{:S(2)}, u32[]{:S(2)}) collective-permute-start(bf16[288,128]{1,0:T(8,128)(2,1)} %get-tuple-element.8.refs_0_), channel_id=1, source_target_pairs={{0,2},{1,3},{2,0},{3,1},{4,6},{5,7},{6,4},{7,5},{8,10},{9,11},{10,... | collective-permute-start | bytes 221192 | tf_op jit(solution)/shard_map/ppermute | solution.py:178
  9.3 0.0 collective-permute-start
  9.3 0.7 %collective-permute-done.11.refs_12_ = bf16[288,128]{1,0:T(8,128)(2,1)S(1)} collective-permute-done((bf16[288,128]{1,0:T(8,128)(2,1)}, bf16[288,128]{1,0:T(8,128)(2,1)S(1)}, u32[]{:S(2)}, u32[]{:S(2)}) %collective-permute-start.11) | collective-permute-done | bytes 73760 | tf_op jit(solution)/shard_map/ppermute | solution.py:178
  10.0 1.9 %collective-permute-start.13 = (bf16[288,128]{1,0:T(8,128)(2,1)S(1)}, bf16[288,128]{1,0:T(8,128)(2,1)S(1)}, u32[]{:S(2)}, u32[]{:S(2)}) collective-permute-start(bf16[288,128]{1,0:T(8,128)(2,1)S(1)} %collective-permute-done.11.refs_12_), channel_id=1, source_target_pairs={{0,2},{1,3},{2,0},{3,1},{4,6},{5,7},{6,4},{7,5},{8,10},{9,11},{10,... | collective-permute-start | bytes 221192 | tf_op jit(solution)/shard_map/ppermute | solution.py:178
  11.8 1.6 %collective-permute-done.7.refs_8_ = bf16[288,128]{1,0:T(8,128)(2,1)S(1)} collective-permute-done((bf16[288,128]{1,0:T(8,128)(2,1)}, bf16[288,128]{1,0:T(8,128)(2,1)S(1)}, u32[]{:S(2)}, u32[]{:S(2)}) %collective-permute-start.7) | collective-permute-done | bytes 73760 | tf_op jit(solution)/shard_map/ppermute | solution.py:178
  13.4 0.0 collective-permute-start.12
  13.4 0.0 collective-permute-done.3.refs_4_
  13.4 1.5 %collective-permute-start.9 = (bf16[288,128]{1,0:T(8,128)(2,1)S(1)}, bf16[288,128]{1,0:T(8,128)(2,1)S(1)}, u32[]{:S(2)}, u32[]{:S(2)}) collective-permute-start(bf16[288,128]{1,0:T(8,128)(2,1)S(1)} %collective-permute-done.7.refs_8_), channel_id=1, source_target_pairs={{0,2},{1,3},{2,0},{3,1},{4,6},{5,7},{6,4},{7,5},{8,10},{9,11},{10,... | collective-permute-start | bytes 221192 | tf_op jit(solution)/shard_map/ppermute | solution.py:178
  14.9 0.0 collective-permute-done.1.refs_2_
  14.9 0.2 collective-permute-start.8
  15.2 0.0 collective-permute-done.refs_1_
  15.2 0.5 collective-permute-start.5
  15.7 0.0 collective-permute-done.13.refs_14_
  15.7 0.0 collective-permute-start.4
  15.7 0.0 collective-permute-done.12.refs_13_
  15.7 0.5 collective-permute-start.2
  16.2 1.9 %collective-permute-done.9.refs_10_ = bf16[288,128]{1,0:T(8,128)(2,1)S(1)} collective-permute-done((bf16[288,128]{1,0:T(8,128)(2,1)S(1)}, bf16[288,128]{1,0:T(8,128)(2,1)S(1)}, u32[]{:S(2)}, u32[]{:S(2)}) %collective-permute-start.9) | collective-permute-done | bytes 73760 | tf_op jit(solution)/shard_map/ppermute | solution.py:178
  18.1 0.0 collective-permute-start.14
  18.1 0.0 collective-permute-done.8.refs_9_
  18.1 0.5 collective-permute-start.10
  18.7 1.0 %collective-permute-done.5.refs_6_ = bf16[288,128]{1,0:T(8,128)(2,1)S(1)} collective-permute-done((bf16[288,128]{1,0:T(8,128)(2,1)S(1)}, bf16[288,128]{1,0:T(8,128)(2,1)S(1)}, u32[]{:S(2)}, u32[]{:S(2)}) %collective-permute-start.5) | collective-permute-done | bytes 73760 | tf_op jit(solution)/shard_map/ppermute | solution.py:178
  19.7 0.0 collective-permute-start.6
  19.7 0.0 collective-permute-done.4.refs_5_
  19.7 0.0 collective-permute-done.2.refs_3_
  19.7 0.0 collective-permute-done.14.refs_15_
  19.7 0.0 collective-permute-done.10.refs_11_
  19.7 1.2 %collective-permute-done.6.refs_7_ = bf16[288,128]{1,0:T(8,128)(2,1)S(1)} collective-permute-done((bf16[288,128]{1,0:T(8,128)(2,1)S(1)}, bf16[288,128]{1,0:T(8,128)(2,1)S(1)}, u32[]{:S(2)}, u32[]{:S(2)}) %collective-permute-start.6) | collective-permute-done | bytes 73760 | tf_op jit(solution)/shard_map/ppermute | solution.py:178
  20.9 0.0 copy-start
  20.9 4.3 %copy-done = bf16[256,180,128]{2,0,1:T(8,128)(2,1)S(1)} copy-done((bf16[256,180,128]{2,0,1:T(8,128)(2,1)S(1)}, bf16[256,180,128]{2,0,1:T(8,128)(2,1)}, u32[]{:S(2)}) %copy-start) | copy-done | bytes 11796504
  25.3 0.0 copy-start.1
  25.3 0.9 %copy-done.1 = bf16[288,128]{1,0:T(8,128)(2,1)S(1)} copy-done((bf16[288,128]{1,0:T(8,128)(2,1)S(1)}, bf16[288,128]{1,0:T(8,128)(2,1)}, u32[]{:S(2)}) %copy-start.1) | copy-done | bytes 73752
  26.2 0.0 copy-start.2
  26.2 0.7 %copy-done.2 = s32[256]{0:T(256)S(1)} copy-done((s32[256]{0:T(256)S(1)}, s32[256]{0:T(256)}, u32[]{:S(2)}) %copy-start.2) | copy-done | bytes 1048
  26.9 22.1 %score.1 = f32[16,8,256]{2,1,0:T(8,128)S(1)} custom-call(s32[1]{0:T(128)} %bitcast.2.me_ref, s32[256]{0:T(256)S(1)} %copy-done.2, s32[1,256]{1,0:T(1,128)S(1)} %bitcast.6, bf16[288,128]{1,0:T(8,128)(2,1)S(1)} %copy-done.1, bf16[288,128]{1,0:T(8,128)(2,1)S(1)} %collective-permute-done.refs_1_, bf16[288,128]{1,0:T(8,128)(2,1)S(1)} %collective-permute-done.1.refs_2_, ...), custom_call_target="tpu_custom_call" | custom-call | tf_op jit(solution)/shard_map/score/pallas_call | solution.py:208
  49.0 12.6 %all_to_all.5.back_ref = f32[16,8,256]{2,1,0:T(8,128)} all-to-all(f32[16,8,256]{2,1,0:T(8,128)S(1)} %score.1), channel_id=1, replica_groups=mesh['groups'=2,'shard'=16] {'shard'}, dimensions={0} | all-to-all | bytes 262144 | tf_op jit(solution)/shard_map/all_to_all | solution.py:224
  61.6 1.7 %pick.1 = f32[8,256]{1,0:T(8,128)} custom-call(s32[8,256]{1,0:T(8,128)} %get-tuple-element.7.slot_ref, f32[16,8,256]{2,1,0:T(8,128)} %all_to_all.5.back_ref), custom_call_target="tpu_custom_call" | custom-call | tf_op jit(solution)/shard_map/pick/pallas_call | solution.py:225
Async XLA Ops:
  1.9 8.0 %collective-permute-start.11 = (bf16[288,128]{1,0:T(8,128)(2,1)}, bf16[288,128]{1,0:T(8,128)(2,1)S(1)}, u32[]{:S(2)}, u32[]{:S(2)}) collective-permute-start(bf16[288,128]{1,0:T(8,128)(2,1)} %get-tuple-element.8.refs_0_), channel_id=1, source_target_pairs={{0,12},{1,13},{2,14},{3,15},{4,8},{5,9},{6,10},{7,11},{8,4},{9,5},... | collective-permute-start | bytes 221192 | tf_op jit(solution)/shard_map/ppermute | solution.py:178
  7.0 6.4 %collective-permute-start.7 = (bf16[288,128]{1,0:T(8,128)(2,1)}, bf16[288,128]{1,0:T(8,128)(2,1)S(1)}, u32[]{:S(2)}, u32[]{:S(2)}) collective-permute-start(bf16[288,128]{1,0:T(8,128)(2,1)} %get-tuple-element.8.refs_0_), channel_id=1, source_target_pairs={{0,8},{1,9},{2,10},{3,11},{4,12},{5,13},{6,14},{7,15},{8,0},{9,1},... | collective-permute-start | bytes 221192 | tf_op jit(solution)/shard_map/ppermute | solution.py:178
  7.0 6.4 %collective-permute-start.3 = (bf16[288,128]{1,0:T(8,128)(2,1)}, bf16[288,128]{1,0:T(8,128)(2,1)S(1)}, u32[]{:S(2)}, u32[]{:S(2)}) collective-permute-start(bf16[288,128]{1,0:T(8,128)(2,1)} %get-tuple-element.8.refs_0_), channel_id=1, source_target_pairs={{0,4},{1,5},{2,6},{3,7},{4,0},{5,1},{6,2},{7,3},{8,12},{9,13},{10,... | collective-permute-start | bytes 221192 | tf_op jit(solution)/shard_map/ppermute | solution.py:178
  7.6 7.4 %collective-permute-start.1 = (bf16[288,128]{1,0:T(8,128)(2,1)}, bf16[288,128]{1,0:T(8,128)(2,1)S(1)}, u32[]{:S(2)}, u32[]{:S(2)}) collective-permute-start(bf16[288,128]{1,0:T(8,128)(2,1)} %get-tuple-element.8.refs_0_), channel_id=1, source_target_pairs={{0,2},{1,3},{2,0},{3,1},{4,6},{5,7},{6,4},{7,5},{8,10},{9,11},{10,... | collective-permute-start | bytes 221192 | tf_op jit(solution)/shard_map/ppermute | solution.py:178
  9.3 5.9 %collective-permute-start = (bf16[288,128]{1,0:T(8,128)(2,1)}, bf16[288,128]{1,0:T(8,128)(2,1)S(1)}, u32[]{:S(2)}, u32[]{:S(2)}) collective-permute-start(bf16[288,128]{1,0:T(8,128)(2,1)} %get-tuple-element.8.refs_0_), channel_id=1, source_target_pairs={{0,1},{1,0},{2,3},{3,2},{4,5},{5,4},{6,7},{7,6},{8,9},{9,8},{10,11... | collective-permute-start | bytes 221192 | tf_op jit(solution)/shard_map/ppermute | solution.py:178
  10.0 5.7 %collective-permute-start.13 = (bf16[288,128]{1,0:T(8,128)(2,1)S(1)}, bf16[288,128]{1,0:T(8,128)(2,1)S(1)}, u32[]{:S(2)}, u32[]{:S(2)}) collective-permute-start(bf16[288,128]{1,0:T(8,128)(2,1)S(1)} %collective-permute-done.11.refs_12_), channel_id=1, source_target_pairs={{0,2},{1,3},{2,0},{3,1},{4,6},{5,7},{6,4},{7,5},{8,10},{9,11},{10,... | collective-permute-start | bytes 221192 | tf_op jit(solution)/shard_map/ppermute | solution.py:178
  13.4 2.3 %collective-permute-start.12 = (bf16[288,128]{1,0:T(8,128)(2,1)S(1)}, bf16[288,128]{1,0:T(8,128)(2,1)S(1)}, u32[]{:S(2)}, u32[]{:S(2)}) collective-permute-start(bf16[288,128]{1,0:T(8,128)(2,1)S(1)} %collective-permute-done.11.refs_12_), channel_id=1, source_target_pairs={{0,1},{1,0},{2,3},{3,2},{4,5},{5,4},{6,7},{7,6},{8,9},{9,8},{10,11... | collective-permute-start | bytes 221192 | tf_op jit(solution)/shard_map/ppermute | solution.py:178
  13.4 4.7 %collective-permute-start.9 = (bf16[288,128]{1,0:T(8,128)(2,1)S(1)}, bf16[288,128]{1,0:T(8,128)(2,1)S(1)}, u32[]{:S(2)}, u32[]{:S(2)}) collective-permute-start(bf16[288,128]{1,0:T(8,128)(2,1)S(1)} %collective-permute-done.7.refs_8_), channel_id=1, source_target_pairs={{0,2},{1,3},{2,0},{3,1},{4,6},{5,7},{6,4},{7,5},{8,10},{9,11},{10,... | collective-permute-start | bytes 221192 | tf_op jit(solution)/shard_map/ppermute | solution.py:178
  14.9 3.2 %collective-permute-start.8 = (bf16[288,128]{1,0:T(8,128)(2,1)S(1)}, bf16[288,128]{1,0:T(8,128)(2,1)S(1)}, u32[]{:S(2)}, u32[]{:S(2)}) collective-permute-start(bf16[288,128]{1,0:T(8,128)(2,1)S(1)} %collective-permute-done.7.refs_8_), channel_id=1, source_target_pairs={{0,1},{1,0},{2,3},{3,2},{4,5},{5,4},{6,7},{7,6},{8,9},{9,8},{10,11... | collective-permute-start | bytes 221192 | tf_op jit(solution)/shard_map/ppermute | solution.py:178
  15.2 4.5 %collective-permute-start.5 = (bf16[288,128]{1,0:T(8,128)(2,1)S(1)}, bf16[288,128]{1,0:T(8,128)(2,1)S(1)}, u32[]{:S(2)}, u32[]{:S(2)}) collective-permute-start(bf16[288,128]{1,0:T(8,128)(2,1)S(1)} %collective-permute-done.3.refs_4_), channel_id=1, source_target_pairs={{0,2},{1,3},{2,0},{3,1},{4,6},{5,7},{6,4},{7,5},{8,10},{9,11},{10,... | collective-permute-start | bytes 221192 | tf_op jit(solution)/shard_map/ppermute | solution.py:178
  15.7 4.0 %collective-permute-start.4 = (bf16[288,128]{1,0:T(8,128)(2,1)S(1)}, bf16[288,128]{1,0:T(8,128)(2,1)S(1)}, u32[]{:S(2)}, u32[]{:S(2)}) collective-permute-start(bf16[288,128]{1,0:T(8,128)(2,1)S(1)} %collective-permute-done.3.refs_4_), channel_id=1, source_target_pairs={{0,1},{1,0},{2,3},{3,2},{4,5},{5,4},{6,7},{7,6},{8,9},{9,8},{10,11... | collective-permute-start | bytes 221192 | tf_op jit(solution)/shard_map/ppermute | solution.py:178
  15.7 4.0 %collective-permute-start.2 = (bf16[288,128]{1,0:T(8,128)(2,1)S(1)}, bf16[288,128]{1,0:T(8,128)(2,1)S(1)}, u32[]{:S(2)}, u32[]{:S(2)}) collective-permute-start(bf16[288,128]{1,0:T(8,128)(2,1)S(1)} %collective-permute-done.1.refs_2_), channel_id=1, source_target_pairs={{0,1},{1,0},{2,3},{3,2},{4,5},{5,4},{6,7},{7,6},{8,9},{9,8},{10,11... | collective-permute-start | bytes 221192 | tf_op jit(solution)/shard_map/ppermute | solution.py:178
  18.1 1.6 %collective-permute-start.14 = (bf16[288,128]{1,0:T(8,128)(2,1)S(1)}, bf16[288,128]{1,0:T(8,128)(2,1)S(1)}, u32[]{:S(2)}, u32[]{:S(2)}) collective-permute-start(bf16[288,128]{1,0:T(8,128)(2,1)S(1)} %collective-permute-done.13.refs_14_), channel_id=1, source_target_pairs={{0,1},{1,0},{2,3},{3,2},{4,5},{5,4},{6,7},{7,6},{8,9},{9,8},{10,11... | collective-permute-start | bytes 221192 | tf_op jit(solution)/shard_map/ppermute | solution.py:178
  18.1 1.6 %collective-permute-start.10 = (bf16[288,128]{1,0:T(8,128)(2,1)S(1)}, bf16[288,128]{1,0:T(8,128)(2,1)S(1)}, u32[]{:S(2)}, u32[]{:S(2)}) collective-permute-start(bf16[288,128]{1,0:T(8,128)(2,1)S(1)} %collective-permute-done.9.refs_10_), channel_id=1, source_target_pairs={{0,1},{1,0},{2,3},{3,2},{4,5},{5,4},{6,7},{7,6},{8,9},{9,8},{10,11... | collective-permute-start | bytes 221192 | tf_op jit(solution)/shard_map/ppermute | solution.py:178
  19.7 1.3 %collective-permute-start.6 = (bf16[288,128]{1,0:T(8,128)(2,1)S(1)}, bf16[288,128]{1,0:T(8,128)(2,1)S(1)}, u32[]{:S(2)}, u32[]{:S(2)}) collective-permute-start(bf16[288,128]{1,0:T(8,128)(2,1)S(1)} %collective-permute-done.5.refs_6_), channel_id=1, source_target_pairs={{0,1},{1,0},{2,3},{3,2},{4,5},{5,4},{6,7},{7,6},{8,9},{9,8},{10,11... | collective-permute-start | bytes 221192 | tf_op jit(solution)/shard_map/ppermute | solution.py:178
  20.9 4.4 %copy-start = (bf16[256,180,128]{2,0,1:T(8,128)(2,1)S(1)}, bf16[256,180,128]{2,0,1:T(8,128)(2,1)}, u32[]{:S(2)}) copy-start(bf16[256,180,128]{2,0,1:T(8,128)(2,1)} %param.6) | copy-start | bytes 35389444
  25.3 0.9 %copy-start.1 = (bf16[288,128]{1,0:T(8,128)(2,1)S(1)}, bf16[288,128]{1,0:T(8,128)(2,1)}, u32[]{:S(2)}) copy-start(bf16[288,128]{1,0:T(8,128)(2,1)} %get-tuple-element.8.refs_0_) | copy-start | bytes 221188
  26.2 0.7 %copy-start.2 = (s32[256]{0:T(256)S(1)}, s32[256]{0:T(256)}, u32[]{:S(2)}) copy-start(s32[256]{0:T(256)} %count_ref.1) | copy-start | bytes 3076

commit v3 on v2

--- a/solution.py
+++ b/solution.py
@@ -9,7 +9,7 @@
 
 PMOST = 16
 LEAST = 45
-PITCH = 24
+PITCH = 17
 LANES = 128
 F32 = jnp.float32
 BF16 = jnp.bfloat16
@@ -59,30 +59,40 @@
     load_ref[tokens:, :] = bits.astype(BF16)
 
 
-def turn(len_ref, in_ref, out_ref, wide_ref):
-    tokens, held, d = in_ref.shape
+def turn(len_ref, in_ref, out_ref, wide_ref, first, last):
+    tokens, _, d = in_ref.shape
 
     def group(g, carry):
         p0 = pl.multiple_of(g * 16, 16)
         for t in range(tokens):
             wide_ref[t * PITCH : t * PITCH + 16, :] = in_ref[t, pl.ds(p0, 16), :].astype(F32)
         for p in range(16):
-            first = wide_ref[p : p + 1, :]
+            live = wide_ref[p : p + 1, :]
             length = len_ref[p0 + p]
             for t in range(0, tokens, 16):
                 rows = wide_ref[pl.ds(p + t * PITCH, 16, stride=PITCH), :]
                 if t + 16 > LEAST:
-                    rows = jnp.where(iota((16, d), 0) < length - t, rows, first)
+                    rows = jnp.where(iota((16, d), 0) < length - t, rows, live)
                 out_ref[p0 + p, t : t + 16] = rows.astype(BF16)
         return carry
 
-    lax.fori_loop(0, held // 16, group, 0)
+    lax.fori_loop(first // 16, last // 16, group, 0)
 
 
 def score_kernel(n, me_ref, count_ref, len_ref, *refs):
     loads, refs = refs[:n], refs[n:]
-    in_ref, out_ref, pas_ref, wide_ref, q_ref, list_vmem, list_smem, best_ref, sem = refs
+    source_ref, out_ref, in_ref, pas_ref, wide_ref = refs[:5]
+    q_ref, list_vmem, list_smem, best_ref, sems = refs[5:]
     held, padded, _ = pas_ref.shape
+    parts = sems.shape[0] - 1
+    step = held // parts
+
+    def fetch(i):
+        at = pl.ds(i * step, step)
+        return pltpu.make_async_copy(source_ref.at[:, at], in_ref.at[:, at], sems.at[i])
+
+    for i in range(parts):
+        fetch(i).start()
     rows = n * held // LANES
     tokens = loads[0].shape[0] - rows
     per = held // LANES
@@ -124,11 +134,13 @@
     own = dot(iota((16, held), 1).astype(F32).astype(BF16), order16, NT)
     list_vmem[PMOST : PMOST + 16, :] = own.astype(I32)
     list_vmem[PMOST + 16 :, :] = jnp.broadcast_to(upto, (16, held)).astype(I32)
-    copy = pltpu.make_async_copy(list_vmem, list_smem, sem)
+    copy = pltpu.make_async_copy(list_vmem, list_smem, sems.at[parts])
     copy.start()
     for k in range(n):
         q_ref[k * tokens : (k + 1) * tokens, :] = loads[k][:tokens, :]
-    turn(count_ref, in_ref, pas_ref, wide_ref)
+    for i in range(parts):
+        fetch(i).wait()
+        turn(count_ref, in_ref, pas_ref, wide_ref, i * step, (i + 1) * step)
     copy.wait()
 
     def walk(size, i, carry):
@@ -208,22 +220,26 @@
     dense = pl.pallas_call(
         functools.partial(score_kernel, n),
         out_shape=jax.ShapeDtypeStruct((n, q_dev, held), F32),
-        in_specs=[spec(SMEM), spec(SMEM), spec(VMEM)] + [spec(VMEM)] * (n + 1),
+        in_specs=[spec(SMEM), spec(SMEM), spec(VMEM)] + [spec(VMEM)] * n + [spec(pltpu.HBM)],
         scratch_shapes=[
+            VMEM((pt, held, d), BF16),
             VMEM((held, padded, d), BF16),
             VMEM((padded * PITCH, d), F32),
             VMEM((n * tokens, d), BF16),
             VMEM((PMOST + 32, held), I32),
             SMEM((PMOST + 32, held), I32),
             VMEM((held, PMOST * qt), F32),
-            pltpu.SemaphoreType.DMA,
+            pltpu.SemaphoreType.DMA((5,)),
         ],
-        compiler_params=pltpu.CompilerParams(vmem_limit_bytes=36 * MIB),
+        compiler_params=pltpu.CompilerParams(vmem_limit_bytes=56 * MIB),
         name="score",
-    )(me, lengths, lengths.reshape(1, held), *loads, passages.transpose(1, 0, 2))
+    )(me, lengths, lengths.reshape(1, held), *loads, pltpu.with_memory_space_constraint(passages.transpose(1, 0, 2), pltpu.HBM))
     back = lax.all_to_all(dense, "shard", split_axis=0, concat_axis=0, tiled=True)
     return pl.pallas_call(
-        pick_kernel, out_shape=jax.ShapeDtypeStruct((q_dev, cand), F32), name="pick"
+        pick_kernel,
+        out_shape=jax.ShapeDtypeStruct((q_dev, cand), F32),
+        compiler_params=pltpu.CompilerParams(vmem_limit_bytes=8 * MIB),
+        name="pick",
     )(slot, back)
 
 

time: 63.7 us -> 58.3 us (0.915)
  local copies, waits for them, and re-layouts: 5.91 us -> 0.57 us
    unnamed x6 -> x32, local copies, waits for them, and re-layouts: 5.91 us -> 0.57 us
    pallas_call x1, Pallas kernels: 1.66 us -> 0.74 us  [shards(): pl.pallas_call(pick_kernel, out_shape=jax.ShapeDtypeStruct((q_dev, cand),...]
    pallas_call x1, Pallas kernels: 22.1 us -> 22.9 us  [shards(): pl.pallas_call(functools.partial(score_kernel, n), out_shape=jax.ShapeDty...]
where the time goes in v3:
time: 58.3 us; the launch traced here: 58.1 us
  Pallas kernels  25.5 us (44%)
  blocking collectives  12.8 us (22%)
  starting transfers between devices  12.5 us (21%)
  waiting for transfers between devices  6.44 us (11%)
    pallas_call x1, Pallas kernels, shards(): pl.pallas_call(functools.partial(score_kernel, n), out_shape=jax.ShapeDty...  22.9 us
    all_to_all x1, blocking collectives, shards(): lax.all_to_all(dense, 'shard', split_axis=0, concat_axis=0, tiled=True)  12.8 us
    ppermute x15, starting transfers between devices, swap(): return lax.ppermute(v, 'shard', [(i, i ^ k) for i in range(n)])  12.5 us
    ppermute x15, waiting for transfers between devices, swap(): return lax.ppermute(v, 'shard', [(i, i ^ k) for i in range(n)])  6.44 us
    pallas_call x1, Pallas kernels, shards(): pl.pallas_call(route_kernel, out_shape=(jax.ShapeDtypeStruct((q_dev, cand...  1.91 us
  transfers between devices with their start and end apart: 15, of which 5 were waited for; matrix products, arithmetic and copies ran while one was open for 0% of the time, Pallas kernels for 0%

profile of v3, /device:TPU:0, one launch (start us, length us, event | category | flops | bytes accessed | tf_op | source)
XLA Modules:
  0.0 58.1 jit_solution(18312508302033398345)
XLA Ops:
  0.0 1.9 %route.1 = (s32[8,256]{1,0:T(8,128)}, bf16[288,128]{1,0:T(8,128)(2,1)}) custom-call(bf16[256,128]{1,0:T(8,128)(2,1)} %bitcast.6, s32[8,256]{1,0:T(8,128)} %cand_ref.1, s32[32,128]{1,0:T(8,128)} %bitcast.7), custom_call_target="tpu_custom_call" | custom-call | tf_op jit(solution)/shard_map/route/pallas_call | solution.py:202
  1.9 5.0 %collective-permute-start.11 = (bf16[288,128]{1,0:T(8,128)(2,1)}, bf16[288,128]{1,0:T(8,128)(2,1)S(1)}, u32[]{:S(2)}, u32[]{:S(2)}) collective-permute-start(bf16[288,128]{1,0:T(8,128)(2,1)} %get-tuple-element.8.refs_0_), channel_id=1, source_target_pairs={{0,12},{1,13},{2,14},{3,15},{4,8},{5,9},{6,10},{7,11},{8,4},{9,5},... | collective-permute-start | bytes 221192 | tf_op jit(solution)/shard_map/ppermute | solution.py:190
  7.0 0.0 collective-permute-start.7
  7.0 0.6 collective-permute-start.3
  7.5 1.7 %collective-permute-start.1 = (bf16[288,128]{1,0:T(8,128)(2,1)}, bf16[288,128]{1,0:T(8,128)(2,1)S(1)}, u32[]{:S(2)}, u32[]{:S(2)}) collective-permute-start(bf16[288,128]{1,0:T(8,128)(2,1)} %get-tuple-element.8.refs_0_), channel_id=1, source_target_pairs={{0,2},{1,3},{2,0},{3,1},{4,6},{5,7},{6,4},{7,5},{8,10},{9,11},{10,... | collective-permute-start | bytes 221192 | tf_op jit(solution)/shard_map/ppermute | solution.py:190
  9.3 0.0 collective-permute-start
  9.3 0.7 %collective-permute-done.11.refs_12_ = bf16[288,128]{1,0:T(8,128)(2,1)S(1)} collective-permute-done((bf16[288,128]{1,0:T(8,128)(2,1)}, bf16[288,128]{1,0:T(8,128)(2,1)S(1)}, u32[]{:S(2)}, u32[]{:S(2)}) %collective-permute-start.11) | collective-permute-done | bytes 73760 | tf_op jit(solution)/shard_map/ppermute | solution.py:190
  10.0 1.9 %collective-permute-start.13 = (bf16[288,128]{1,0:T(8,128)(2,1)S(1)}, bf16[288,128]{1,0:T(8,128)(2,1)S(1)}, u32[]{:S(2)}, u32[]{:S(2)}) collective-permute-start(bf16[288,128]{1,0:T(8,128)(2,1)S(1)} %collective-permute-done.11.refs_12_), channel_id=1, source_target_pairs={{0,2},{1,3},{2,0},{3,1},{4,6},{5,7},{6,4},{7,5},{8,10},{9,11},{10,... | collective-permute-start | bytes 221192 | tf_op jit(solution)/shard_map/ppermute | solution.py:190
  11.8 1.6 %collective-permute-done.7.refs_8_ = bf16[288,128]{1,0:T(8,128)(2,1)S(1)} collective-permute-done((bf16[288,128]{1,0:T(8,128)(2,1)}, bf16[288,128]{1,0:T(8,128)(2,1)S(1)}, u32[]{:S(2)}, u32[]{:S(2)}) %collective-permute-start.7) | collective-permute-done | bytes 73760 | tf_op jit(solution)/shard_map/ppermute | solution.py:190
  13.4 0.0 collective-permute-start.12
  13.4 0.0 collective-permute-done.3.refs_4_
  13.4 0.0 copy-start.3
  13.4 1.6 %collective-permute-start.9 = (bf16[288,128]{1,0:T(8,128)(2,1)S(1)}, bf16[288,128]{1,0:T(8,128)(2,1)S(1)}, u32[]{:S(2)}, u32[]{:S(2)}) collective-permute-start(bf16[288,128]{1,0:T(8,128)(2,1)S(1)} %collective-permute-done.7.refs_8_), channel_id=1, source_target_pairs={{0,2},{1,3},{2,0},{3,1},{4,6},{5,7},{6,4},{7,5},{8,10},{9,11},{10,... | collective-permute-start | bytes 221192 | tf_op jit(solution)/shard_map/ppermute | solution.py:190
  15.0 0.0 collective-permute-done.1.refs_2_
  15.0 0.2 collective-permute-start.8
  15.2 0.0 collective-permute-done.refs_1_
  15.2 0.5 collective-permute-start.5
  15.7 0.0 collective-permute-done.13.refs_14_
  15.7 0.1 collective-permute-start.4
  15.7 0.0 collective-permute-done.12.refs_13_
  15.8 0.4 collective-permute-start.2
  16.2 1.9 %collective-permute-done.9.refs_10_ = bf16[288,128]{1,0:T(8,128)(2,1)S(1)} collective-permute-done((bf16[288,128]{1,0:T(8,128)(2,1)S(1)}, bf16[288,128]{1,0:T(8,128)(2,1)S(1)}, u32[]{:S(2)}, u32[]{:S(2)}) %collective-permute-start.9) | collective-permute-done | bytes 73760 | tf_op jit(solution)/shard_map/ppermute | solution.py:190
  18.1 0.0 collective-permute-start.14
  18.1 0.0 collective-permute-done.8.refs_9_
  18.1 0.0 copy-start.9
  18.1 0.5 collective-permute-start.10
  18.6 1.1 %collective-permute-done.5.refs_6_ = bf16[288,128]{1,0:T(8,128)(2,1)S(1)} collective-permute-done((bf16[288,128]{1,0:T(8,128)(2,1)S(1)}, bf16[288,128]{1,0:T(8,128)(2,1)S(1)}, u32[]{:S(2)}, u32[]{:S(2)}) %collective-permute-start.5) | collective-permute-done | bytes 73760 | tf_op jit(solution)/shard_map/ppermute | solution.py:190
  19.7 0.0 collective-permute-start.6
  19.7 0.0 collective-permute-done.4.refs_5_
  19.7 0.0 copy-start.11
  19.7 0.0 collective-permute-done.2.refs_3_
  19.7 0.0 copy-start.12
  19.7 0.0 collective-permute-done.14.refs_15_
  19.7 0.0 copy-start.13
  19.8 0.0 collective-permute-done.10.refs_11_
  19.8 0.0 copy-start.14
  19.8 1.2 %collective-permute-done.6.refs_7_ = bf16[288,128]{1,0:T(8,128)(2,1)S(1)} collective-permute-done((bf16[288,128]{1,0:T(8,128)(2,1)S(1)}, bf16[288,128]{1,0:T(8,128)(2,1)S(1)}, u32[]{:S(2)}, u32[]{:S(2)}) %collective-permute-start.6) | collective-permute-done | bytes 73760 | tf_op jit(solution)/shard_map/ppermute | solution.py:190
  21.0 0.0 copy-done.1
  21.0 0.0 copy-done.2
  21.0 0.0 copy-done.3
  21.0 0.0 copy-done.4
  21.0 0.0 copy-done.5
  21.0 0.0 copy-done.6
  21.1 0.5 copy-done.15
  21.6 22.9 %score.1 = f32[16,8,256]{2,1,0:T(8,128)} custom-call(s32[1]{0:T(128)} %bitcast.2.me_ref, s32[256]{0:T(256)} %count_ref.1, s32[1,256]{1,0:T(1,128)} %bitcast.8, bf16[288,128]{1,0:T(8,128)(2,1)} %get-tuple-element.8.refs_0_, bf16[288,128]{1,0:T(8,128)(2,1)} %copy-done.5, bf16[288,128]{1,0:T(8,128)(2,1)} %copy-done.4, bf16[288,128]{1,0:T(8,128)(2,1)} %copy-done.12, ...), custom_call_target="tpu_custom_call" | custom-call | tf_op jit(solution)/shard_map/score/pallas_call | solution.py:220
  44.5 12.8 %all_to_all.5.back_ref = f32[16,8,256]{2,1,0:T(8,128)S(1)} all-to-all(f32[16,8,256]{2,1,0:T(8,128)} %score.1), channel_id=1, replica_groups=mesh['groups'=2,'shard'=16] {'shard'}, dimensions={0} | all-to-all | bytes 262144 | tf_op jit(solution)/shard_map/all_to_all | solution.py:237
  57.3 0.0 copy-done
  57.3 0.7 %pick.1 = f32[8,256]{1,0:T(8,128)} custom-call(s32[8,256]{1,0:T(8,128)S(1)} %copy-done, f32[16,8,256]{2,1,0:T(8,128)S(1)} %all_to_all.5.back_ref), custom_call_target="tpu_custom_call" | custom-call | tf_op jit(solution)/shard_map/pick/pallas_call | solution.py:238
  (18 shorter events, 0.0 us)
Async XLA Ops:
  1.9 55.4 %copy-start = (s32[8,256]{1,0:T(8,128)S(1)}, s32[8,256]{1,0:T(8,128)}, u32[]{:S(2)}) copy-start(s32[8,256]{1,0:T(8,128)} %get-tuple-element.7.slot_ref) | copy-start | bytes 24580
  1.9 8.0 %collective-permute-start.11 = (bf16[288,128]{1,0:T(8,128)(2,1)}, bf16[288,128]{1,0:T(8,128)(2,1)S(1)}, u32[]{:S(2)}, u32[]{:S(2)}) collective-permute-start(bf16[288,128]{1,0:T(8,128)(2,1)} %get-tuple-element.8.refs_0_), channel_id=1, source_target_pairs={{0,12},{1,13},{2,14},{3,15},{4,8},{5,9},{6,10},{7,11},{8,4},{9,5},... | collective-permute-start | bytes 221192 | tf_op jit(solution)/shard_map/ppermute | solution.py:190
  7.0 6.4 %collective-permute-start.7 = (bf16[288,128]{1,0:T(8,128)(2,1)}, bf16[288,128]{1,0:T(8,128)(2,1)S(1)}, u32[]{:S(2)}, u32[]{:S(2)}) collective-permute-start(bf16[288,128]{1,0:T(8,128)(2,1)} %get-tuple-element.8.refs_0_), channel_id=1, source_target_pairs={{0,8},{1,9},{2,10},{3,11},{4,12},{5,13},{6,14},{7,15},{8,0},{9,1},... | collective-permute-start | bytes 221192 | tf_op jit(solution)/shard_map/ppermute | solution.py:190
  7.0 6.4 %collective-permute-start.3 = (bf16[288,128]{1,0:T(8,128)(2,1)}, bf16[288,128]{1,0:T(8,128)(2,1)S(1)}, u32[]{:S(2)}, u32[]{:S(2)}) collective-permute-start(bf16[288,128]{1,0:T(8,128)(2,1)} %get-tuple-element.8.refs_0_), channel_id=1, source_target_pairs={{0,4},{1,5},{2,6},{3,7},{4,0},{5,1},{6,2},{7,3},{8,12},{9,13},{10,... | collective-permute-start | bytes 221192 | tf_op jit(solution)/shard_map/ppermute | solution.py:190
  7.5 7.5 %collective-permute-start.1 = (bf16[288,128]{1,0:T(8,128)(2,1)}, bf16[288,128]{1,0:T(8,128)(2,1)S(1)}, u32[]{:S(2)}, u32[]{:S(2)}) collective-permute-start(bf16[288,128]{1,0:T(8,128)(2,1)} %get-tuple-element.8.refs_0_), channel_id=1, source_target_pairs={{0,2},{1,3},{2,0},{3,1},{4,6},{5,7},{6,4},{7,5},{8,10},{9,11},{10,... | collective-permute-start | bytes 221192 | tf_op jit(solution)/shard_map/ppermute | solution.py:190
  9.3 5.9 %collective-permute-start = (bf16[288,128]{1,0:T(8,128)(2,1)}, bf16[288,128]{1,0:T(8,128)(2,1)S(1)}, u32[]{:S(2)}, u32[]{:S(2)}) collective-permute-start(bf16[288,128]{1,0:T(8,128)(2,1)} %get-tuple-element.8.refs_0_), channel_id=1, source_target_pairs={{0,1},{1,0},{2,3},{3,2},{4,5},{5,4},{6,7},{7,6},{8,9},{9,8},{10,11... | collective-permute-start | bytes 221192 | tf_op jit(solution)/shard_map/ppermute | solution.py:190
  10.0 11.0 %copy-start.1 = (bf16[288,128]{1,0:T(8,128)(2,1)}, bf16[288,128]{1,0:T(8,128)(2,1)S(1)}, u32[]{:S(2)}) copy-start(bf16[288,128]{1,0:T(8,128)(2,1)S(1)} %collective-permute-done.11.refs_12_) | copy-start | bytes 221188
  10.0 5.7 %collective-permute-start.13 = (bf16[288,128]{1,0:T(8,128)(2,1)S(1)}, bf16[288,128]{1,0:T(8,128)(2,1)S(1)}, u32[]{:S(2)}, u32[]{:S(2)}) collective-permute-start(bf16[288,128]{1,0:T(8,128)(2,1)S(1)} %collective-permute-done.11.refs_12_), channel_id=1, source_target_pairs={{0,2},{1,3},{2,0},{3,1},{4,6},{5,7},{6,4},{7,5},{8,10},{9,11},{10,... | collective-permute-start | bytes 221192 | tf_op jit(solution)/shard_map/ppermute | solution.py:190
  13.4 7.6 %copy-start.2 = (bf16[288,128]{1,0:T(8,128)(2,1)}, bf16[288,128]{1,0:T(8,128)(2,1)S(1)}, u32[]{:S(2)}) copy-start(bf16[288,128]{1,0:T(8,128)(2,1)S(1)} %collective-permute-done.7.refs_8_) | copy-start | bytes 221188
  13.4 2.4 %collective-permute-start.12 = (bf16[288,128]{1,0:T(8,128)(2,1)S(1)}, bf16[288,128]{1,0:T(8,128)(2,1)S(1)}, u32[]{:S(2)}, u32[]{:S(2)}) collective-permute-start(bf16[288,128]{1,0:T(8,128)(2,1)S(1)} %collective-permute-done.11.refs_12_), channel_id=1, source_target_pairs={{0,1},{1,0},{2,3},{3,2},{4,5},{5,4},{6,7},{7,6},{8,9},{9,8},{10,11... | collective-permute-start | bytes 221192 | tf_op jit(solution)/shard_map/ppermute | solution.py:190
  13.4 7.6 %copy-start.3 = (bf16[288,128]{1,0:T(8,128)(2,1)}, bf16[288,128]{1,0:T(8,128)(2,1)S(1)}, u32[]{:S(2)}) copy-start(bf16[288,128]{1,0:T(8,128)(2,1)S(1)} %collective-permute-done.3.refs_4_) | copy-start | bytes 221188
  13.4 4.7 %collective-permute-start.9 = (bf16[288,128]{1,0:T(8,128)(2,1)S(1)}, bf16[288,128]{1,0:T(8,128)(2,1)S(1)}, u32[]{:S(2)}, u32[]{:S(2)}) collective-permute-start(bf16[288,128]{1,0:T(8,128)(2,1)S(1)} %collective-permute-done.7.refs_8_), channel_id=1, source_target_pairs={{0,2},{1,3},{2,0},{3,1},{4,6},{5,7},{6,4},{7,5},{8,10},{9,11},{10,... | collective-permute-start | bytes 221192 | tf_op jit(solution)/shard_map/ppermute | solution.py:190
  15.0 6.0 %copy-start.4 = (bf16[288,128]{1,0:T(8,128)(2,1)}, bf16[288,128]{1,0:T(8,128)(2,1)S(1)}, u32[]{:S(2)}) copy-start(bf16[288,128]{1,0:T(8,128)(2,1)S(1)} %collective-permute-done.1.refs_2_) | copy-start | bytes 221188
  15.0 3.1 %collective-permute-start.8 = (bf16[288,128]{1,0:T(8,128)(2,1)S(1)}, bf16[288,128]{1,0:T(8,128)(2,1)S(1)}, u32[]{:S(2)}, u32[]{:S(2)}) collective-permute-start(bf16[288,128]{1,0:T(8,128)(2,1)S(1)} %collective-permute-done.7.refs_8_), channel_id=1, source_target_pairs={{0,1},{1,0},{2,3},{3,2},{4,5},{5,4},{6,7},{7,6},{8,9},{9,8},{10,11... | collective-permute-start | bytes 221192 | tf_op jit(solution)/shard_map/ppermute | solution.py:190
  15.2 5.8 %copy-start.5 = (bf16[288,128]{1,0:T(8,128)(2,1)}, bf16[288,128]{1,0:T(8,128)(2,1)S(1)}, u32[]{:S(2)}) copy-start(bf16[288,128]{1,0:T(8,128)(2,1)S(1)} %collective-permute-done.refs_1_) | copy-start | bytes 221188
  15.2 4.5 %collective-permute-start.5 = (bf16[288,128]{1,0:T(8,128)(2,1)S(1)}, bf16[288,128]{1,0:T(8,128)(2,1)S(1)}, u32[]{:S(2)}, u32[]{:S(2)}) collective-permute-start(bf16[288,128]{1,0:T(8,128)(2,1)S(1)} %collective-permute-done.3.refs_4_), channel_id=1, source_target_pairs={{0,2},{1,3},{2,0},{3,1},{4,6},{5,7},{6,4},{7,5},{8,10},{9,11},{10,... | collective-permute-start | bytes 221192 | tf_op jit(solution)/shard_map/ppermute | solution.py:190
  15.7 5.3 %copy-start.6 = (bf16[288,128]{1,0:T(8,128)(2,1)}, bf16[288,128]{1,0:T(8,128)(2,1)S(1)}, u32[]{:S(2)}) copy-start(bf16[288,128]{1,0:T(8,128)(2,1)S(1)} %collective-permute-done.13.refs_14_) | copy-start | bytes 221188
  15.7 4.0 %collective-permute-start.4 = (bf16[288,128]{1,0:T(8,128)(2,1)S(1)}, bf16[288,128]{1,0:T(8,128)(2,1)S(1)}, u32[]{:S(2)}, u32[]{:S(2)}) collective-permute-start(bf16[288,128]{1,0:T(8,128)(2,1)S(1)} %collective-permute-done.3.refs_4_), channel_id=1, source_target_pairs={{0,1},{1,0},{2,3},{3,2},{4,5},{5,4},{6,7},{7,6},{8,9},{9,8},{10,11... | collective-permute-start | bytes 221192 | tf_op jit(solution)/shard_map/ppermute | solution.py:190
  15.8 5.3 %copy-start.7 = (bf16[288,128]{1,0:T(8,128)(2,1)}, bf16[288,128]{1,0:T(8,128)(2,1)S(1)}, u32[]{:S(2)}) copy-start(bf16[288,128]{1,0:T(8,128)(2,1)S(1)} %collective-permute-done.12.refs_13_) | copy-start | bytes 221188
  15.8 4.0 %collective-permute-start.2 = (bf16[288,128]{1,0:T(8,128)(2,1)S(1)}, bf16[288,128]{1,0:T(8,128)(2,1)S(1)}, u32[]{:S(2)}, u32[]{:S(2)}) collective-permute-start(bf16[288,128]{1,0:T(8,128)(2,1)S(1)} %collective-permute-done.1.refs_2_), channel_id=1, source_target_pairs={{0,1},{1,0},{2,3},{3,2},{4,5},{5,4},{6,7},{7,6},{8,9},{9,8},{10,11... | collective-permute-start | bytes 221192 | tf_op jit(solution)/shard_map/ppermute | solution.py:190
  18.1 2.9 %copy-start.8 = (bf16[288,128]{1,0:T(8,128)(2,1)}, bf16[288,128]{1,0:T(8,128)(2,1)S(1)}, u32[]{:S(2)}) copy-start(bf16[288,128]{1,0:T(8,128)(2,1)S(1)} %collective-permute-done.9.refs_10_) | copy-start | bytes 221188
  18.1 1.6 %collective-permute-start.14 = (bf16[288,128]{1,0:T(8,128)(2,1)S(1)}, bf16[288,128]{1,0:T(8,128)(2,1)S(1)}, u32[]{:S(2)}, u32[]{:S(2)}) collective-permute-start(bf16[288,128]{1,0:T(8,128)(2,1)S(1)} %collective-permute-done.13.refs_14_), channel_id=1, source_target_pairs={{0,1},{1,0},{2,3},{3,2},{4,5},{5,4},{6,7},{7,6},{8,9},{9,8},{10,11... | collective-permute-start | bytes 221192 | tf_op jit(solution)/shard_map/ppermute | solution.py:190
  18.1 2.9 %copy-start.9 = (bf16[288,128]{1,0:T(8,128)(2,1)}, bf16[288,128]{1,0:T(8,128)(2,1)S(1)}, u32[]{:S(2)}) copy-start(bf16[288,128]{1,0:T(8,128)(2,1)S(1)} %collective-permute-done.8.refs_9_) | copy-start | bytes 221188
  18.1 1.6 %collective-permute-start.10 = (bf16[288,128]{1,0:T(8,128)(2,1)S(1)}, bf16[288,128]{1,0:T(8,128)(2,1)S(1)}, u32[]{:S(2)}, u32[]{:S(2)}) collective-permute-start(bf16[288,128]{1,0:T(8,128)(2,1)S(1)} %collective-permute-done.9.refs_10_), channel_id=1, source_target_pairs={{0,1},{1,0},{2,3},{3,2},{4,5},{5,4},{6,7},{7,6},{8,9},{9,8},{10,11... | collective-permute-start | bytes 221192 | tf_op jit(solution)/shard_map/ppermute | solution.py:190
  19.7 1.3 %copy-start.10 = (bf16[288,128]{1,0:T(8,128)(2,1)}, bf16[288,128]{1,0:T(8,128)(2,1)S(1)}, u32[]{:S(2)}) copy-start(bf16[288,128]{1,0:T(8,128)(2,1)S(1)} %collective-permute-done.5.refs_6_) | copy-start | bytes 221188
  19.7 1.3 %collective-permute-start.6 = (bf16[288,128]{1,0:T(8,128)(2,1)S(1)}, bf16[288,128]{1,0:T(8,128)(2,1)S(1)}, u32[]{:S(2)}, u32[]{:S(2)}) collective-permute-start(bf16[288,128]{1,0:T(8,128)(2,1)S(1)} %collective-permute-done.5.refs_6_), channel_id=1, source_target_pairs={{0,1},{1,0},{2,3},{3,2},{4,5},{5,4},{6,7},{7,6},{8,9},{9,8},{10,11... | collective-permute-start | bytes 221192 | tf_op jit(solution)/shard_map/ppermute | solution.py:190
  19.7 1.3 %copy-start.11 = (bf16[288,128]{1,0:T(8,128)(2,1)}, bf16[288,128]{1,0:T(8,128)(2,1)S(1)}, u32[]{:S(2)}) copy-start(bf16[288,128]{1,0:T(8,128)(2,1)S(1)} %collective-permute-done.4.refs_5_) | copy-start | bytes 221188
  19.7 1.3 %copy-start.12 = (bf16[288,128]{1,0:T(8,128)(2,1)}, bf16[288,128]{1,0:T(8,128)(2,1)S(1)}, u32[]{:S(2)}) copy-start(bf16[288,128]{1,0:T(8,128)(2,1)S(1)} %collective-permute-done.2.refs_3_) | copy-start | bytes 221188
  19.7 1.3 %copy-start.13 = (bf16[288,128]{1,0:T(8,128)(2,1)}, bf16[288,128]{1,0:T(8,128)(2,1)S(1)}, u32[]{:S(2)}) copy-start(bf16[288,128]{1,0:T(8,128)(2,1)S(1)} %collective-permute-done.14.refs_15_) | copy-start | bytes 221188
  19.8 1.3 %copy-start.14 = (bf16[288,128]{1,0:T(8,128)(2,1)}, bf16[288,128]{1,0:T(8,128)(2,1)S(1)}, u32[]{:S(2)}) copy-start(bf16[288,128]{1,0:T(8,128)(2,1)S(1)} %collective-permute-done.10.refs_11_) | copy-start | bytes 221188
  21.0 0.6 %copy-start.15 = (bf16[288,128]{1,0:T(8,128)(2,1)}, bf16[288,128]{1,0:T(8,128)(2,1)S(1)}, u32[]{:S(2)}) copy-start(bf16[288,128]{1,0:T(8,128)(2,1)S(1)} %collective-permute-done.6.refs_7_) | copy-start | bytes 221188

commit v4 on v3

--- a/solution.py
+++ b/solution.py
@@ -10,6 +10,8 @@
 PMOST = 16
 LEAST = 45
 PITCH = 17
+DEPTH = 48
+WALK = 32
 LANES = 128
 F32 = jnp.float32
 BF16 = jnp.bfloat16
@@ -59,37 +61,39 @@
     load_ref[tokens:, :] = bits.astype(BF16)
 
 
-def turn(len_ref, in_ref, out_ref, wide_ref, first, last):
-    tokens, _, d = in_ref.shape
+def turn(len_ref, in_ref, out_ref, wide_ref, first_ref, start, stop):
+    d = in_ref.shape[2]
 
     def group(g, carry):
         p0 = pl.multiple_of(g * 16, 16)
-        for t in range(tokens):
-            wide_ref[t * PITCH : t * PITCH + 16, :] = in_ref[t, pl.ds(p0, 16), :].astype(F32)
+        for t in range(stop - start):
+            wide_ref[t * PITCH : t * PITCH + 16, :] = in_ref[start + t, pl.ds(p0, 16), :].astype(F32)
+        live = first_ref[pl.ds(p0, 16), :]
         for p in range(16):
-            live = wide_ref[p : p + 1, :]
             length = len_ref[p0 + p]
-            for t in range(0, tokens, 16):
-                rows = wide_ref[pl.ds(p + t * PITCH, 16, stride=PITCH), :]
+            for t in range(start, stop, 16):
+                rows = wide_ref[pl.ds(p + (t - start) * PITCH, 16, stride=PITCH), :]
                 if t + 16 > LEAST:
-                    rows = jnp.where(iota((16, d), 0) < length - t, rows, live)
+                    rows = jnp.where(iota((16, d), 0) < length - t, rows, live[p : p + 1])
                 out_ref[p0 + p, t : t + 16] = rows.astype(BF16)
         return carry
 
-    lax.fori_loop(first // 16, last // 16, group, 0)
+    lax.fori_loop(0, in_ref.shape[1] // 16, group, 0)
 
 
 def score_kernel(n, me_ref, count_ref, len_ref, *refs):
     loads, refs = refs[:n], refs[n:]
-    source_ref, out_ref, in_ref, pas_ref, wide_ref = refs[:5]
-    q_ref, list_vmem, list_smem, best_ref, sems = refs[5:]
+    source_ref, out_ref, in_ref, pas_ref, wide_ref, first_ref = refs[:6]
+    q_ref, list_vmem, list_smem, best_ref, sems = refs[6:]
     held, padded, _ = pas_ref.shape
-    parts = sems.shape[0] - 1
-    step = held // parts
+    depth = wide_ref.shape[0] // PITCH
+    starts = list(range(0, in_ref.shape[0], depth))
+    stops = starts[1:] + [in_ref.shape[0]]
+    parts = len(starts)
 
     def fetch(i):
-        at = pl.ds(i * step, step)
-        return pltpu.make_async_copy(source_ref.at[:, at], in_ref.at[:, at], sems.at[i])
+        at = pl.ds(starts[i], stops[i] - starts[i])
+        return pltpu.make_async_copy(source_ref.at[at], in_ref.at[at], sems.at[i])
 
     for i in range(parts):
         fetch(i).start()
@@ -100,6 +104,7 @@
     qt = tokens // q_dev
     total = n * q_dev
     low, high = (LEAST + 15) // 16, padded // 16
+    levels = list(range(min(8, high), high, 2)) + [high]
     me = me_ref[0]
     size = jnp.clip((len_ref[...] + 15) // 16, low, high)
     level = iota((16, held), 0)
@@ -140,32 +145,38 @@
         q_ref[k * tokens : (k + 1) * tokens, :] = loads[k][:tokens, :]
     for i in range(parts):
         fetch(i).wait()
-        turn(count_ref, in_ref, pas_ref, wide_ref, i * step, (i + 1) * step)
+        if i == 0:
+            first_ref[...] = in_ref[0].astype(F32)
+        turn(count_ref, in_ref, pas_ref, wide_ref, first_ref, starts[i], stops[i])
     copy.wait()
 
     def walk(size, i, carry):
-        for g in (0, 8):
+        for g in range(0, WALK, 8):
             best = []
             for u in range(g, g + 8):
-                at = i * 16 + u
+                at = i * WALK + u
                 block = jnp.concatenate(
                     [q_ref[pl.ds(pl.multiple_of(list_smem[r, at], qt), qt), :] for r in range(PMOST)],
                     axis=0,
                 )
                 part = pas_ref[list_smem[PMOST, at], : size * 16]
                 best.append(jnp.max(dot(part, block, NT), axis=0, keepdims=True))
-            at = pl.multiple_of(i * 16 + g, 8)
+            at = pl.multiple_of(i * WALK + g, 8)
             best_ref[pl.ds(at, 8), :] = jnp.concatenate(best, axis=0)
         return carry
 
     start = 0
-    for s in range(low, high + 1):
-        stop = list_smem[PMOST + 16 + s, 0] // 16
+    for s in levels:
+        stop = list_smem[PMOST + 16 + s, 0] // WALK
         lax.fori_loop(start, stop, functools.partial(walk, s), 0)
         start = stop
     wide = PMOST * qt
     mean = jnp.where(iota((PMOST, wide), 1) // qt == iota((PMOST, wide), 0), 1.0 / qt, 0.0)
-    score = dot(mean, best_ref[...], NT, precision=lax.Precision.HIGHEST)
+    best = best_ref[...]
+    coarse = best.astype(BF16)
+    fine = (best - coarse.astype(F32)).astype(BF16)
+    mean = mean.astype(BF16)
+    score = dot(mean, coarse, NT) + dot(mean, fine, NT)
     score = dot(score, order, NN, precision=lax.Precision.HIGHEST)
     dense = jnp.zeros((total, held), F32)
     for r in range(PMOST):
@@ -208,13 +219,11 @@
         name="route",
     )(queries.reshape(tokens, d), candidates, placement.reshape(rows, LANES))
     blocks = {0: load}
-    for k in range(4, n, 4):
+    for k in range(n - 4, 0, -4):
         blocks[k] = swap(load, k, n)
-    blocks[2] = swap(load, 2, n)
-    blocks[1] = swap(load, 1, n)
-    for k in range(4, n, 4):
+    for k in range(n - 4, -1, -4):
         blocks[k + 2] = swap(blocks[k], 2, n)
-    for k in range(2, n, 2):
+    for k in range(n - 2, -1, -2):
         blocks[k + 1] = swap(blocks[k], 1, n)
     loads = [blocks[k] for k in range(n)]
     dense = pl.pallas_call(
@@ -224,12 +233,13 @@
         scratch_shapes=[
             VMEM((pt, held, d), BF16),
             VMEM((held, padded, d), BF16),
-            VMEM((padded * PITCH, d), F32),
+            VMEM((DEPTH * PITCH, d), F32),
+            VMEM((held, d), F32),
             VMEM((n * tokens, d), BF16),
             VMEM((PMOST + 32, held), I32),
             SMEM((PMOST + 32, held), I32),
             VMEM((held, PMOST * qt), F32),
-            pltpu.SemaphoreType.DMA((5,)),
+            pltpu.SemaphoreType.DMA(((pt + DEPTH - 1) // DEPTH + 1,)),
         ],
         compiler_params=pltpu.CompilerParams(vmem_limit_bytes=56 * MIB),
         name="score",

time: 58.3 us -> 57.1 us (0.979)
  Pallas kernels: 25.5 us -> 24.2 us
    pallas_call x1, Pallas kernels: 22.9 us -> 21.5 us  [shards(): pl.pallas_call(functools.partial(score_kernel, n), out_shape=jax.ShapeDty...]
where the time goes in v4:
time: 57.1 us; the launch traced here: 56.8 us
  Pallas kernels  24.2 us (42%)
  blocking collectives  12.9 us (23%)
  starting transfers between devices  12.5 us (22%)
  waiting for transfers between devices  6.44 us (11%)
    pallas_call x1, Pallas kernels, shards(): pl.pallas_call(functools.partial(score_kernel, n), out_shape=jax.ShapeDty...  21.5 us
    all_to_all x1, blocking collectives, shards(): lax.all_to_all(dense, 'shard', split_axis=0, concat_axis=0, tiled=True)  12.9 us
    ppermute x15, starting transfers between devices, swap(): return lax.ppermute(v, 'shard', [(i, i ^ k) for i in range(n)])  12.5 us
    ppermute x15, waiting for transfers between devices, swap(): return lax.ppermute(v, 'shard', [(i, i ^ k) for i in range(n)])  6.44 us
    pallas_call x1, Pallas kernels, shards(): pl.pallas_call(route_kernel, out_shape=(jax.ShapeDtypeStruct((q_dev, cand...  1.91 us
  transfers between devices with their start and end apart: 15, of which 5 were waited for; matrix products, arithmetic and copies ran while one was open for 0% of the time, Pallas kernels for 0%

profile of v4, /device:TPU:0, one launch (start us, length us, event | category | flops | bytes accessed | tf_op | source)
XLA Modules:
  0.0 56.8 jit_solution(12115077827060626636)
XLA Ops:
  0.0 1.9 %route.1 = (s32[8,256]{1,0:T(8,128)}, bf16[288,128]{1,0:T(8,128)(2,1)}) custom-call(bf16[256,128]{1,0:T(8,128)(2,1)} %bitcast.6, s32[8,256]{1,0:T(8,128)} %cand_ref.1, s32[32,128]{1,0:T(8,128)} %bitcast.7), custom_call_target="tpu_custom_call" | custom-call | tf_op jit(solution)/shard_map/route/pallas_call | solution.py:213
  1.9 5.0 %collective-permute-start.11 = (bf16[288,128]{1,0:T(8,128)(2,1)}, bf16[288,128]{1,0:T(8,128)(2,1)S(1)}, u32[]{:S(2)}, u32[]{:S(2)}) collective-permute-start(bf16[288,128]{1,0:T(8,128)(2,1)} %get-tuple-element.8.refs_0_), channel_id=1, source_target_pairs={{0,12},{1,13},{2,14},{3,15},{4,8},{5,9},{6,10},{7,11},{8,4},{9,5},... | collective-permute-start | bytes 221192 | tf_op jit(solution)/shard_map/ppermute | solution.py:201
  7.0 0.0 collective-permute-start.7
  7.0 0.6 collective-permute-start.3
  7.5 1.7 %collective-permute-start.1 = (bf16[288,128]{1,0:T(8,128)(2,1)}, bf16[288,128]{1,0:T(8,128)(2,1)S(1)}, u32[]{:S(2)}, u32[]{:S(2)}) collective-permute-start(bf16[288,128]{1,0:T(8,128)(2,1)} %get-tuple-element.8.refs_0_), channel_id=1, source_target_pairs={{0,2},{1,3},{2,0},{3,1},{4,6},{5,7},{6,4},{7,5},{8,10},{9,11},{10,... | collective-permute-start | bytes 221192 | tf_op jit(solution)/shard_map/ppermute | solution.py:201
  9.3 0.0 collective-permute-start
  9.3 0.7 %collective-permute-done.11.refs_12_ = bf16[288,128]{1,0:T(8,128)(2,1)S(1)} collective-permute-done((bf16[288,128]{1,0:T(8,128)(2,1)}, bf16[288,128]{1,0:T(8,128)(2,1)S(1)}, u32[]{:S(2)}, u32[]{:S(2)}) %collective-permute-start.11) | collective-permute-done | bytes 73760 | tf_op jit(solution)/shard_map/ppermute | solution.py:201
  10.0 1.9 %collective-permute-start.13 = (bf16[288,128]{1,0:T(8,128)(2,1)S(1)}, bf16[288,128]{1,0:T(8,128)(2,1)S(1)}, u32[]{:S(2)}, u32[]{:S(2)}) collective-permute-start(bf16[288,128]{1,0:T(8,128)(2,1)S(1)} %collective-permute-done.11.refs_12_), channel_id=1, source_target_pairs={{0,2},{1,3},{2,0},{3,1},{4,6},{5,7},{6,4},{7,5},{8,10},{9,11},{10,... | collective-permute-start | bytes 221192 | tf_op jit(solution)/shard_map/ppermute | solution.py:201
  11.8 1.6 %collective-permute-done.7.refs_8_ = bf16[288,128]{1,0:T(8,128)(2,1)S(1)} collective-permute-done((bf16[288,128]{1,0:T(8,128)(2,1)}, bf16[288,128]{1,0:T(8,128)(2,1)S(1)}, u32[]{:S(2)}, u32[]{:S(2)}) %collective-permute-start.7) | collective-permute-done | bytes 73760 | tf_op jit(solution)/shard_map/ppermute | solution.py:201
  13.4 0.0 collective-permute-start.12
  13.4 0.0 collective-permute-done.3.refs_4_
  13.4 0.0 copy-start.3
  13.4 1.6 %collective-permute-start.9 = (bf16[288,128]{1,0:T(8,128)(2,1)S(1)}, bf16[288,128]{1,0:T(8,128)(2,1)S(1)}, u32[]{:S(2)}, u32[]{:S(2)}) collective-permute-start(bf16[288,128]{1,0:T(8,128)(2,1)S(1)} %collective-permute-done.7.refs_8_), channel_id=1, source_target_pairs={{0,2},{1,3},{2,0},{3,1},{4,6},{5,7},{6,4},{7,5},{8,10},{9,11},{10,... | collective-permute-start | bytes 221192 | tf_op jit(solution)/shard_map/ppermute | solution.py:201
  15.0 0.0 collective-permute-done.1.refs_2_
  15.0 0.2 collective-permute-start.8
  15.2 0.0 collective-permute-done.refs_1_
  15.2 0.5 collective-permute-start.5
  15.7 0.0 collective-permute-done.13.refs_14_
  15.7 0.1 collective-permute-start.4
  15.7 0.0 collective-permute-done.12.refs_13_
  15.8 0.4 collective-permute-start.2
  16.2 1.9 %collective-permute-done.9.refs_10_ = bf16[288,128]{1,0:T(8,128)(2,1)S(1)} collective-permute-done((bf16[288,128]{1,0:T(8,128)(2,1)S(1)}, bf16[288,128]{1,0:T(8,128)(2,1)S(1)}, u32[]{:S(2)}, u32[]{:S(2)}) %collective-permute-start.9) | collective-permute-done | bytes 73760 | tf_op jit(solution)/shard_map/ppermute | solution.py:201
  18.1 0.0 collective-permute-start.14
  18.1 0.0 collective-permute-done.8.refs_9_
  18.1 0.0 copy-start.9
  18.1 0.5 collective-permute-start.10
  18.6 1.1 %collective-permute-done.5.refs_6_ = bf16[288,128]{1,0:T(8,128)(2,1)S(1)} collective-permute-done((bf16[288,128]{1,0:T(8,128)(2,1)S(1)}, bf16[288,128]{1,0:T(8,128)(2,1)S(1)}, u32[]{:S(2)}, u32[]{:S(2)}) %collective-permute-start.5) | collective-permute-done | bytes 73760 | tf_op jit(solution)/shard_map/ppermute | solution.py:201
  19.7 0.0 collective-permute-start.6
  19.7 0.0 collective-permute-done.4.refs_5_
  19.7 0.0 copy-start.11
  19.7 0.0 collective-permute-done.2.refs_3_
  19.7 0.0 copy-start.12
  19.7 0.0 collective-permute-done.14.refs_15_
  19.7 0.0 copy-start.13
  19.8 0.0 collective-permute-done.10.refs_11_
  19.8 0.0 copy-start.14
  19.8 1.2 %collective-permute-done.6.refs_7_ = bf16[288,128]{1,0:T(8,128)(2,1)S(1)} collective-permute-done((bf16[288,128]{1,0:T(8,128)(2,1)S(1)}, bf16[288,128]{1,0:T(8,128)(2,1)S(1)}, u32[]{:S(2)}, u32[]{:S(2)}) %collective-permute-start.6) | collective-permute-done | bytes 73760 | tf_op jit(solution)/shard_map/ppermute | solution.py:201
  21.0 0.0 copy-done.1
  21.0 0.0 copy-done.2
  21.0 0.0 copy-done.3
  21.0 0.0 copy-done.4
  21.0 0.0 copy-done.5
  21.0 0.0 copy-done.6
  21.0 0.0 copy-done.7
  21.1 0.5 copy-done.15
  21.6 21.5 %score.1 = f32[16,8,256]{2,1,0:T(8,128)} custom-call(s32[1]{0:T(128)} %bitcast.2.me_ref, s32[256]{0:T(256)} %count_ref.1, s32[1,256]{1,0:T(1,128)} %bitcast.8, bf16[288,128]{1,0:T(8,128)(2,1)} %get-tuple-element.8.refs_0_, bf16[288,128]{1,0:T(8,128)(2,1)} %copy-done.5, bf16[288,128]{1,0:T(8,128)(2,1)} %copy-done.4, bf16[288,128]{1,0:T(8,128)(2,1)} %copy-done.12, ...), custom_call_target="tpu_custom_call" | custom-call | tf_op jit(solution)/shard_map/score/pallas_call | solution.py:229
  43.1 12.9 %all_to_all.5.back_ref = f32[16,8,256]{2,1,0:T(8,128)S(1)} all-to-all(f32[16,8,256]{2,1,0:T(8,128)} %score.1), channel_id=1, replica_groups=mesh['groups'=2,'shard'=16] {'shard'}, dimensions={0} | all-to-all | bytes 262144 | tf_op jit(solution)/shard_map/all_to_all | solution.py:247
  56.0 0.7 %pick.1 = f32[8,256]{1,0:T(8,128)} custom-call(s32[8,256]{1,0:T(8,128)S(1)} %copy-done, f32[16,8,256]{2,1,0:T(8,128)S(1)} %all_to_all.5.back_ref), custom_call_target="tpu_custom_call" | custom-call | tf_op jit(solution)/shard_map/pick/pallas_call | solution.py:248
  (18 shorter events, 0.0 us)
Async XLA Ops:
  1.9 54.1 %copy-start = (s32[8,256]{1,0:T(8,128)S(1)}, s32[8,256]{1,0:T(8,128)}, u32[]{:S(2)}) copy-start(s32[8,256]{1,0:T(8,128)} %get-tuple-element.7.slot_ref) | copy-start | bytes 24580
  1.9 8.0 %collective-permute-start.11 = (bf16[288,128]{1,0:T(8,128)(2,1)}, bf16[288,128]{1,0:T(8,128)(2,1)S(1)}, u32[]{:S(2)}, u32[]{:S(2)}) collective-permute-start(bf16[288,128]{1,0:T(8,128)(2,1)} %get-tuple-element.8.refs_0_), channel_id=1, source_target_pairs={{0,12},{1,13},{2,14},{3,15},{4,8},{5,9},{6,10},{7,11},{8,4},{9,5},... | collective-permute-start | bytes 221192 | tf_op jit(solution)/shard_map/ppermute | solution.py:201
  7.0 6.4 %collective-permute-start.7 = (bf16[288,128]{1,0:T(8,128)(2,1)}, bf16[288,128]{1,0:T(8,128)(2,1)S(1)}, u32[]{:S(2)}, u32[]{:S(2)}) collective-permute-start(bf16[288,128]{1,0:T(8,128)(2,1)} %get-tuple-element.8.refs_0_), channel_id=1, source_target_pairs={{0,8},{1,9},{2,10},{3,11},{4,12},{5,13},{6,14},{7,15},{8,0},{9,1},... | collective-permute-start | bytes 221192 | tf_op jit(solution)/shard_map/ppermute | solution.py:201
  7.0 6.4 %collective-permute-start.3 = (bf16[288,128]{1,0:T(8,128)(2,1)}, bf16[288,128]{1,0:T(8,128)(2,1)S(1)}, u32[]{:S(2)}, u32[]{:S(2)}) collective-permute-start(bf16[288,128]{1,0:T(8,128)(2,1)} %get-tuple-element.8.refs_0_), channel_id=1, source_target_pairs={{0,4},{1,5},{2,6},{3,7},{4,0},{5,1},{6,2},{7,3},{8,12},{9,13},{10,... | collective-permute-start | bytes 221192 | tf_op jit(solution)/shard_map/ppermute | solution.py:201
  7.5 7.5 %collective-permute-start.1 = (bf16[288,128]{1,0:T(8,128)(2,1)}, bf16[288,128]{1,0:T(8,128)(2,1)S(1)}, u32[]{:S(2)}, u32[]{:S(2)}) collective-permute-start(bf16[288,128]{1,0:T(8,128)(2,1)} %get-tuple-element.8.refs_0_), channel_id=1, source_target_pairs={{0,2},{1,3},{2,0},{3,1},{4,6},{5,7},{6,4},{7,5},{8,10},{9,11},{10,... | collective-permute-start | bytes 221192 | tf_op jit(solution)/shard_map/ppermute | solution.py:201
  9.3 5.9 %collective-permute-start = (bf16[288,128]{1,0:T(8,128)(2,1)}, bf16[288,128]{1,0:T(8,128)(2,1)S(1)}, u32[]{:S(2)}, u32[]{:S(2)}) collective-permute-start(bf16[288,128]{1,0:T(8,128)(2,1)} %get-tuple-element.8.refs_0_), channel_id=1, source_target_pairs={{0,1},{1,0},{2,3},{3,2},{4,5},{5,4},{6,7},{7,6},{8,9},{9,8},{10,11... | collective-permute-start | bytes 221192 | tf_op jit(solution)/shard_map/ppermute | solution.py:201
  10.0 11.0 %copy-start.1 = (bf16[288,128]{1,0:T(8,128)(2,1)}, bf16[288,128]{1,0:T(8,128)(2,1)S(1)}, u32[]{:S(2)}) copy-start(bf16[288,128]{1,0:T(8,128)(2,1)S(1)} %collective-permute-done.11.refs_12_) | copy-start | bytes 221188
  10.0 5.7 %collective-permute-start.13 = (bf16[288,128]{1,0:T(8,128)(2,1)S(1)}, bf16[288,128]{1,0:T(8,128)(2,1)S(1)}, u32[]{:S(2)}, u32[]{:S(2)}) collective-permute-start(bf16[288,128]{1,0:T(8,128)(2,1)S(1)} %collective-permute-done.11.refs_12_), channel_id=1, source_target_pairs={{0,2},{1,3},{2,0},{3,1},{4,6},{5,7},{6,4},{7,5},{8,10},{9,11},{10,... | collective-permute-start | bytes 221192 | tf_op jit(solution)/shard_map/ppermute | solution.py:201
  13.4 7.6 %copy-start.2 = (bf16[288,128]{1,0:T(8,128)(2,1)}, bf16[288,128]{1,0:T(8,128)(2,1)S(1)}, u32[]{:S(2)}) copy-start(bf16[288,128]{1,0:T(8,128)(2,1)S(1)} %collective-permute-done.7.refs_8_) | copy-start | bytes 221188
  13.4 2.4 %collective-permute-start.12 = (bf16[288,128]{1,0:T(8,128)(2,1)S(1)}, bf16[288,128]{1,0:T(8,128)(2,1)S(1)}, u32[]{:S(2)}, u32[]{:S(2)}) collective-permute-start(bf16[288,128]{1,0:T(8,128)(2,1)S(1)} %collective-permute-done.11.refs_12_), channel_id=1, source_target_pairs={{0,1},{1,0},{2,3},{3,2},{4,5},{5,4},{6,7},{7,6},{8,9},{9,8},{10,11... | collective-permute-start | bytes 221192 | tf_op jit(solution)/shard_map/ppermute | solution.py:201
  13.4 7.6 %copy-start.3 = (bf16[288,128]{1,0:T(8,128)(2,1)}, bf16[288,128]{1,0:T(8,128)(2,1)S(1)}, u32[]{:S(2)}) copy-start(bf16[288,128]{1,0:T(8,128)(2,1)S(1)} %collective-permute-done.3.refs_4_) | copy-start | bytes 221188
  13.4 4.7 %collective-permute-start.9 = (bf16[288,128]{1,0:T(8,128)(2,1)S(1)}, bf16[288,128]{1,0:T(8,128)(2,1)S(1)}, u32[]{:S(2)}, u32[]{:S(2)}) collective-permute-start(bf16[288,128]{1,0:T(8,128)(2,1)S(1)} %collective-permute-done.7.refs_8_), channel_id=1, source_target_pairs={{0,2},{1,3},{2,0},{3,1},{4,6},{5,7},{6,4},{7,5},{8,10},{9,11},{10,... | collective-permute-start | bytes 221192 | tf_op jit(solution)/shard_map/ppermute | solution.py:201
  15.0 6.0 %copy-start.4 = (bf16[288,128]{1,0:T(8,128)(2,1)}, bf16[288,128]{1,0:T(8,128)(2,1)S(1)}, u32[]{:S(2)}) copy-start(bf16[288,128]{1,0:T(8,128)(2,1)S(1)} %collective-permute-done.1.refs_2_) | copy-start | bytes 221188
  15.0 3.1 %collective-permute-start.8 = (bf16[288,128]{1,0:T(8,128)(2,1)S(1)}, bf16[288,128]{1,0:T(8,128)(2,1)S(1)}, u32[]{:S(2)}, u32[]{:S(2)}) collective-permute-start(bf16[288,128]{1,0:T(8,128)(2,1)S(1)} %collective-permute-done.7.refs_8_), channel_id=1, source_target_pairs={{0,1},{1,0},{2,3},{3,2},{4,5},{5,4},{6,7},{7,6},{8,9},{9,8},{10,11... | collective-permute-start | bytes 221192 | tf_op jit(solution)/shard_map/ppermute | solution.py:201
  15.2 5.8 %copy-start.5 = (bf16[288,128]{1,0:T(8,128)(2,1)}, bf16[288,128]{1,0:T(8,128)(2,1)S(1)}, u32[]{:S(2)}) copy-start(bf16[288,128]{1,0:T(8,128)(2,1)S(1)} %collective-permute-done.refs_1_) | copy-start | bytes 221188
  15.2 4.5 %collective-permute-start.5 = (bf16[288,128]{1,0:T(8,128)(2,1)S(1)}, bf16[288,128]{1,0:T(8,128)(2,1)S(1)}, u32[]{:S(2)}, u32[]{:S(2)}) collective-permute-start(bf16[288,128]{1,0:T(8,128)(2,1)S(1)} %collective-permute-done.3.refs_4_), channel_id=1, source_target_pairs={{0,2},{1,3},{2,0},{3,1},{4,6},{5,7},{6,4},{7,5},{8,10},{9,11},{10,... | collective-permute-start | bytes 221192 | tf_op jit(solution)/shard_map/ppermute | solution.py:201
  15.7 5.3 %copy-start.6 = (bf16[288,128]{1,0:T(8,128)(2,1)}, bf16[288,128]{1,0:T(8,128)(2,1)S(1)}, u32[]{:S(2)}) copy-start(bf16[288,128]{1,0:T(8,128)(2,1)S(1)} %collective-permute-done.13.refs_14_) | copy-start | bytes 221188
  15.7 4.0 %collective-permute-start.4 = (bf16[288,128]{1,0:T(8,128)(2,1)S(1)}, bf16[288,128]{1,0:T(8,128)(2,1)S(1)}, u32[]{:S(2)}, u32[]{:S(2)}) collective-permute-start(bf16[288,128]{1,0:T(8,128)(2,1)S(1)} %collective-permute-done.3.refs_4_), channel_id=1, source_target_pairs={{0,1},{1,0},{2,3},{3,2},{4,5},{5,4},{6,7},{7,6},{8,9},{9,8},{10,11... | collective-permute-start | bytes 221192 | tf_op jit(solution)/shard_map/ppermute | solution.py:201
  15.8 5.3 %copy-start.7 = (bf16[288,128]{1,0:T(8,128)(2,1)}, bf16[288,128]{1,0:T(8,128)(2,1)S(1)}, u32[]{:S(2)}) copy-start(bf16[288,128]{1,0:T(8,128)(2,1)S(1)} %collective-permute-done.12.refs_13_) | copy-start | bytes 221188
  15.8 4.0 %collective-permute-start.2 = (bf16[288,128]{1,0:T(8,128)(2,1)S(1)}, bf16[288,128]{1,0:T(8,128)(2,1)S(1)}, u32[]{:S(2)}, u32[]{:S(2)}) collective-permute-start(bf16[288,128]{1,0:T(8,128)(2,1)S(1)} %collective-permute-done.1.refs_2_), channel_id=1, source_target_pairs={{0,1},{1,0},{2,3},{3,2},{4,5},{5,4},{6,7},{7,6},{8,9},{9,8},{10,11... | collective-permute-start | bytes 221192 | tf_op jit(solution)/shard_map/ppermute | solution.py:201
  18.1 2.9 %copy-start.8 = (bf16[288,128]{1,0:T(8,128)(2,1)}, bf16[288,128]{1,0:T(8,128)(2,1)S(1)}, u32[]{:S(2)}) copy-start(bf16[288,128]{1,0:T(8,128)(2,1)S(1)} %collective-permute-done.9.refs_10_) | copy-start | bytes 221188
  18.1 1.6 %collective-permute-start.14 = (bf16[288,128]{1,0:T(8,128)(2,1)S(1)}, bf16[288,128]{1,0:T(8,128)(2,1)S(1)}, u32[]{:S(2)}, u32[]{:S(2)}) collective-permute-start(bf16[288,128]{1,0:T(8,128)(2,1)S(1)} %collective-permute-done.13.refs_14_), channel_id=1, source_target_pairs={{0,1},{1,0},{2,3},{3,2},{4,5},{5,4},{6,7},{7,6},{8,9},{9,8},{10,11... | collective-permute-start | bytes 221192 | tf_op jit(solution)/shard_map/ppermute | solution.py:201
  18.1 2.9 %copy-start.9 = (bf16[288,128]{1,0:T(8,128)(2,1)}, bf16[288,128]{1,0:T(8,128)(2,1)S(1)}, u32[]{:S(2)}) copy-start(bf16[288,128]{1,0:T(8,128)(2,1)S(1)} %collective-permute-done.8.refs_9_) | copy-start | bytes 221188
  18.1 1.6 %collective-permute-start.10 = (bf16[288,128]{1,0:T(8,128)(2,1)S(1)}, bf16[288,128]{1,0:T(8,128)(2,1)S(1)}, u32[]{:S(2)}, u32[]{:S(2)}) collective-permute-start(bf16[288,128]{1,0:T(8,128)(2,1)S(1)} %collective-permute-done.9.refs_10_), channel_id=1, source_target_pairs={{0,1},{1,0},{2,3},{3,2},{4,5},{5,4},{6,7},{7,6},{8,9},{9,8},{10,11... | collective-permute-start | bytes 221192 | tf_op jit(solution)/shard_map/ppermute | solution.py:201
  19.7 1.3 %copy-start.10 = (bf16[288,128]{1,0:T(8,128)(2,1)}, bf16[288,128]{1,0:T(8,128)(2,1)S(1)}, u32[]{:S(2)}) copy-start(bf16[288,128]{1,0:T(8,128)(2,1)S(1)} %collective-permute-done.5.refs_6_) | copy-start | bytes 221188
  19.7 1.3 %collective-permute-start.6 = (bf16[288,128]{1,0:T(8,128)(2,1)S(1)}, bf16[288,128]{1,0:T(8,128)(2,1)S(1)}, u32[]{:S(2)}, u32[]{:S(2)}) collective-permute-start(bf16[288,128]{1,0:T(8,128)(2,1)S(1)} %collective-permute-done.5.refs_6_), channel_id=1, source_target_pairs={{0,1},{1,0},{2,3},{3,2},{4,5},{5,4},{6,7},{7,6},{8,9},{9,8},{10,11... | collective-permute-start | bytes 221192 | tf_op jit(solution)/shard_map/ppermute | solution.py:201
  19.7 1.3 %copy-start.11 = (bf16[288,128]{1,0:T(8,128)(2,1)}, bf16[288,128]{1,0:T(8,128)(2,1)S(1)}, u32[]{:S(2)}) copy-start(bf16[288,128]{1,0:T(8,128)(2,1)S(1)} %collective-permute-done.4.refs_5_) | copy-start | bytes 221188
  19.7 1.3 %copy-start.12 = (bf16[288,128]{1,0:T(8,128)(2,1)}, bf16[288,128]{1,0:T(8,128)(2,1)S(1)}, u32[]{:S(2)}) copy-start(bf16[288,128]{1,0:T(8,128)(2,1)S(1)} %collective-permute-done.2.refs_3_) | copy-start | bytes 221188
  19.7 1.3 %copy-start.13 = (bf16[288,128]{1,0:T(8,128)(2,1)}, bf16[288,128]{1,0:T(8,128)(2,1)S(1)}, u32[]{:S(2)}) copy-start(bf16[288,128]{1,0:T(8,128)(2,1)S(1)} %collective-permute-done.14.refs_15_) | copy-start | bytes 221188
  19.8 1.3 %copy-start.14 = (bf16[288,128]{1,0:T(8,128)(2,1)}, bf16[288,128]{1,0:T(8,128)(2,1)S(1)}, u32[]{:S(2)}) copy-start(bf16[288,128]{1,0:T(8,128)(2,1)S(1)} %collective-permute-done.10.refs_11_) | copy-start | bytes 221188
  21.0 0.6 %copy-start.15 = (bf16[288,128]{1,0:T(8,128)(2,1)}, bf16[288,128]{1,0:T(8,128)(2,1)S(1)}, u32[]{:S(2)}) copy-start(bf16[288,128]{1,0:T(8,128)(2,1)S(1)} %collective-permute-done.6.refs_7_) | copy-start | bytes 221188

commit v5 on v4

--- a/solution.py
+++ b/solution.py
@@ -81,10 +81,10 @@
     lax.fori_loop(0, in_ref.shape[1] // 16, group, 0)
 
 
-def score_kernel(n, me_ref, count_ref, len_ref, *refs):
-    loads, refs = refs[:n], refs[n:]
+def score_kernel(n, me_ref, count_hbm, len_hbm, own_ref, *refs):
+    loads, refs = (None,) + refs[: n - 1], refs[n - 1 :]
     source_ref, out_ref, in_ref, pas_ref, wide_ref, first_ref = refs[:6]
-    q_ref, list_vmem, list_smem, best_ref, sems = refs[6:]
+    q_ref, list_vmem, list_smem, best_ref, count_ref, len_ref, bits_ref, sems = refs[6:]
     held, padded, _ = pas_ref.shape
     depth = wide_ref.shape[0] // PITCH
     starts = list(range(0, in_ref.shape[0], depth))
@@ -95,10 +95,26 @@
         at = pl.ds(starts[i], stops[i] - starts[i])
         return pltpu.make_async_copy(source_ref.at[at], in_ref.at[at], sems.at[i])
 
+    small = [
+        pltpu.make_async_copy(source, target, sems.at[parts + 1 + i])
+        for i, (source, target) in enumerate(
+            (
+                (own_ref.at[pl.ds(own_ref.shape[0] - bits_ref.shape[0], bits_ref.shape[0])], bits_ref),
+                (len_hbm, len_ref),
+                (count_hbm, count_ref),
+                (
+                    own_ref.at[pl.ds(0, own_ref.shape[0] - bits_ref.shape[0])],
+                    q_ref.at[pl.ds(0, own_ref.shape[0] - bits_ref.shape[0])],
+                ),
+            )
+        )
+    ]
+    for copy in small:
+        copy.start()
     for i in range(parts):
         fetch(i).start()
     rows = n * held // LANES
-    tokens = loads[0].shape[0] - rows
+    tokens = own_ref.shape[0] - rows
     per = held // LANES
     q_dev = out_ref.shape[1]
     qt = tokens // q_dev
@@ -106,6 +122,23 @@
     low, high = (LEAST + 15) // 16, padded // 16
     levels = list(range(min(8, high), high, 2)) + [high]
     me = me_ref[0]
+    for k in range(1, n):
+        q_ref[k * tokens : (k + 1) * tokens, :] = loads[k][:tokens, :]
+    small[0].wait()
+    bits = jnp.concatenate([bits_ref[...]] + [loads[k][tokens:, :] for k in range(1, n)], axis=0)
+    halves = []
+    for h in range(per):
+        pick = iota((n, n * rows), 1) == iota((n, n * rows), 0) * rows + me * per + h
+        halves.append(dot(jnp.where(pick, 1.0, 0.0).astype(BF16), bits, NN))
+    masks = jnp.concatenate(halves, axis=1).astype(I32)
+    named = [
+        (jnp.broadcast_to(masks[k : k + 1], (q_dev, held)) >> iota((q_dev, held), 0)) & 1
+        for k in range(n)
+    ]
+    named = jnp.concatenate(named, axis=0).astype(F32)
+    below = jnp.where(iota((total, total), 0) > iota((total, total), 1), 1.0, 0.0).astype(BF16)
+    rank = jnp.where(named > 0.5, dot(below, named.astype(BF16), NN) + 1.0, 0.0)
+    small[1].wait()
     size = jnp.clip((len_ref[...] + 15) // 16, low, high)
     level = iota((16, held), 0)
     member = size == level
@@ -116,20 +149,6 @@
     place = jnp.sum(jnp.where(member, less + within, 0.0), axis=0, keepdims=True)
     order = jnp.where(iota((held, held), 0) == place.astype(I32), 1.0, 0.0)
     order16 = order.astype(BF16)
-
-    bits = jnp.concatenate([loads[k][tokens:, :] for k in range(n)], axis=0)
-    halves = []
-    for h in range(per):
-        pick = iota((n, n * rows), 1) == iota((n, n * rows), 0) * rows + me * per + h
-        halves.append(dot(jnp.where(pick, 1.0, 0.0).astype(BF16), bits, NN))
-    masks = jnp.concatenate(halves, axis=1).astype(I32)
-    named = [
-        (jnp.broadcast_to(masks[k : k + 1], (q_dev, held)) >> iota((q_dev, held), 0)) & 1
-        for k in range(n)
-    ]
-    named = jnp.concatenate(named, axis=0).astype(F32)
-    below = jnp.where(iota((total, total), 0) > iota((total, total), 1), 1.0, 0.0).astype(BF16)
-    rank = jnp.where(named > 0.5, dot(below, named.astype(BF16), NN) + 1.0, 0.0)
     ranked = dot(rank.astype(BF16), order16, NT)
     ids = iota((total, held), 0).astype(F32)
     lines = [
@@ -141,14 +160,14 @@
     list_vmem[PMOST + 16 :, :] = jnp.broadcast_to(upto, (16, held)).astype(I32)
     copy = pltpu.make_async_copy(list_vmem, list_smem, sems.at[parts])
     copy.start()
-    for k in range(n):
-        q_ref[k * tokens : (k + 1) * tokens, :] = loads[k][:tokens, :]
+    small[2].wait()
     for i in range(parts):
         fetch(i).wait()
         if i == 0:
             first_ref[...] = in_ref[0].astype(F32)
         turn(count_ref, in_ref, pas_ref, wide_ref, first_ref, starts[i], stops[i])
     copy.wait()
+    small[3].wait()
 
     def walk(size, i, carry):
         for g in range(0, WALK, 8):
@@ -195,6 +214,10 @@
 
 def spec(space):
     return pl.BlockSpec(memory_space=space)
+
+
+def in_hbm(x):
+    return pltpu.with_memory_space_constraint(x, pltpu.HBM)
 
 
 def swap(v, k, n):
@@ -229,7 +252,7 @@
     dense = pl.pallas_call(
         functools.partial(score_kernel, n),
         out_shape=jax.ShapeDtypeStruct((n, q_dev, held), F32),
-        in_specs=[spec(SMEM), spec(SMEM), spec(VMEM)] + [spec(VMEM)] * n + [spec(pltpu.HBM)],
+        in_specs=[spec(SMEM)] + [spec(pltpu.HBM)] * 3 + [spec(VMEM)] * (n - 1) + [spec(pltpu.HBM)],
         scratch_shapes=[
             VMEM((pt, held, d), BF16),
             VMEM((held, padded, d), BF16),
@@ -239,11 +262,21 @@
             VMEM((PMOST + 32, held), I32),
             SMEM((PMOST + 32, held), I32),
             VMEM((held, PMOST * qt), F32),
-            pltpu.SemaphoreType.DMA(((pt + DEPTH - 1) // DEPTH + 1,)),
+            SMEM((held,), I32),
+            VMEM((1, held), I32),
+            VMEM((rows, d), BF16),
+            pltpu.SemaphoreType.DMA(((pt + DEPTH - 1) // DEPTH + 5,)),
         ],
-        compiler_params=pltpu.CompilerParams(vmem_limit_bytes=56 * MIB),
+        compiler_params=pltpu.CompilerParams(vmem_limit_bytes=30 * MIB),
         name="score",
-    )(me, lengths, lengths.reshape(1, held), *loads, pltpu.with_memory_space_constraint(passages.transpose(1, 0, 2), pltpu.HBM))
+    )(
+        me,
+        in_hbm(lengths),
+        in_hbm(lengths.reshape(1, held)),
+        in_hbm(load),
+        *loads[1:],
+        in_hbm(passages.transpose(1, 0, 2)),
+    )
     back = lax.all_to_all(dense, "shard", split_axis=0, concat_axis=0, tiled=True)
     return pl.pallas_call(
         pick_kernel,

time: 57.1 us -> 54.1 us (0.947)
  Pallas kernels: 24.2 us -> 21.8 us
    pallas_call x1, Pallas kernels: 21.5 us -> 19.1 us  [shards(): pl.pallas_call(functools.partial(score_kernel, n), out_shape=jax.ShapeDty...]
where the time goes in v5:
time: 54.1 us; the launch traced here: 53.8 us
  Pallas kernels  21.8 us (40%)
  blocking collectives  13 us (24%)
  starting transfers between devices  12.5 us (23%)
  waiting for transfers between devices  6.48 us (12%)
    pallas_call x1, Pallas kernels, shards(): pl.pallas_call(functools.partial(score_kernel, n), out_shape=jax.ShapeDty...  19.1 us
    all_to_all x1, blocking collectives, shards(): lax.all_to_all(dense, 'shard', split_axis=0, concat_axis=0, tiled=True)  13 us
    ppermute x15, starting transfers between devices, swap(): return lax.ppermute(v, 'shard', [(i, i ^ k) for i in range(n)])  12.5 us
    ppermute x15, waiting for transfers between devices, swap(): return lax.ppermute(v, 'shard', [(i, i ^ k) for i in range(n)])  6.48 us
    pallas_call x1, Pallas kernels, shards(): pl.pallas_call(route_kernel, out_shape=(jax.ShapeDtypeStruct((q_dev, cand...  1.93 us
  transfers between devices with their start and end apart: 15, of which 5 were waited for; matrix products, arithmetic and copies ran while one was open for 0% of the time, Pallas kernels for 0%

profile of v5, /device:TPU:0, one launch (start us, length us, event | category | flops | bytes accessed | tf_op | source)
XLA Modules:
  0.0 53.8 jit_solution(8816259104858568453)
XLA Ops:
  0.0 1.9 %route.1 = (s32[8,256]{1,0:T(8,128)}, bf16[288,128]{1,0:T(8,128)(2,1)}) custom-call(bf16[256,128]{1,0:T(8,128)(2,1)} %bitcast.6, s32[8,256]{1,0:T(8,128)} %cand_ref.1, s32[32,128]{1,0:T(8,128)} %bitcast.7), custom_call_target="tpu_custom_call" | custom-call | tf_op jit(solution)/shard_map/route/pallas_call | solution.py:236
  1.9 0.0 copy-start
  1.9 5.0 %collective-permute-start.11 = (bf16[288,128]{1,0:T(8,128)(2,1)}, bf16[288,128]{1,0:T(8,128)(2,1)S(1)}, u32[]{:S(2)}, u32[]{:S(2)}) collective-permute-start(bf16[288,128]{1,0:T(8,128)(2,1)} %get-tuple-element.8.own_ref), channel_id=1, source_target_pairs={{0,12},{1,13},{2,14},{3,15},{4,8},{5,9},{6,10},{7,11},{8,4},{9,5},... | collective-permute-start | bytes 221192 | tf_op jit(solution)/shard_map/ppermute | solution.py:224
  7.0 0.0 collective-permute-start.7
  7.0 0.6 %collective-permute-start.3 = (bf16[288,128]{1,0:T(8,128)(2,1)}, bf16[288,128]{1,0:T(8,128)(2,1)S(1)}, u32[]{:S(2)}, u32[]{:S(2)}) collective-permute-start(bf16[288,128]{1,0:T(8,128)(2,1)} %get-tuple-element.8.own_ref), channel_id=1, source_target_pairs={{0,4},{1,5},{2,6},{3,7},{4,0},{5,1},{6,2},{7,3},{8,12},{9,13},{10,... | collective-permute-start | bytes 221192 | tf_op jit(solution)/shard_map/ppermute | solution.py:224
  7.5 1.7 %collective-permute-start.1 = (bf16[288,128]{1,0:T(8,128)(2,1)}, bf16[288,128]{1,0:T(8,128)(2,1)S(1)}, u32[]{:S(2)}, u32[]{:S(2)}) collective-permute-start(bf16[288,128]{1,0:T(8,128)(2,1)} %get-tuple-element.8.own_ref), channel_id=1, source_target_pairs={{0,2},{1,3},{2,0},{3,1},{4,6},{5,7},{6,4},{7,5},{8,10},{9,11},{10,... | collective-permute-start | bytes 221192 | tf_op jit(solution)/shard_map/ppermute | solution.py:224
  9.3 0.0 collective-permute-start
  9.3 0.7 %collective-permute-done.11.refs_11_ = bf16[288,128]{1,0:T(8,128)(2,1)S(1)} collective-permute-done((bf16[288,128]{1,0:T(8,128)(2,1)}, bf16[288,128]{1,0:T(8,128)(2,1)S(1)}, u32[]{:S(2)}, u32[]{:S(2)}) %collective-permute-start.11) | collective-permute-done | bytes 73760 | tf_op jit(solution)/shard_map/ppermute | solution.py:224
  10.0 1.9 %collective-permute-start.13 = (bf16[288,128]{1,0:T(8,128)(2,1)S(1)}, bf16[288,128]{1,0:T(8,128)(2,1)S(1)}, u32[]{:S(2)}, u32[]{:S(2)}) collective-permute-start(bf16[288,128]{1,0:T(8,128)(2,1)S(1)} %collective-permute-done.11.refs_11_), channel_id=1, source_target_pairs={{0,2},{1,3},{2,0},{3,1},{4,6},{5,7},{6,4},{7,5},{8,10},{9,11},{10,... | collective-permute-start | bytes 221192 | tf_op jit(solution)/shard_map/ppermute | solution.py:224
  11.8 1.6 %collective-permute-done.7.refs_7_ = bf16[288,128]{1,0:T(8,128)(2,1)S(1)} collective-permute-done((bf16[288,128]{1,0:T(8,128)(2,1)}, bf16[288,128]{1,0:T(8,128)(2,1)S(1)}, u32[]{:S(2)}, u32[]{:S(2)}) %collective-permute-start.7) | collective-permute-done | bytes 73760 | tf_op jit(solution)/shard_map/ppermute | solution.py:224
  13.4 0.0 collective-permute-start.12
  13.4 0.0 collective-permute-done.3.refs_3_
  13.4 1.5 %collective-permute-start.9 = (bf16[288,128]{1,0:T(8,128)(2,1)S(1)}, bf16[288,128]{1,0:T(8,128)(2,1)S(1)}, u32[]{:S(2)}, u32[]{:S(2)}) collective-permute-start(bf16[288,128]{1,0:T(8,128)(2,1)S(1)} %collective-permute-done.7.refs_7_), channel_id=1, source_target_pairs={{0,2},{1,3},{2,0},{3,1},{4,6},{5,7},{6,4},{7,5},{8,10},{9,11},{10,... | collective-permute-start | bytes 221192 | tf_op jit(solution)/shard_map/ppermute | solution.py:224
  14.9 0.0 collective-permute-done.1.refs_1_
  14.9 0.2 collective-permute-start.8
  15.2 0.0 collective-permute-done.refs_0_
  15.2 0.5 collective-permute-start.5
  15.7 0.0 collective-permute-done.13.refs_13_
  15.7 0.0 collective-permute-start.4
  15.7 0.0 collective-permute-done.12.refs_12_
  15.7 0.5 collective-permute-start.2
  16.2 1.9 %collective-permute-done.9.refs_9_ = bf16[288,128]{1,0:T(8,128)(2,1)S(1)} collective-permute-done((bf16[288,128]{1,0:T(8,128)(2,1)S(1)}, bf16[288,128]{1,0:T(8,128)(2,1)S(1)}, u32[]{:S(2)}, u32[]{:S(2)}) %collective-permute-start.9) | collective-permute-done | bytes 73760 | tf_op jit(solution)/shard_map/ppermute | solution.py:224
  18.1 0.0 collective-permute-start.14
  18.1 0.0 collective-permute-done.8.refs_8_
  18.1 0.5 collective-permute-start.10
  18.7 1.0 %collective-permute-done.5.refs_5_ = bf16[288,128]{1,0:T(8,128)(2,1)S(1)} collective-permute-done((bf16[288,128]{1,0:T(8,128)(2,1)S(1)}, bf16[288,128]{1,0:T(8,128)(2,1)S(1)}, u32[]{:S(2)}, u32[]{:S(2)}) %collective-permute-start.5) | collective-permute-done | bytes 73760 | tf_op jit(solution)/shard_map/ppermute | solution.py:224
  19.7 0.0 collective-permute-start.6
  19.7 0.0 collective-permute-done.4.refs_4_
  19.7 0.0 collective-permute-done.2.refs_2_
  19.7 0.0 collective-permute-done.14.refs_14_
  19.7 0.0 collective-permute-done.10.refs_10_
  19.7 1.2 %collective-permute-done.6.refs_6_ = bf16[288,128]{1,0:T(8,128)(2,1)S(1)} collective-permute-done((bf16[288,128]{1,0:T(8,128)(2,1)S(1)}, bf16[288,128]{1,0:T(8,128)(2,1)S(1)}, u32[]{:S(2)}, u32[]{:S(2)}) %collective-permute-start.6) | collective-permute-done | bytes 73760 | tf_op jit(solution)/shard_map/ppermute | solution.py:224
  20.9 19.1 %score.1 = f32[16,8,256]{2,1,0:T(8,128)S(1)} custom-call(s32[1]{0:T(128)} %bitcast.2.me_ref, s32[256]{0:T(256)} %count_hbm.1, s32[1,256]{1,0:T(1,128)} %bitcast.8, bf16[288,128]{1,0:T(8,128)(2,1)} %get-tuple-element.8.own_ref, bf16[288,128]{1,0:T(8,128)(2,1)S(1)} %collective-permute-done.refs_0_, bf16[288,128]{1,0:T(8,128)(2,1)S(1)} %collective-permute-done.1.refs_1_, ...), custom_call_target="tpu_custom_call" | custom-call | tf_op jit(solution)/shard_map/score/pallas_call | solution.py:252
  40.1 13.0 %all_to_all.5.back_ref = f32[16,8,256]{2,1,0:T(8,128)S(1)} all-to-all(f32[16,8,256]{2,1,0:T(8,128)S(1)} %score.1), channel_id=1, replica_groups=mesh['groups'=2,'shard'=16] {'shard'}, dimensions={0} | all-to-all | bytes 262144 | tf_op jit(solution)/shard_map/all_to_all | solution.py:280
  53.1 0.0 copy-done
  53.1 0.7 %pick.1 = f32[8,256]{1,0:T(8,128)} custom-call(s32[8,256]{1,0:T(8,128)S(1)} %copy-done, f32[16,8,256]{2,1,0:T(8,128)S(1)} %all_to_all.5.back_ref), custom_call_target="tpu_custom_call" | custom-call | tf_op jit(solution)/shard_map/pick/pallas_call | solution.py:281
Async XLA Ops:
  1.9 51.1 %copy-start = (s32[8,256]{1,0:T(8,128)S(1)}, s32[8,256]{1,0:T(8,128)}, u32[]{:S(2)}) copy-start(s32[8,256]{1,0:T(8,128)} %get-tuple-element.7.slot_ref) | copy-start | bytes 24580
  1.9 8.0 %collective-permute-start.11 = (bf16[288,128]{1,0:T(8,128)(2,1)}, bf16[288,128]{1,0:T(8,128)(2,1)S(1)}, u32[]{:S(2)}, u32[]{:S(2)}) collective-permute-start(bf16[288,128]{1,0:T(8,128)(2,1)} %get-tuple-element.8.own_ref), channel_id=1, source_target_pairs={{0,12},{1,13},{2,14},{3,15},{4,8},{5,9},{6,10},{7,11},{8,4},{9,5},... | collective-permute-start | bytes 221192 | tf_op jit(solution)/shard_map/ppermute | solution.py:224
  7.0 6.4 %collective-permute-start.7 = (bf16[288,128]{1,0:T(8,128)(2,1)}, bf16[288,128]{1,0:T(8,128)(2,1)S(1)}, u32[]{:S(2)}, u32[]{:S(2)}) collective-permute-start(bf16[288,128]{1,0:T(8,128)(2,1)} %get-tuple-element.8.own_ref), channel_id=1, source_target_pairs={{0,8},{1,9},{2,10},{3,11},{4,12},{5,13},{6,14},{7,15},{8,0},{9,1},... | collective-permute-start | bytes 221192 | tf_op jit(solution)/shard_map/ppermute | solution.py:224
  7.0 6.4 %collective-permute-start.3 = (bf16[288,128]{1,0:T(8,128)(2,1)}, bf16[288,128]{1,0:T(8,128)(2,1)S(1)}, u32[]{:S(2)}, u32[]{:S(2)}) collective-permute-start(bf16[288,128]{1,0:T(8,128)(2,1)} %get-tuple-element.8.own_ref), channel_id=1, source_target_pairs={{0,4},{1,5},{2,6},{3,7},{4,0},{5,1},{6,2},{7,3},{8,12},{9,13},{10,... | collective-permute-start | bytes 221192 | tf_op jit(solution)/shard_map/ppermute | solution.py:224
  7.5 7.4 %collective-permute-start.1 = (bf16[288,128]{1,0:T(8,128)(2,1)}, bf16[288,128]{1,0:T(8,128)(2,1)S(1)}, u32[]{:S(2)}, u32[]{:S(2)}) collective-permute-start(bf16[288,128]{1,0:T(8,128)(2,1)} %get-tuple-element.8.own_ref), channel_id=1, source_target_pairs={{0,2},{1,3},{2,0},{3,1},{4,6},{5,7},{6,4},{7,5},{8,10},{9,11},{10,... | collective-permute-start | bytes 221192 | tf_op jit(solution)/shard_map/ppermute | solution.py:224
  9.3 5.9 %collective-permute-start = (bf16[288,128]{1,0:T(8,128)(2,1)}, bf16[288,128]{1,0:T(8,128)(2,1)S(1)}, u32[]{:S(2)}, u32[]{:S(2)}) collective-permute-start(bf16[288,128]{1,0:T(8,128)(2,1)} %get-tuple-element.8.own_ref), channel_id=1, source_target_pairs={{0,1},{1,0},{2,3},{3,2},{4,5},{5,4},{6,7},{7,6},{8,9},{9,8},{10,11... | collective-permute-start | bytes 221192 | tf_op jit(solution)/shard_map/ppermute | solution.py:224
  10.0 5.7 %collective-permute-start.13 = (bf16[288,128]{1,0:T(8,128)(2,1)S(1)}, bf16[288,128]{1,0:T(8,128)(2,1)S(1)}, u32[]{:S(2)}, u32[]{:S(2)}) collective-permute-start(bf16[288,128]{1,0:T(8,128)(2,1)S(1)} %collective-permute-done.11.refs_11_), channel_id=1, source_target_pairs={{0,2},{1,3},{2,0},{3,1},{4,6},{5,7},{6,4},{7,5},{8,10},{9,11},{10,... | collective-permute-start | bytes 221192 | tf_op jit(solution)/shard_map/ppermute | solution.py:224
  13.4 2.3 %collective-permute-start.12 = (bf16[288,128]{1,0:T(8,128)(2,1)S(1)}, bf16[288,128]{1,0:T(8,128)(2,1)S(1)}, u32[]{:S(2)}, u32[]{:S(2)}) collective-permute-start(bf16[288,128]{1,0:T(8,128)(2,1)S(1)} %collective-permute-done.11.refs_11_), channel_id=1, source_target_pairs={{0,1},{1,0},{2,3},{3,2},{4,5},{5,4},{6,7},{7,6},{8,9},{9,8},{10,11... | collective-permute-start | bytes 221192 | tf_op jit(solution)/shard_map/ppermute | solution.py:224
  13.4 4.7 %collective-permute-start.9 = (bf16[288,128]{1,0:T(8,128)(2,1)S(1)}, bf16[288,128]{1,0:T(8,128)(2,1)S(1)}, u32[]{:S(2)}, u32[]{:S(2)}) collective-permute-start(bf16[288,128]{1,0:T(8,128)(2,1)S(1)} %collective-permute-done.7.refs_7_), channel_id=1, source_target_pairs={{0,2},{1,3},{2,0},{3,1},{4,6},{5,7},{6,4},{7,5},{8,10},{9,11},{10,... | collective-permute-start | bytes 221192 | tf_op jit(solution)/shard_map/ppermute | solution.py:224
  14.9 3.2 %collective-permute-start.8 = (bf16[288,128]{1,0:T(8,128)(2,1)S(1)}, bf16[288,128]{1,0:T(8,128)(2,1)S(1)}, u32[]{:S(2)}, u32[]{:S(2)}) collective-permute-start(bf16[288,128]{1,0:T(8,128)(2,1)S(1)} %collective-permute-done.7.refs_7_), channel_id=1, source_target_pairs={{0,1},{1,0},{2,3},{3,2},{4,5},{5,4},{6,7},{7,6},{8,9},{9,8},{10,11... | collective-permute-start | bytes 221192 | tf_op jit(solution)/shard_map/ppermute | solution.py:224
  15.2 4.5 %collective-permute-start.5 = (bf16[288,128]{1,0:T(8,128)(2,1)S(1)}, bf16[288,128]{1,0:T(8,128)(2,1)S(1)}, u32[]{:S(2)}, u32[]{:S(2)}) collective-permute-start(bf16[288,128]{1,0:T(8,128)(2,1)S(1)} %collective-permute-done.3.refs_3_), channel_id=1, source_target_pairs={{0,2},{1,3},{2,0},{3,1},{4,6},{5,7},{6,4},{7,5},{8,10},{9,11},{10,... | collective-permute-start | bytes 221192 | tf_op jit(solution)/shard_map/ppermute | solution.py:224
  15.7 4.0 %collective-permute-start.4 = (bf16[288,128]{1,0:T(8,128)(2,1)S(1)}, bf16[288,128]{1,0:T(8,128)(2,1)S(1)}, u32[]{:S(2)}, u32[]{:S(2)}) collective-permute-start(bf16[288,128]{1,0:T(8,128)(2,1)S(1)} %collective-permute-done.3.refs_3_), channel_id=1, source_target_pairs={{0,1},{1,0},{2,3},{3,2},{4,5},{5,4},{6,7},{7,6},{8,9},{9,8},{10,11... | collective-permute-start | bytes 221192 | tf_op jit(solution)/shard_map/ppermute | solution.py:224
  15.7 4.0 %collective-permute-start.2 = (bf16[288,128]{1,0:T(8,128)(2,1)S(1)}, bf16[288,128]{1,0:T(8,128)(2,1)S(1)}, u32[]{:S(2)}, u32[]{:S(2)}) collective-permute-start(bf16[288,128]{1,0:T(8,128)(2,1)S(1)} %collective-permute-done.1.refs_1_), channel_id=1, source_target_pairs={{0,1},{1,0},{2,3},{3,2},{4,5},{5,4},{6,7},{7,6},{8,9},{9,8},{10,11... | collective-permute-start | bytes 221192 | tf_op jit(solution)/shard_map/ppermute | solution.py:224
  18.1 1.6 %collective-permute-start.14 = (bf16[288,128]{1,0:T(8,128)(2,1)S(1)}, bf16[288,128]{1,0:T(8,128)(2,1)S(1)}, u32[]{:S(2)}, u32[]{:S(2)}) collective-permute-start(bf16[288,128]{1,0:T(8,128)(2,1)S(1)} %collective-permute-done.13.refs_13_), channel_id=1, source_target_pairs={{0,1},{1,0},{2,3},{3,2},{4,5},{5,4},{6,7},{7,6},{8,9},{9,8},{10,11... | collective-permute-start | bytes 221192 | tf_op jit(solution)/shard_map/ppermute | solution.py:224
  18.1 1.6 %collective-permute-start.10 = (bf16[288,128]{1,0:T(8,128)(2,1)S(1)}, bf16[288,128]{1,0:T(8,128)(2,1)S(1)}, u32[]{:S(2)}, u32[]{:S(2)}) collective-permute-start(bf16[288,128]{1,0:T(8,128)(2,1)S(1)} %collective-permute-done.9.refs_9_), channel_id=1, source_target_pairs={{0,1},{1,0},{2,3},{3,2},{4,5},{5,4},{6,7},{7,6},{8,9},{9,8},{10,11... | collective-permute-start | bytes 221192 | tf_op jit(solution)/shard_map/ppermute | solution.py:224
  19.7 1.3 %collective-permute-start.6 = (bf16[288,128]{1,0:T(8,128)(2,1)S(1)}, bf16[288,128]{1,0:T(8,128)(2,1)S(1)}, u32[]{:S(2)}, u32[]{:S(2)}) collective-permute-start(bf16[288,128]{1,0:T(8,128)(2,1)S(1)} %collective-permute-done.5.refs_5_), channel_id=1, source_target_pairs={{0,1},{1,0},{2,3},{3,2},{4,5},{5,4},{6,7},{7,6},{8,9},{9,8},{10,11... | collective-permute-start | bytes 221192 | tf_op jit(solution)/shard_map/ppermute | solution.py:224

commit v6 on v5

--- a/solution.py
+++ b/solution.py
@@ -156,8 +156,9 @@
     ]
     list_vmem[0:PMOST, :] = jnp.concatenate(lines, axis=0).astype(I32) * qt
     own = dot(iota((16, held), 1).astype(F32).astype(BF16), order16, NT)
-    list_vmem[PMOST : PMOST + 16, :] = own.astype(I32)
-    list_vmem[PMOST + 16 :, :] = jnp.broadcast_to(upto, (16, held)).astype(I32)
+    counts = jnp.sum(jnp.where(iota((16, held), 1) == level, upto, 0.0), axis=0, keepdims=True)
+    own = jnp.where(iota((8, held), 0) == 0, own[:8], counts)
+    list_vmem[PMOST:, :] = own.astype(I32)
     copy = pltpu.make_async_copy(list_vmem, list_smem, sems.at[parts])
     copy.start()
     small[2].wait()
@@ -186,7 +187,7 @@
 
     start = 0
     for s in levels:
-        stop = list_smem[PMOST + 16 + s, 0] // WALK
+        stop = list_smem[PMOST + 1, s] // WALK
         lax.fori_loop(start, stop, functools.partial(walk, s), 0)
         start = stop
     wide = PMOST * qt
@@ -196,7 +197,12 @@
     fine = (best - coarse.astype(F32)).astype(BF16)
     mean = mean.astype(BF16)
     score = dot(mean, coarse, NT) + dot(mean, fine, NT)
-    score = dot(score, order, NN, precision=lax.Precision.HIGHEST)
+    pieces, rest = [], score
+    for _ in range(3):
+        pieces.append(rest.astype(BF16))
+        rest = rest - pieces[-1].astype(F32)
+    spread = dot(jnp.concatenate(pieces, axis=0), order16, NN)
+    score = spread[:PMOST] + spread[PMOST : 2 * PMOST] + spread[2 * PMOST :]
     dense = jnp.zeros((total, held), F32)
     for r in range(PMOST):
         dense = jnp.where(rank == r + 1.0, score[r : r + 1, :], dense)
@@ -259,8 +265,8 @@
             VMEM((DEPTH * PITCH, d), F32),
             VMEM((held, d), F32),
             VMEM((n * tokens, d), BF16),
-            VMEM((PMOST + 32, held), I32),
-            SMEM((PMOST + 32, held), I32),
+            VMEM((PMOST + 8, held), I32),
+            SMEM((PMOST + 8, held), I32),
             VMEM((held, PMOST * qt), F32),
             SMEM((held,), I32),
             VMEM((1, held), I32),

time: 54.1 us -> 53.8 us (level)
  no operation moved by 1% of the time
where the time goes in v6:
time: 53.8 us; the launch traced here: 53.6 us
  Pallas kernels  21.9 us (41%)
  blocking collectives  12.7 us (24%)
  starting transfers between devices  12.5 us (23%)
  waiting for transfers between devices  6.48 us (12%)
    pallas_call x1, Pallas kernels, shards(): pl.pallas_call(functools.partial(score_kernel, n), out_shape=jax.ShapeDty...  19.2 us
    all_to_all x1, blocking collectives, shards(): lax.all_to_all(dense, 'shard', split_axis=0, concat_axis=0, tiled=True)  12.7 us
    ppermute x15, starting transfers between devices, swap(): return lax.ppermute(v, 'shard', [(i, i ^ k) for i in range(n)])  12.5 us
    ppermute x15, waiting for transfers between devices, swap(): return lax.ppermute(v, 'shard', [(i, i ^ k) for i in range(n)])  6.48 us
    pallas_call x1, Pallas kernels, shards(): pl.pallas_call(route_kernel, out_shape=(jax.ShapeDtypeStruct((q_dev, cand...  1.93 us
  transfers between devices with their start and end apart: 15, of which 5 were waited for; matrix products, arithmetic and copies ran while one was open for 0% of the time, Pallas kernels for 0%

profile of v6, /device:TPU:0, one launch (start us, length us, event | category | flops | bytes accessed | tf_op | source)
XLA Modules:
  0.0 53.6 jit_solution(8895116587996693623)
XLA Ops:
  0.0 1.9 %route.1 = (s32[8,256]{1,0:T(8,128)}, bf16[288,128]{1,0:T(8,128)(2,1)}) custom-call(bf16[256,128]{1,0:T(8,128)(2,1)} %bitcast.6, s32[8,256]{1,0:T(8,128)} %cand_ref.1, s32[32,128]{1,0:T(8,128)} %bitcast.7), custom_call_target="tpu_custom_call" | custom-call | tf_op jit(solution)/shard_map/route/pallas_call | solution.py:242
  1.9 0.0 copy-start
  1.9 5.0 %collective-permute-start.11 = (bf16[288,128]{1,0:T(8,128)(2,1)}, bf16[288,128]{1,0:T(8,128)(2,1)S(1)}, u32[]{:S(2)}, u32[]{:S(2)}) collective-permute-start(bf16[288,128]{1,0:T(8,128)(2,1)} %get-tuple-element.8.own_ref), channel_id=1, source_target_pairs={{0,12},{1,13},{2,14},{3,15},{4,8},{5,9},{6,10},{7,11},{8,4},{9,5},... | collective-permute-start | bytes 221192 | tf_op jit(solution)/shard_map/ppermute | solution.py:230
  7.0 0.0 collective-permute-start.7
  7.0 0.6 %collective-permute-start.3 = (bf16[288,128]{1,0:T(8,128)(2,1)}, bf16[288,128]{1,0:T(8,128)(2,1)S(1)}, u32[]{:S(2)}, u32[]{:S(2)}) collective-permute-start(bf16[288,128]{1,0:T(8,128)(2,1)} %get-tuple-element.8.own_ref), channel_id=1, source_target_pairs={{0,4},{1,5},{2,6},{3,7},{4,0},{5,1},{6,2},{7,3},{8,12},{9,13},{10,... | collective-permute-start | bytes 221192 | tf_op jit(solution)/shard_map/ppermute | solution.py:230
  7.5 1.7 %collective-permute-start.1 = (bf16[288,128]{1,0:T(8,128)(2,1)}, bf16[288,128]{1,0:T(8,128)(2,1)S(1)}, u32[]{:S(2)}, u32[]{:S(2)}) collective-permute-start(bf16[288,128]{1,0:T(8,128)(2,1)} %get-tuple-element.8.own_ref), channel_id=1, source_target_pairs={{0,2},{1,3},{2,0},{3,1},{4,6},{5,7},{6,4},{7,5},{8,10},{9,11},{10,... | collective-permute-start | bytes 221192 | tf_op jit(solution)/shard_map/ppermute | solution.py:230
  9.3 0.0 collective-permute-start
  9.3 0.7 %collective-permute-done.11.refs_11_ = bf16[288,128]{1,0:T(8,128)(2,1)S(1)} collective-permute-done((bf16[288,128]{1,0:T(8,128)(2,1)}, bf16[288,128]{1,0:T(8,128)(2,1)S(1)}, u32[]{:S(2)}, u32[]{:S(2)}) %collective-permute-start.11) | collective-permute-done | bytes 73760 | tf_op jit(solution)/shard_map/ppermute | solution.py:230
  10.0 1.9 %collective-permute-start.13 = (bf16[288,128]{1,0:T(8,128)(2,1)S(1)}, bf16[288,128]{1,0:T(8,128)(2,1)S(1)}, u32[]{:S(2)}, u32[]{:S(2)}) collective-permute-start(bf16[288,128]{1,0:T(8,128)(2,1)S(1)} %collective-permute-done.11.refs_11_), channel_id=1, source_target_pairs={{0,2},{1,3},{2,0},{3,1},{4,6},{5,7},{6,4},{7,5},{8,10},{9,11},{10,... | collective-permute-start | bytes 221192 | tf_op jit(solution)/shard_map/ppermute | solution.py:230
  11.8 1.6 %collective-permute-done.7.refs_7_ = bf16[288,128]{1,0:T(8,128)(2,1)S(1)} collective-permute-done((bf16[288,128]{1,0:T(8,128)(2,1)}, bf16[288,128]{1,0:T(8,128)(2,1)S(1)}, u32[]{:S(2)}, u32[]{:S(2)}) %collective-permute-start.7) | collective-permute-done | bytes 73760 | tf_op jit(solution)/shard_map/ppermute | solution.py:230
  13.4 0.0 collective-permute-start.12
  13.4 0.0 collective-permute-done.3.refs_3_
  13.4 1.5 %collective-permute-start.9 = (bf16[288,128]{1,0:T(8,128)(2,1)S(1)}, bf16[288,128]{1,0:T(8,128)(2,1)S(1)}, u32[]{:S(2)}, u32[]{:S(2)}) collective-permute-start(bf16[288,128]{1,0:T(8,128)(2,1)S(1)} %collective-permute-done.7.refs_7_), channel_id=1, source_target_pairs={{0,2},{1,3},{2,0},{3,1},{4,6},{5,7},{6,4},{7,5},{8,10},{9,11},{10,... | collective-permute-start | bytes 221192 | tf_op jit(solution)/shard_map/ppermute | solution.py:230
  14.9 0.0 collective-permute-done.1.refs_1_
  14.9 0.2 collective-permute-start.8
  15.2 0.0 collective-permute-done.refs_0_
  15.2 0.5 collective-permute-start.5
  15.7 0.0 collective-permute-done.13.refs_13_
  15.7 0.0 collective-permute-start.4
  15.7 0.0 collective-permute-done.12.refs_12_
  15.7 0.5 collective-permute-start.2
  16.2 1.9 %collective-permute-done.9.refs_9_ = bf16[288,128]{1,0:T(8,128)(2,1)S(1)} collective-permute-done((bf16[288,128]{1,0:T(8,128)(2,1)S(1)}, bf16[288,128]{1,0:T(8,128)(2,1)S(1)}, u32[]{:S(2)}, u32[]{:S(2)}) %collective-permute-start.9) | collective-permute-done | bytes 73760 | tf_op jit(solution)/shard_map/ppermute | solution.py:230
  18.1 0.0 collective-permute-start.14
  18.1 0.0 collective-permute-done.8.refs_8_
  18.1 0.5 collective-permute-start.10
  18.7 1.0 %collective-permute-done.5.refs_5_ = bf16[288,128]{1,0:T(8,128)(2,1)S(1)} collective-permute-done((bf16[288,128]{1,0:T(8,128)(2,1)S(1)}, bf16[288,128]{1,0:T(8,128)(2,1)S(1)}, u32[]{:S(2)}, u32[]{:S(2)}) %collective-permute-start.5) | collective-permute-done | bytes 73760 | tf_op jit(solution)/shard_map/ppermute | solution.py:230
  19.7 0.0 collective-permute-start.6
  19.7 0.0 collective-permute-done.4.refs_4_
  19.7 0.0 collective-permute-done.2.refs_2_
  19.7 0.0 collective-permute-done.14.refs_14_
  19.7 0.0 collective-permute-done.10.refs_10_
  19.7 1.2 %collective-permute-done.6.refs_6_ = bf16[288,128]{1,0:T(8,128)(2,1)S(1)} collective-permute-done((bf16[288,128]{1,0:T(8,128)(2,1)S(1)}, bf16[288,128]{1,0:T(8,128)(2,1)S(1)}, u32[]{:S(2)}, u32[]{:S(2)}) %collective-permute-start.6) | collective-permute-done | bytes 73760 | tf_op jit(solution)/shard_map/ppermute | solution.py:230
  20.9 19.2 %score.1 = f32[16,8,256]{2,1,0:T(8,128)S(1)} custom-call(s32[1]{0:T(128)} %bitcast.2.me_ref, s32[256]{0:T(256)} %count_hbm.1, s32[1,256]{1,0:T(1,128)} %bitcast.8, bf16[288,128]{1,0:T(8,128)(2,1)} %get-tuple-element.8.own_ref, bf16[288,128]{1,0:T(8,128)(2,1)S(1)} %collective-permute-done.refs_0_, bf16[288,128]{1,0:T(8,128)(2,1)S(1)} %collective-permute-done.1.refs_1_, ...), custom_call_target="tpu_custom_call" | custom-call | tf_op jit(solution)/shard_map/score/pallas_call | solution.py:258
  40.1 12.7 %all_to_all.5.back_ref = f32[16,8,256]{2,1,0:T(8,128)S(1)} all-to-all(f32[16,8,256]{2,1,0:T(8,128)S(1)} %score.1), channel_id=1, replica_groups=mesh['groups'=2,'shard'=16] {'shard'}, dimensions={0} | all-to-all | bytes 262144 | tf_op jit(solution)/shard_map/all_to_all | solution.py:286
  52.9 0.0 copy-done
  52.9 0.7 %pick.1 = f32[8,256]{1,0:T(8,128)} custom-call(s32[8,256]{1,0:T(8,128)S(1)} %copy-done, f32[16,8,256]{2,1,0:T(8,128)S(1)} %all_to_all.5.back_ref), custom_call_target="tpu_custom_call" | custom-call | tf_op jit(solution)/shard_map/pick/pallas_call | solution.py:287
Async XLA Ops:
  1.9 50.9 %copy-start = (s32[8,256]{1,0:T(8,128)S(1)}, s32[8,256]{1,0:T(8,128)}, u32[]{:S(2)}) copy-start(s32[8,256]{1,0:T(8,128)} %get-tuple-element.7.slot_ref) | copy-start | bytes 24580
  1.9 8.0 %collective-permute-start.11 = (bf16[288,128]{1,0:T(8,128)(2,1)}, bf16[288,128]{1,0:T(8,128)(2,1)S(1)}, u32[]{:S(2)}, u32[]{:S(2)}) collective-permute-start(bf16[288,128]{1,0:T(8,128)(2,1)} %get-tuple-element.8.own_ref), channel_id=1, source_target_pairs={{0,12},{1,13},{2,14},{3,15},{4,8},{5,9},{6,10},{7,11},{8,4},{9,5},... | collective-permute-start | bytes 221192 | tf_op jit(solution)/shard_map/ppermute | solution.py:230
  7.0 6.4 %collective-permute-start.7 = (bf16[288,128]{1,0:T(8,128)(2,1)}, bf16[288,128]{1,0:T(8,128)(2,1)S(1)}, u32[]{:S(2)}, u32[]{:S(2)}) collective-permute-start(bf16[288,128]{1,0:T(8,128)(2,1)} %get-tuple-element.8.own_ref), channel_id=1, source_target_pairs={{0,8},{1,9},{2,10},{3,11},{4,12},{5,13},{6,14},{7,15},{8,0},{9,1},... | collective-permute-start | bytes 221192 | tf_op jit(solution)/shard_map/ppermute | solution.py:230
  7.0 6.4 %collective-permute-start.3 = (bf16[288,128]{1,0:T(8,128)(2,1)}, bf16[288,128]{1,0:T(8,128)(2,1)S(1)}, u32[]{:S(2)}, u32[]{:S(2)}) collective-permute-start(bf16[288,128]{1,0:T(8,128)(2,1)} %get-tuple-element.8.own_ref), channel_id=1, source_target_pairs={{0,4},{1,5},{2,6},{3,7},{4,0},{5,1},{6,2},{7,3},{8,12},{9,13},{10,... | collective-permute-start | bytes 221192 | tf_op jit(solution)/shard_map/ppermute | solution.py:230
  7.5 7.4 %collective-permute-start.1 = (bf16[288,128]{1,0:T(8,128)(2,1)}, bf16[288,128]{1,0:T(8,128)(2,1)S(1)}, u32[]{:S(2)}, u32[]{:S(2)}) collective-permute-start(bf16[288,128]{1,0:T(8,128)(2,1)} %get-tuple-element.8.own_ref), channel_id=1, source_target_pairs={{0,2},{1,3},{2,0},{3,1},{4,6},{5,7},{6,4},{7,5},{8,10},{9,11},{10,... | collective-permute-start | bytes 221192 | tf_op jit(solution)/shard_map/ppermute | solution.py:230
  9.3 5.9 %collective-permute-start = (bf16[288,128]{1,0:T(8,128)(2,1)}, bf16[288,128]{1,0:T(8,128)(2,1)S(1)}, u32[]{:S(2)}, u32[]{:S(2)}) collective-permute-start(bf16[288,128]{1,0:T(8,128)(2,1)} %get-tuple-element.8.own_ref), channel_id=1, source_target_pairs={{0,1},{1,0},{2,3},{3,2},{4,5},{5,4},{6,7},{7,6},{8,9},{9,8},{10,11... | collective-permute-start | bytes 221192 | tf_op jit(solution)/shard_map/ppermute | solution.py:230
  10.0 5.7 %collective-permute-start.13 = (bf16[288,128]{1,0:T(8,128)(2,1)S(1)}, bf16[288,128]{1,0:T(8,128)(2,1)S(1)}, u32[]{:S(2)}, u32[]{:S(2)}) collective-permute-start(bf16[288,128]{1,0:T(8,128)(2,1)S(1)} %collective-permute-done.11.refs_11_), channel_id=1, source_target_pairs={{0,2},{1,3},{2,0},{3,1},{4,6},{5,7},{6,4},{7,5},{8,10},{9,11},{10,... | collective-permute-start | bytes 221192 | tf_op jit(solution)/shard_map/ppermute | solution.py:230
  13.4 2.3 %collective-permute-start.12 = (bf16[288,128]{1,0:T(8,128)(2,1)S(1)}, bf16[288,128]{1,0:T(8,128)(2,1)S(1)}, u32[]{:S(2)}, u32[]{:S(2)}) collective-permute-start(bf16[288,128]{1,0:T(8,128)(2,1)S(1)} %collective-permute-done.11.refs_11_), channel_id=1, source_target_pairs={{0,1},{1,0},{2,3},{3,2},{4,5},{5,4},{6,7},{7,6},{8,9},{9,8},{10,11... | collective-permute-start | bytes 221192 | tf_op jit(solution)/shard_map/ppermute | solution.py:230
  13.4 4.7 %collective-permute-start.9 = (bf16[288,128]{1,0:T(8,128)(2,1)S(1)}, bf16[288,128]{1,0:T(8,128)(2,1)S(1)}, u32[]{:S(2)}, u32[]{:S(2)}) collective-permute-start(bf16[288,128]{1,0:T(8,128)(2,1)S(1)} %collective-permute-done.7.refs_7_), channel_id=1, source_target_pairs={{0,2},{1,3},{2,0},{3,1},{4,6},{5,7},{6,4},{7,5},{8,10},{9,11},{10,... | collective-permute-start | bytes 221192 | tf_op jit(solution)/shard_map/ppermute | solution.py:230
  14.9 3.2 %collective-permute-start.8 = (bf16[288,128]{1,0:T(8,128)(2,1)S(1)}, bf16[288,128]{1,0:T(8,128)(2,1)S(1)}, u32[]{:S(2)}, u32[]{:S(2)}) collective-permute-start(bf16[288,128]{1,0:T(8,128)(2,1)S(1)} %collective-permute-done.7.refs_7_), channel_id=1, source_target_pairs={{0,1},{1,0},{2,3},{3,2},{4,5},{5,4},{6,7},{7,6},{8,9},{9,8},{10,11... | collective-permute-start | bytes 221192 | tf_op jit(solution)/shard_map/ppermute | solution.py:230
  15.2 4.5 %collective-permute-start.5 = (bf16[288,128]{1,0:T(8,128)(2,1)S(1)}, bf16[288,128]{1,0:T(8,128)(2,1)S(1)}, u32[]{:S(2)}, u32[]{:S(2)}) collective-permute-start(bf16[288,128]{1,0:T(8,128)(2,1)S(1)} %collective-permute-done.3.refs_3_), channel_id=1, source_target_pairs={{0,2},{1,3},{2,0},{3,1},{4,6},{5,7},{6,4},{7,5},{8,10},{9,11},{10,... | collective-permute-start | bytes 221192 | tf_op jit(solution)/shard_map/ppermute | solution.py:230
  15.7 4.0 %collective-permute-start.4 = (bf16[288,128]{1,0:T(8,128)(2,1)S(1)}, bf16[288,128]{1,0:T(8,128)(2,1)S(1)}, u32[]{:S(2)}, u32[]{:S(2)}) collective-permute-start(bf16[288,128]{1,0:T(8,128)(2,1)S(1)} %collective-permute-done.3.refs_3_), channel_id=1, source_target_pairs={{0,1},{1,0},{2,3},{3,2},{4,5},{5,4},{6,7},{7,6},{8,9},{9,8},{10,11... | collective-permute-start | bytes 221192 | tf_op jit(solution)/shard_map/ppermute | solution.py:230
  15.7 4.0 %collective-permute-start.2 = (bf16[288,128]{1,0:T(8,128)(2,1)S(1)}, bf16[288,128]{1,0:T(8,128)(2,1)S(1)}, u32[]{:S(2)}, u32[]{:S(2)}) collective-permute-start(bf16[288,128]{1,0:T(8,128)(2,1)S(1)} %collective-permute-done.1.refs_1_), channel_id=1, source_target_pairs={{0,1},{1,0},{2,3},{3,2},{4,5},{5,4},{6,7},{7,6},{8,9},{9,8},{10,11... | collective-permute-start | bytes 221192 | tf_op jit(solution)/shard_map/ppermute | solution.py:230
  18.1 1.6 %collective-permute-start.14 = (bf16[288,128]{1,0:T(8,128)(2,1)S(1)}, bf16[288,128]{1,0:T(8,128)(2,1)S(1)}, u32[]{:S(2)}, u32[]{:S(2)}) collective-permute-start(bf16[288,128]{1,0:T(8,128)(2,1)S(1)} %collective-permute-done.13.refs_13_), channel_id=1, source_target_pairs={{0,1},{1,0},{2,3},{3,2},{4,5},{5,4},{6,7},{7,6},{8,9},{9,8},{10,11... | collective-permute-start | bytes 221192 | tf_op jit(solution)/shard_map/ppermute | solution.py:230
  18.1 1.6 %collective-permute-start.10 = (bf16[288,128]{1,0:T(8,128)(2,1)S(1)}, bf16[288,128]{1,0:T(8,128)(2,1)S(1)}, u32[]{:S(2)}, u32[]{:S(2)}) collective-permute-start(bf16[288,128]{1,0:T(8,128)(2,1)S(1)} %collective-permute-done.9.refs_9_), channel_id=1, source_target_pairs={{0,1},{1,0},{2,3},{3,2},{4,5},{5,4},{6,7},{7,6},{8,9},{9,8},{10,11... | collective-permute-start | bytes 221192 | tf_op jit(solution)/shard_map/ppermute | solution.py:230
  19.7 1.3 %collective-permute-start.6 = (bf16[288,128]{1,0:T(8,128)(2,1)S(1)}, bf16[288,128]{1,0:T(8,128)(2,1)S(1)}, u32[]{:S(2)}, u32[]{:S(2)}) collective-permute-start(bf16[288,128]{1,0:T(8,128)(2,1)S(1)} %collective-permute-done.5.refs_5_), channel_id=1, source_target_pairs={{0,1},{1,0},{2,3},{3,2},{4,5},{5,4},{6,7},{7,6},{8,9},{9,8},{10,11... | collective-permute-start | bytes 221192 | tf_op jit(solution)/shard_map/ppermute | solution.py:230

commit v7 on v6

--- a/solution.py
+++ b/solution.py
@@ -10,7 +10,7 @@
 PMOST = 16
 LEAST = 45
 PITCH = 17
-DEPTH = 48
+DEPTH = 32
 WALK = 32
 LANES = 128
 F32 = jnp.float32

time: 53.8 us -> 53.8 us (level)
  no operation moved by 1% of the time
where the time goes in v7:
time: 53.8 us; the launch traced here: 53.4 us
  Pallas kernels  21.9 us (41%)
  starting transfers between devices  12.5 us (23%)
  blocking collectives  12.5 us (23%)
  waiting for transfers between devices  6.48 us (12%)
    pallas_call x1, Pallas kernels, shards(): pl.pallas_call(functools.partial(score_kernel, n), out_shape=jax.ShapeDty...  19.3 us
    all_to_all x1, blocking collectives, shards(): lax.all_to_all(dense, 'shard', split_axis=0, concat_axis=0, tiled=True)  12.5 us
    ppermute x15, starting transfers between devices, swap(): return lax.ppermute(v, 'shard', [(i, i ^ k) for i in range(n)])  12.5 us
    ppermute x15, waiting for transfers between devices, swap(): return lax.ppermute(v, 'shard', [(i, i ^ k) for i in range(n)])  6.48 us
    pallas_call x1, Pallas kernels, shards(): pl.pallas_call(route_kernel, out_shape=(jax.ShapeDtypeStruct((q_dev, cand...  1.93 us
  transfers between devices with their start and end apart: 15, of which 5 were waited for; matrix products, arithmetic and copies ran while one was open for 0% of the time, Pallas kernels for 0%

profile of v7, /device:TPU:0, one launch (start us, length us, event | category | flops | bytes accessed | tf_op | source)
XLA Modules:
  0.0 53.4 jit_solution(5217270656456929222)
XLA Ops:
  0.0 1.9 %route.1 = (s32[8,256]{1,0:T(8,128)}, bf16[288,128]{1,0:T(8,128)(2,1)}) custom-call(bf16[256,128]{1,0:T(8,128)(2,1)} %bitcast.6, s32[8,256]{1,0:T(8,128)} %cand_ref.1, s32[32,128]{1,0:T(8,128)} %bitcast.7), custom_call_target="tpu_custom_call" | custom-call | tf_op jit(solution)/shard_map/route/pallas_call | solution.py:242
  1.9 0.0 copy-start
  1.9 5.0 %collective-permute-start.11 = (bf16[288,128]{1,0:T(8,128)(2,1)}, bf16[288,128]{1,0:T(8,128)(2,1)S(1)}, u32[]{:S(2)}, u32[]{:S(2)}) collective-permute-start(bf16[288,128]{1,0:T(8,128)(2,1)} %get-tuple-element.8.own_ref), channel_id=1, source_target_pairs={{0,12},{1,13},{2,14},{3,15},{4,8},{5,9},{6,10},{7,11},{8,4},{9,5},... | collective-permute-start | bytes 221192 | tf_op jit(solution)/shard_map/ppermute | solution.py:230
  7.0 0.0 collective-permute-start.7
  7.0 0.6 %collective-permute-start.3 = (bf16[288,128]{1,0:T(8,128)(2,1)}, bf16[288,128]{1,0:T(8,128)(2,1)S(1)}, u32[]{:S(2)}, u32[]{:S(2)}) collective-permute-start(bf16[288,128]{1,0:T(8,128)(2,1)} %get-tuple-element.8.own_ref), channel_id=1, source_target_pairs={{0,4},{1,5},{2,6},{3,7},{4,0},{5,1},{6,2},{7,3},{8,12},{9,13},{10,... | collective-permute-start | bytes 221192 | tf_op jit(solution)/shard_map/ppermute | solution.py:230
  7.5 1.7 %collective-permute-start.1 = (bf16[288,128]{1,0:T(8,128)(2,1)}, bf16[288,128]{1,0:T(8,128)(2,1)S(1)}, u32[]{:S(2)}, u32[]{:S(2)}) collective-permute-start(bf16[288,128]{1,0:T(8,128)(2,1)} %get-tuple-element.8.own_ref), channel_id=1, source_target_pairs={{0,2},{1,3},{2,0},{3,1},{4,6},{5,7},{6,4},{7,5},{8,10},{9,11},{10,... | collective-permute-start | bytes 221192 | tf_op jit(solution)/shard_map/ppermute | solution.py:230
  9.3 0.0 collective-permute-start
  9.3 0.7 %collective-permute-done.11.refs_11_ = bf16[288,128]{1,0:T(8,128)(2,1)S(1)} collective-permute-done((bf16[288,128]{1,0:T(8,128)(2,1)}, bf16[288,128]{1,0:T(8,128)(2,1)S(1)}, u32[]{:S(2)}, u32[]{:S(2)}) %collective-permute-start.11) | collective-permute-done | bytes 73760 | tf_op jit(solution)/shard_map/ppermute | solution.py:230
  10.0 1.9 %collective-permute-start.13 = (bf16[288,128]{1,0:T(8,128)(2,1)S(1)}, bf16[288,128]{1,0:T(8,128)(2,1)S(1)}, u32[]{:S(2)}, u32[]{:S(2)}) collective-permute-start(bf16[288,128]{1,0:T(8,128)(2,1)S(1)} %collective-permute-done.11.refs_11_), channel_id=1, source_target_pairs={{0,2},{1,3},{2,0},{3,1},{4,6},{5,7},{6,4},{7,5},{8,10},{9,11},{10,... | collective-permute-start | bytes 221192 | tf_op jit(solution)/shard_map/ppermute | solution.py:230
  11.8 1.6 %collective-permute-done.7.refs_7_ = bf16[288,128]{1,0:T(8,128)(2,1)S(1)} collective-permute-done((bf16[288,128]{1,0:T(8,128)(2,1)}, bf16[288,128]{1,0:T(8,128)(2,1)S(1)}, u32[]{:S(2)}, u32[]{:S(2)}) %collective-permute-start.7) | collective-permute-done | bytes 73760 | tf_op jit(solution)/shard_map/ppermute | solution.py:230
  13.4 0.0 collective-permute-start.12
  13.4 0.0 collective-permute-done.3.refs_3_
  13.4 1.5 %collective-permute-start.9 = (bf16[288,128]{1,0:T(8,128)(2,1)S(1)}, bf16[288,128]{1,0:T(8,128)(2,1)S(1)}, u32[]{:S(2)}, u32[]{:S(2)}) collective-permute-start(bf16[288,128]{1,0:T(8,128)(2,1)S(1)} %collective-permute-done.7.refs_7_), channel_id=1, source_target_pairs={{0,2},{1,3},{2,0},{3,1},{4,6},{5,7},{6,4},{7,5},{8,10},{9,11},{10,... | collective-permute-start | bytes 221192 | tf_op jit(solution)/shard_map/ppermute | solution.py:230
  14.9 0.0 collective-permute-done.1.refs_1_
  14.9 0.2 collective-permute-start.8
  15.2 0.0 collective-permute-done.refs_0_
  15.2 0.5 collective-permute-start.5
  15.7 0.0 collective-permute-done.13.refs_13_
  15.7 0.0 collective-permute-start.4
  15.7 0.0 collective-permute-done.12.refs_12_
  15.7 0.5 collective-permute-start.2
  16.2 1.9 %collective-permute-done.9.refs_9_ = bf16[288,128]{1,0:T(8,128)(2,1)S(1)} collective-permute-done((bf16[288,128]{1,0:T(8,128)(2,1)S(1)}, bf16[288,128]{1,0:T(8,128)(2,1)S(1)}, u32[]{:S(2)}, u32[]{:S(2)}) %collective-permute-start.9) | collective-permute-done | bytes 73760 | tf_op jit(solution)/shard_map/ppermute | solution.py:230
  18.1 0.0 collective-permute-start.14
  18.1 0.0 collective-permute-done.8.refs_8_
  18.1 0.5 collective-permute-start.10
  18.7 1.0 %collective-permute-done.5.refs_5_ = bf16[288,128]{1,0:T(8,128)(2,1)S(1)} collective-permute-done((bf16[288,128]{1,0:T(8,128)(2,1)S(1)}, bf16[288,128]{1,0:T(8,128)(2,1)S(1)}, u32[]{:S(2)}, u32[]{:S(2)}) %collective-permute-start.5) | collective-permute-done | bytes 73760 | tf_op jit(solution)/shard_map/ppermute | solution.py:230
  19.7 0.0 collective-permute-start.6
  19.7 0.0 collective-permute-done.4.refs_4_
  19.7 0.0 collective-permute-done.2.refs_2_
  19.7 0.0 collective-permute-done.14.refs_14_
  19.7 0.0 collective-permute-done.10.refs_10_
  19.7 1.2 %collective-permute-done.6.refs_6_ = bf16[288,128]{1,0:T(8,128)(2,1)S(1)} collective-permute-done((bf16[288,128]{1,0:T(8,128)(2,1)S(1)}, bf16[288,128]{1,0:T(8,128)(2,1)S(1)}, u32[]{:S(2)}, u32[]{:S(2)}) %collective-permute-start.6) | collective-permute-done | bytes 73760 | tf_op jit(solution)/shard_map/ppermute | solution.py:230
  20.9 19.3 %score.1 = f32[16,8,256]{2,1,0:T(8,128)S(1)} custom-call(s32[1]{0:T(128)} %bitcast.2.me_ref, s32[256]{0:T(256)} %count_hbm.1, s32[1,256]{1,0:T(1,128)} %bitcast.8, bf16[288,128]{1,0:T(8,128)(2,1)} %get-tuple-element.8.own_ref, bf16[288,128]{1,0:T(8,128)(2,1)S(1)} %collective-permute-done.refs_0_, bf16[288,128]{1,0:T(8,128)(2,1)S(1)} %collective-permute-done.1.refs_1_, ...), custom_call_target="tpu_custom_call" | custom-call | tf_op jit(solution)/shard_map/score/pallas_call | solution.py:258
  40.2 12.5 %all_to_all.5.back_ref = f32[16,8,256]{2,1,0:T(8,128)S(1)} all-to-all(f32[16,8,256]{2,1,0:T(8,128)S(1)} %score.1), channel_id=1, replica_groups=mesh['groups'=2,'shard'=16] {'shard'}, dimensions={0} | all-to-all | bytes 262144 | tf_op jit(solution)/shard_map/all_to_all | solution.py:286
  52.7 0.0 copy-done
  52.7 0.7 %pick.1 = f32[8,256]{1,0:T(8,128)} custom-call(s32[8,256]{1,0:T(8,128)S(1)} %copy-done, f32[16,8,256]{2,1,0:T(8,128)S(1)} %all_to_all.5.back_ref), custom_call_target="tpu_custom_call" | custom-call | tf_op jit(solution)/shard_map/pick/pallas_call | solution.py:287
Async XLA Ops:
  1.9 50.8 %copy-start = (s32[8,256]{1,0:T(8,128)S(1)}, s32[8,256]{1,0:T(8,128)}, u32[]{:S(2)}) copy-start(s32[8,256]{1,0:T(8,128)} %get-tuple-element.7.slot_ref) | copy-start | bytes 24580
  1.9 8.0 %collective-permute-start.11 = (bf16[288,128]{1,0:T(8,128)(2,1)}, bf16[288,128]{1,0:T(8,128)(2,1)S(1)}, u32[]{:S(2)}, u32[]{:S(2)}) collective-permute-start(bf16[288,128]{1,0:T(8,128)(2,1)} %get-tuple-element.8.own_ref), channel_id=1, source_target_pairs={{0,12},{1,13},{2,14},{3,15},{4,8},{5,9},{6,10},{7,11},{8,4},{9,5},... | collective-permute-start | bytes 221192 | tf_op jit(solution)/shard_map/ppermute | solution.py:230
  7.0 6.4 %collective-permute-start.7 = (bf16[288,128]{1,0:T(8,128)(2,1)}, bf16[288,128]{1,0:T(8,128)(2,1)S(1)}, u32[]{:S(2)}, u32[]{:S(2)}) collective-permute-start(bf16[288,128]{1,0:T(8,128)(2,1)} %get-tuple-element.8.own_ref), channel_id=1, source_target_pairs={{0,8},{1,9},{2,10},{3,11},{4,12},{5,13},{6,14},{7,15},{8,0},{9,1},... | collective-permute-start | bytes 221192 | tf_op jit(solution)/shard_map/ppermute | solution.py:230
  7.0 6.4 %collective-permute-start.3 = (bf16[288,128]{1,0:T(8,128)(2,1)}, bf16[288,128]{1,0:T(8,128)(2,1)S(1)}, u32[]{:S(2)}, u32[]{:S(2)}) collective-permute-start(bf16[288,128]{1,0:T(8,128)(2,1)} %get-tuple-element.8.own_ref), channel_id=1, source_target_pairs={{0,4},{1,5},{2,6},{3,7},{4,0},{5,1},{6,2},{7,3},{8,12},{9,13},{10,... | collective-permute-start | bytes 221192 | tf_op jit(solution)/shard_map/ppermute | solution.py:230
  7.5 7.4 %collective-permute-start.1 = (bf16[288,128]{1,0:T(8,128)(2,1)}, bf16[288,128]{1,0:T(8,128)(2,1)S(1)}, u32[]{:S(2)}, u32[]{:S(2)}) collective-permute-start(bf16[288,128]{1,0:T(8,128)(2,1)} %get-tuple-element.8.own_ref), channel_id=1, source_target_pairs={{0,2},{1,3},{2,0},{3,1},{4,6},{5,7},{6,4},{7,5},{8,10},{9,11},{10,... | collective-permute-start | bytes 221192 | tf_op jit(solution)/shard_map/ppermute | solution.py:230
  9.3 5.9 %collective-permute-start = (bf16[288,128]{1,0:T(8,128)(2,1)}, bf16[288,128]{1,0:T(8,128)(2,1)S(1)}, u32[]{:S(2)}, u32[]{:S(2)}) collective-permute-start(bf16[288,128]{1,0:T(8,128)(2,1)} %get-tuple-element.8.own_ref), channel_id=1, source_target_pairs={{0,1},{1,0},{2,3},{3,2},{4,5},{5,4},{6,7},{7,6},{8,9},{9,8},{10,11... | collective-permute-start | bytes 221192 | tf_op jit(solution)/shard_map/ppermute | solution.py:230
  10.0 5.7 %collective-permute-start.13 = (bf16[288,128]{1,0:T(8,128)(2,1)S(1)}, bf16[288,128]{1,0:T(8,128)(2,1)S(1)}, u32[]{:S(2)}, u32[]{:S(2)}) collective-permute-start(bf16[288,128]{1,0:T(8,128)(2,1)S(1)} %collective-permute-done.11.refs_11_), channel_id=1, source_target_pairs={{0,2},{1,3},{2,0},{3,1},{4,6},{5,7},{6,4},{7,5},{8,10},{9,11},{10,... | collective-permute-start | bytes 221192 | tf_op jit(solution)/shard_map/ppermute | solution.py:230
  13.4 2.3 %collective-permute-start.12 = (bf16[288,128]{1,0:T(8,128)(2,1)S(1)}, bf16[288,128]{1,0:T(8,128)(2,1)S(1)}, u32[]{:S(2)}, u32[]{:S(2)}) collective-permute-start(bf16[288,128]{1,0:T(8,128)(2,1)S(1)} %collective-permute-done.11.refs_11_), channel_id=1, source_target_pairs={{0,1},{1,0},{2,3},{3,2},{4,5},{5,4},{6,7},{7,6},{8,9},{9,8},{10,11... | collective-permute-start | bytes 221192 | tf_op jit(solution)/shard_map/ppermute | solution.py:230
  13.4 4.7 %collective-permute-start.9 = (bf16[288,128]{1,0:T(8,128)(2,1)S(1)}, bf16[288,128]{1,0:T(8,128)(2,1)S(1)}, u32[]{:S(2)}, u32[]{:S(2)}) collective-permute-start(bf16[288,128]{1,0:T(8,128)(2,1)S(1)} %collective-permute-done.7.refs_7_), channel_id=1, source_target_pairs={{0,2},{1,3},{2,0},{3,1},{4,6},{5,7},{6,4},{7,5},{8,10},{9,11},{10,... | collective-permute-start | bytes 221192 | tf_op jit(solution)/shard_map/ppermute | solution.py:230
  14.9 3.2 %collective-permute-start.8 = (bf16[288,128]{1,0:T(8,128)(2,1)S(1)}, bf16[288,128]{1,0:T(8,128)(2,1)S(1)}, u32[]{:S(2)}, u32[]{:S(2)}) collective-permute-start(bf16[288,128]{1,0:T(8,128)(2,1)S(1)} %collective-permute-done.7.refs_7_), channel_id=1, source_target_pairs={{0,1},{1,0},{2,3},{3,2},{4,5},{5,4},{6,7},{7,6},{8,9},{9,8},{10,11... | collective-permute-start | bytes 221192 | tf_op jit(solution)/shard_map/ppermute | solution.py:230
  15.2 4.5 %collective-permute-start.5 = (bf16[288,128]{1,0:T(8,128)(2,1)S(1)}, bf16[288,128]{1,0:T(8,128)(2,1)S(1)}, u32[]{:S(2)}, u32[]{:S(2)}) collective-permute-start(bf16[288,128]{1,0:T(8,128)(2,1)S(1)} %collective-permute-done.3.refs_3_), channel_id=1, source_target_pairs={{0,2},{1,3},{2,0},{3,1},{4,6},{5,7},{6,4},{7,5},{8,10},{9,11},{10,... | collective-permute-start | bytes 221192 | tf_op jit(solution)/shard_map/ppermute | solution.py:230
  15.7 4.0 %collective-permute-start.4 = (bf16[288,128]{1,0:T(8,128)(2,1)S(1)}, bf16[288,128]{1,0:T(8,128)(2,1)S(1)}, u32[]{:S(2)}, u32[]{:S(2)}) collective-permute-start(bf16[288,128]{1,0:T(8,128)(2,1)S(1)} %collective-permute-done.3.refs_3_), channel_id=1, source_target_pairs={{0,1},{1,0},{2,3},{3,2},{4,5},{5,4},{6,7},{7,6},{8,9},{9,8},{10,11... | collective-permute-start | bytes 221192 | tf_op jit(solution)/shard_map/ppermute | solution.py:230
  15.7 4.0 %collective-permute-start.2 = (bf16[288,128]{1,0:T(8,128)(2,1)S(1)}, bf16[288,128]{1,0:T(8,128)(2,1)S(1)}, u32[]{:S(2)}, u32[]{:S(2)}) collective-permute-start(bf16[288,128]{1,0:T(8,128)(2,1)S(1)} %collective-permute-done.1.refs_1_), channel_id=1, source_target_pairs={{0,1},{1,0},{2,3},{3,2},{4,5},{5,4},{6,7},{7,6},{8,9},{9,8},{10,11... | collective-permute-start | bytes 221192 | tf_op jit(solution)/shard_map/ppermute | solution.py:230
  18.1 1.6 %collective-permute-start.14 = (bf16[288,128]{1,0:T(8,128)(2,1)S(1)}, bf16[288,128]{1,0:T(8,128)(2,1)S(1)}, u32[]{:S(2)}, u32[]{:S(2)}) collective-permute-start(bf16[288,128]{1,0:T(8,128)(2,1)S(1)} %collective-permute-done.13.refs_13_), channel_id=1, source_target_pairs={{0,1},{1,0},{2,3},{3,2},{4,5},{5,4},{6,7},{7,6},{8,9},{9,8},{10,11... | collective-permute-start | bytes 221192 | tf_op jit(solution)/shard_map/ppermute | solution.py:230
  18.1 1.6 %collective-permute-start.10 = (bf16[288,128]{1,0:T(8,128)(2,1)S(1)}, bf16[288,128]{1,0:T(8,128)(2,1)S(1)}, u32[]{:S(2)}, u32[]{:S(2)}) collective-permute-start(bf16[288,128]{1,0:T(8,128)(2,1)S(1)} %collective-permute-done.9.refs_9_), channel_id=1, source_target_pairs={{0,1},{1,0},{2,3},{3,2},{4,5},{5,4},{6,7},{7,6},{8,9},{9,8},{10,11... | collective-permute-start | bytes 221192 | tf_op jit(solution)/shard_map/ppermute | solution.py:230
  19.7 1.3 %collective-permute-start.6 = (bf16[288,128]{1,0:T(8,128)(2,1)S(1)}, bf16[288,128]{1,0:T(8,128)(2,1)S(1)}, u32[]{:S(2)}, u32[]{:S(2)}) collective-permute-start(bf16[288,128]{1,0:T(8,128)(2,1)S(1)} %collective-permute-done.5.refs_5_), channel_id=1, source_target_pairs={{0,1},{1,0},{2,3},{3,2},{4,5},{5,4},{6,7},{7,6},{8,9},{9,8},{10,11... | collective-permute-start | bytes 221192 | tf_op jit(solution)/shard_map/ppermute | solution.py:230
